TPU v7x, 32 devices: a whole 2x2x4 slice. The times are simulated.
32 devices in a mesh: heads: 1, ctx: 32 (over z, y, x, core).
Axes of the slice: x: 2, y: 2, z: 4, core: 2. Of those that a mesh axis runs over, the one named last changes fastest.
Arguments:
- hidden: bfloat16 [4096, 4096], P('ctx', 'heads'), may hold values from -6 to 6
- w_query: bfloat16 [4096, 1024], P('ctx', 'heads'), may hold values from -0.09375 to 0.09375
- key_input: bfloat16 [4096, 1024], P('ctx', 'heads'), may hold values from -6 to 6
- values: bfloat16 [4096, 512], P('ctx', 'heads'), may hold values from -6 to 6
- cotangent: bfloat16 [4096, 512], P('ctx', 'heads'), may hold values from -6 to 6
Outputs:
- attended: bfloat16 [4096, 512], P('ctx', 'heads')
- query_grad: float32 [4096, 1024], P('ctx', 'heads')
- key_grad: bfloat16 [4096, 1024], P('ctx', 'heads')
- value_grad: bfloat16 [4096, 512], P('ctx', 'heads')
All inputs are finite; a program needn't handle non-finite values.
Results may differ from a plain program's by a relative error of at most 0.015.
Values may be sent and summed in bfloat16 or wider, within the bound.
No kernel may reach another device: no remote copies, remote signals or barrier semaphores. Data moves between devices by JAX's collectives and lax.ppermute only.
A program may use at most 128 MiB of HBM per device.

v0:
```python
import jax
import jax.numpy as jnp
from jax import lax
from jax.sharding import PartitionSpec as P

HEAD_DIM = 128
FEAT = 256
HEADS_GROUP = 4


EPSILON = 1e-06
HIGHEST = lax.Precision.HIGHEST


def partner(block, axis, stride):
    count = lax.axis_size(axis)
    route = []
    for low in range(count):
        high = low | 1 << stride
        if high != low and high < count:
            route += [(low, high), (high, low)]
    return lax.ppermute(block, axis, route)


def prefix(array, axis, join, neutral, backward):
    count = lax.axis_size(axis)
    place = lax.axis_index(axis)
    ahead = count - 1 - place if backward else place
    gathered = lax.all_gather(array.astype(jnp.bfloat16), axis)
    state = jnp.zeros_like(array) + jnp.asarray(neutral, array.dtype)

    def one(lap, state):
        source = count - 1 - lap if backward else lap
        return join(state, lax.dynamic_index_in_dim(gathered, source, 0, False).astype(array.dtype))

    return lax.fori_loop(0, ahead, one, state)


def add_states(earlier, later_one):
    return earlier + later_one


def split_grad(full_hidden, d_query):
    ctx_count = lax.axis_size("ctx")
    group_size = min(8, ctx_count)
    low_bits = group_size.bit_length() - 1
    high_bits = ctx_count.bit_length() - 1 - low_bits
    my_index = lax.axis_index("ctx")
    rows_here, width = full_hidden.shape
    row_block = width // ctx_count
    outer_count = ctx_count // group_size
    query_slabs = d_query[None]
    for bit_level in range(low_bits):
        incoming = partner(query_slabs, "ctx", bit_level)
        query_slabs = jnp.concatenate([query_slabs, incoming], axis=0)
    columns = full_hidden.reshape(rows_here, outer_count, group_size, row_block)
    for bit_level in range(low_bits):
        my_bit = my_index >> bit_level & 1
        shaped = columns.reshape(
            rows_here, outer_count, group_size >> bit_level + 1, 2, 1 << bit_level, row_block
        )
        flipped = jnp.flip(shaped, axis=3).reshape(columns.shape)
        columns = jnp.where(my_bit == 1, flipped, columns)
    for bit_level in range(low_bits):
        shaped = columns.reshape(
            rows_here, outer_count, group_size >> bit_level + 1, 2, 1 << bit_level, row_block
        )
        arrived = partner(shaped[:, :, :, 1], "ctx", bit_level)
        shaped = jnp.stack([shaped[:, :, :, 0], arrived], axis=3)
        columns = shaped.reshape(rows_here, outer_count, group_size, row_block)
    partial_value = jnp.einsum(
        "takr,ktf->arf", columns, query_slabs, preferred_element_type=jnp.float32
    )
    for bit_level in range(high_bits):
        my_bit = my_index >> low_bits + bit_level & 1
        halves = partial_value.reshape(
            partial_value.shape[0] // 2, 2, row_block, partial_value.shape[2]
        )
        kept_half = jnp.where(my_bit == 1, halves[:, 1], halves[:, 0])
        sent_half = jnp.where(my_bit == 1, halves[:, 0], halves[:, 1])
        partial_value = kept_half + partner(
            sent_half.astype(jnp.bfloat16), "ctx", low_bits + bit_level
        ).astype(sent_half.dtype)
    return partial_value.reshape(row_block, partial_value.shape[2])


def reduce_grad(full_hidden, d_query):
    return split_grad(full_hidden, d_query)


def key_value_grads(query_feats, key_feats, value_rows, d_num, scores, mixed_scores, key_input):
    local_grad = jnp.einsum("thf,the->hfe", query_feats, d_num, preferred_element_type=jnp.float32)
    later_state = prefix(local_grad, "ctx", add_states, jnp.zeros_like(local_grad), True)
    d_vals = jnp.einsum("hts,the->she", scores, d_num, preferred_element_type=jnp.float32)
    d_vals = d_vals + jnp.einsum(
        "shf,hfe->she", key_feats.astype(jnp.float32), later_state, precision=HIGHEST
    )
    d_featk = jnp.einsum(
        "hts,thf->shf", mixed_scores, query_feats, preferred_element_type=jnp.float32
    )
    d_featk = d_featk + jnp.einsum(
        "she,hfe->shf", value_rows.astype(jnp.float32), later_state, precision=HIGHEST
    )
    rows_here = key_input.shape[0]
    value_grad = d_vals.reshape(rows_here, -1).astype(jnp.bfloat16)
    key_grad = jnp.where(key_input > 0, d_featk.reshape(rows_here, -1), 0.0).astype(jnp.bfloat16)
    return (key_grad, value_grad)


def body(hidden, w_query, key_input, values, cotangent):
    rows_here = hidden.shape[0]
    head_count = HEADS_GROUP
    full_hidden = lax.all_gather(hidden, "heads", axis=1, tiled=True)
    query_proj = jnp.dot(
        full_hidden,
        lax.all_gather(w_query, "ctx", axis=0, tiled=True),
        preferred_element_type=jnp.float32,
    )
    query_feats = (
        jnp.maximum(query_proj, 0.0).astype(jnp.bfloat16).reshape(rows_here, head_count, FEAT)
    )
    key_feats = jnp.maximum(key_input, jnp.zeros_like(key_input)).reshape(
        rows_here, head_count, FEAT
    )
    value_rows = values.reshape(rows_here, head_count, HEAD_DIM)
    causal = jnp.arange(rows_here)[:, None] >= jnp.arange(rows_here)[None, :]
    raw_scores = jnp.einsum(
        "thf,shf->hts", query_feats, key_feats, preferred_element_type=jnp.float32
    )
    scores = jnp.where(causal[None], raw_scores, 0.0).astype(jnp.bfloat16)
    local_state = jnp.einsum(
        "shf,she->hfe", key_feats, value_rows, preferred_element_type=jnp.float32
    )
    prior_state = prefix(local_state, "ctx", add_states, jnp.zeros_like(local_state), False)
    numerator = jnp.einsum("hts,she->the", scores, value_rows, preferred_element_type=jnp.float32)
    numerator = numerator + jnp.einsum(
        "thf,hfe->the", query_feats.astype(jnp.float32), prior_state, precision=HIGHEST
    )
    inv_rms = lax.rsqrt(jnp.mean(numerator * numerator, axis=-1, keepdims=True) + EPSILON)
    normed = numerator * inv_rms
    attended = normed.astype(jnp.bfloat16).reshape(rows_here, head_count * HEAD_DIM)
    grad_out = cotangent.astype(jnp.float32).reshape(rows_here, head_count, HEAD_DIM)
    d_num = (
        inv_rms * (grad_out - normed * jnp.mean(grad_out * normed, axis=-1, keepdims=True))
    ).astype(jnp.bfloat16)
    mixed_raw = jnp.einsum("the,she->hts", d_num, value_rows, preferred_element_type=jnp.float32)
    mixed_scores = jnp.where(causal[None], mixed_raw, 0.0).astype(jnp.bfloat16)
    d_featq = jnp.einsum(
        "hts,shf->thf", mixed_scores, key_feats, preferred_element_type=jnp.float32
    )
    d_featq = d_featq + jnp.einsum(
        "the,hfe->thf", d_num.astype(jnp.float32), prior_state, precision=HIGHEST
    )
    d_query = jnp.where(query_proj > 0, d_featq.reshape(rows_here, head_count * FEAT), 0.0).astype(
        jnp.bfloat16
    )
    key_grad, value_grad = key_value_grads(
        query_feats, key_feats, value_rows, d_num, scores, mixed_scores, key_input
    )
    query_grad = reduce_grad(full_hidden, d_query)
    return (attended, query_grad, key_grad, value_grad)


def solution(mesh):
    return jax.shard_map(
        body,
        mesh=mesh,
        in_specs=(
            P("ctx", "heads"),
            P("ctx", "heads"),
            P("ctx", "heads"),
            P("ctx", "heads"),
            P("ctx", "heads"),
        ),
        out_specs=(P("ctx", "heads"), P("ctx", "heads"), P("ctx", "heads"), P("ctx", "heads")),
        check_vma=False,
    )
```

profile of v0, /device:TPU:0, one launch (start us, length us, event | category | flops | bytes accessed | tf_op | source)
XLA Modules:
  0.0 342.4 jit_solution(15147136410363322772)
XLA Ops:
  10.3 81.3 %all-gather.8.cloned.1.call-done = bf16[128,256,128]{2,1,0:T(8,128)(2,1)} async-done(((bf16[4,256,128]{2,1,0:T(8,128)(2,1)}), bf16[128,256,128]{2,1,0:T(8,128)(2,1)}) %all-gather.8.cloned.1.call-update) | async-done | bytes 8388624 | tf_op jit(solution)/shard_map/all_gather | solution.py:29
  91.7 78.9 %all-gather.6.cloned.1.call-done = bf16[4096,1024]{1,0:T(8,128)(2,1)} async-done(((bf16[128,1024]{1,0:T(8,128)(2,1)}), bf16[4096,1024]{1,0:T(8,128)(2,1)}) %all-gather.6.cloned.1.call-update) | async-done | bytes 8388624 | tf_op jit(solution)/shard_map/all_gather | solution.py:116
  170.6 5.4 %maximum_convert_fusion = (bf16[128,1024]{1,0:T(8,128)(2,1)S(1)}, f32[128,1024]{1,0:T(8,128)}) fusion(bf16[128,4096]{1,0:T(8,128)(2,1)S(1)} %copy-done.2, bf16[4096,1024]{1,0:T(8,128)(2,1)} %all-gather.6.cloned.1.call-done), kind=kOutput, calls=%fused_computation.49 | convolution fusion | flops 1074003968 | bytes 10223616 | tf_op jit(solution)/shard_map/dot_general | solution.py:114
  181.4 1.1 broadcast_select_fusion
  182.5 1.3 rev.13
  183.8 1.2 select_select_fusion.1
  185.0 2.4 rev.14
  188.0 1.1 copy.112
  189.1 1.5 collective-permute-start
  191.8 1.5 collective-permute-done.3
  194.2 1.4 collective-permute-start.4
  195.9 1.1 fusion.16
  197.7 13.8 %collective-permute-done.4 = bf16[2,128,1024]{2,1,0:T(8,128)(2,1)} collective-permute-done((bf16[2,128,1024]{2,1,0:T(8,128)(2,1)}, bf16[2,128,1024]{2,1,0:T(8,128)(2,1)}, u32[]{:S(2)}, u32[]{:S(2)}) %collective-permute-start.4) | collective-permute-done | bytes 524320 | tf_op jit(solution)/shard_map/ppermute | solution.py:22
  211.4 2.1 pad_maximum_fusion.2
  213.6 3.9 %collective-permute-start.5 = (bf16[4,128,1024]{2,1,0:T(8,128)(2,1)}, bf16[4,128,1024]{2,1,0:T(8,128)(2,1)}, u32[]{:S(2)}, u32[]{:S(2)}) collective-permute-start(bf16[4,128,1024]{2,1,0:T(8,128)(2,1)} %pad_maximum_fusion.2), channel_id=1, source_target_pairs={{0,4},{4,0},{1,5},{5,1},{2,6},{6,2},{3,7},{7,3},{8,12},{12,8},{9,1... | collective-permute-start | bytes 3145736 | tf_op jit(solution)/shard_map/ppermute | solution.py:22
  217.5 9.6 %collective-permute-done.1 = bf16[128,4,2,2,128]{4,0,3,2,1:T(8,128)(2,1)S(1)} collective-permute-done((bf16[128,4,2,2,128]{4,0,3,2,1:T(8,128)(2,1)S(1)}, bf16[128,4,2,2,128]{4,0,3,2,1:T(8,128)(2,1)S(1)}, u32[]{:S(2)}, u32[]{:S(2)}) %collective-permute-start.1) | collective-permute-done | bytes 524320 | tf_op jit(solution)/shard_map/ppermute | solution.py:22
  227.2 2.8 collective-permute-start.2
  230.0 34.0 %collective-permute-done.2 = bf16[128,4,1,4,128]{4,0,3,1,2:T(8,128)(2,1)S(1)} collective-permute-done((bf16[128,4,1,4,128]{4,0,3,1,2:T(8,128)(2,1)S(1)}, bf16[128,4,1,4,128]{4,0,3,1,2:T(8,128)(2,1)S(1)}, u32[]{:S(2)}, u32[]{:S(2)}) %collective-permute-start.2) | collective-permute-done | bytes 524320 | tf_op jit(solution)/shard_map/ppermute | solution.py:22
  264.8 1.1 pad_maximum_fusion.1
  266.0 1.3 copy.114
  267.3 2.9 fusion.7
  270.3 1.4 copy-done.3
  271.7 1.6 collective-permute-start.6
  273.3 10.8 %collective-permute-done.6 = bf16[2,128,1024]{2,1,0:T(8,128)(2,1)S(1)} collective-permute-done((bf16[2,128,1024]{2,1,0:T(8,128)(2,1)S(1)}, bf16[2,128,1024]{2,1,0:T(8,128)(2,1)S(1)}, u32[]{:S(2)}, u32[]{:S(2)}) %collective-permute-start.6) | collective-permute-done | bytes 524320 | tf_op jit(solution)/shard_map/ppermute | solution.py:22
  284.2 1.8 fusion.14
  287.4 10.5 %collective-permute-done.7 = bf16[1,128,1024]{2,1,0:T(8,128)(2,1)S(1)} collective-permute-done((bf16[1,128,1024]{2,1,0:T(8,128)(2,1)S(1)}, bf16[1,128,1024]{2,1,0:T(8,128)(2,1)S(1)}, u32[]{:S(2)}, u32[]{:S(2)}) %collective-permute-start.7) | collective-permute-done | bytes 262176 | tf_op jit(solution)/shard_map/ppermute | solution.py:22
  298.8 33.9 %while.23 = (s32[]{:T(128)}, f32[4,256,128]{2,1,0:T(8,128)S(1)}, s32[]{:T(128)}, bf16[32,4,256,128]{3,2,1,0:T(8,128)(2,1)}, s32[]{:T(128)}, /*index=5*/s32[]{:T(128)}, s32[]{:T(128)}, s32[]{:T(128)}) while((s32[]{:T(128)}, f32[4,256,128]{2,1,0:T(8,128)S(1)}, s32[]{:T(128)}, bf16[32,4,256,128]{3,2,1,0:T(8,128)(2,1)}, s32[]{:T(128)}, ...), condition=%wide.region_5.6_spmd, body=%wide.region_4.5_spmd.sunk | while | flops 262150 | bytes 1310855 | solution.py:36
  298.8 1.1 convert_add_fusion.5
  299.9 1.1 convert_add_fusion.5
  306.5 1.1 convert_add_fusion.5
  307.5 1.1 convert_add_fusion.5
  308.6 1.1 convert_add_fusion.5
  (104 shorter events, 46.2 us)
Async XLA Ops:
  7.2 1.3 copy-start
  7.2 3.0 copy-start.12
  7.2 84.5 %all-gather.8.cloned.1.call-start = ((), (), s32[]{:S(2)}) async-start(), calls=%async_computation.1 | async-start | bytes 8650752 | tf_op jit(solution)/shard_map/all_gather | solution.py:29
  9.4 161.2 %all-gather.6.cloned.1.call-start = ((), (), s32[]{:S(2)}) async-start(), calls=%async_computation | async-start | bytes 8650752 | tf_op jit(solution)/shard_map/all_gather | solution.py:116
  10.2 288.6 %all-gather.10.cloned.1.call-start = ((), (), s32[]{:S(2)}) async-start(), calls=%async_computation.2 | async-start | bytes 8650752 | tf_op jit(solution)/shard_map/all_gather | solution.py:29
  91.7 78.9 %copy-start.2 = (bf16[128,4096]{1,0:T(8,128)(2,1)S(1)}, bf16[128,4096]{1,0:T(8,128)(2,1)}, u32[]{:S(2)}) copy-start(bf16[128,4096]{1,0:T(8,128)(2,1)} %param.9) | copy-start | bytes 3145732
  176.5 0.7 copy-start.10
  178.6 1.0 copy-start.5
  180.4 1.0 copy-start.1
  187.9 2.7 copy-start.6
  188.0 3.6 %copy-start.4 = (f32[128,1024]{1,0:T(8,128)S(1)}, f32[128,1024]{1,0:T(8,128)}, u32[]{:S(2)}) copy-start(f32[128,1024]{1,0:T(8,128)} %get-tuple-element.126) | copy-start | bytes 1572868
  189.1 6.7 %collective-permute-start = (bf16[128,4,4,1,128]{4,0,3,2,1:T(8,128)(2,1)}, bf16[128,4,4,1,128]{4,0,3,2,1:T(8,128)(2,1)}, u32[]{:S(2)}, u32[]{:S(2)}) collective-permute-start(bf16[128,4,4,1,128]{4,0,3,2,1:T(8,128)(2,1)} %bitcast.176), channel_id=1, source_target_pairs={{0,1},{1,0},{2,3},{3,2},{4,5},{5,4},{6,7},{7,6},{8,9},{9,8},{10,11... | collective-permute-start | bytes 1572872 | tf_op jit(solution)/shard_map/ppermute | solution.py:22
  191.7 1.6 collective-permute-start.3
  194.2 17.3 %collective-permute-start.4 = (bf16[2,128,1024]{2,1,0:T(8,128)(2,1)}, bf16[2,128,1024]{2,1,0:T(8,128)(2,1)}, u32[]{:S(2)}, u32[]{:S(2)}) collective-permute-start(bf16[2,128,1024]{2,1,0:T(8,128)(2,1)} %pad_maximum_fusion.4), channel_id=1, source_target_pairs={{0,2},{2,0},{1,3},{3,1},{4,6},{6,4},{5,7},{7,5},{8,10},{10,8},{9,1... | collective-permute-start | bytes 1572872 | tf_op jit(solution)/shard_map/ppermute | solution.py:22
  197.0 30.0 %collective-permute-start.1 = (bf16[128,4,2,2,128]{4,0,3,2,1:T(8,128)(2,1)S(1)}, bf16[128,4,2,2,128]{4,0,3,2,1:T(8,128)(2,1)S(1)}, u32[]{:S(2)}, u32[]{:S(2)}) collective-permute-start(bf16[128,4,2,2,128]{4,0,3,2,1:T(8,128)(2,1)S(1)} %get-tuple-element.120), channel_id=1, source_target_pairs={{0,2},{2,0},{1,3},{3,1},{4,6},{6,4},{5,7},{7,5},{8,10},{10,8},{9,1... | collective-permute-start | bytes 1572872 | tf_op jit(solution)/shard_map/ppermute | solution.py:22
  213.6 53.7 %collective-permute-start.5 = (bf16[4,128,1024]{2,1,0:T(8,128)(2,1)}, bf16[4,128,1024]{2,1,0:T(8,128)(2,1)}, u32[]{:S(2)}, u32[]{:S(2)}) collective-permute-start(bf16[4,128,1024]{2,1,0:T(8,128)(2,1)} %pad_maximum_fusion.2), channel_id=1, source_target_pairs={{0,4},{4,0},{1,5},{5,1},{2,6},{6,2},{3,7},{7,3},{8,12},{12,8},{9,1... | collective-permute-start | bytes 3145736 | tf_op jit(solution)/shard_map/ppermute | solution.py:22
  227.2 36.8 %collective-permute-start.2 = (bf16[128,4,1,4,128]{4,0,3,1,2:T(8,128)(2,1)S(1)}, bf16[128,4,1,4,128]{4,0,3,1,2:T(8,128)(2,1)S(1)}, u32[]{:S(2)}, u32[]{:S(2)}) collective-permute-start(bf16[128,4,1,4,128]{4,0,3,1,2:T(8,128)(2,1)S(1)} %get-tuple-element.118), channel_id=1, source_target_pairs={{0,4},{4,0},{1,5},{5,1},{2,6},{6,2},{3,7},{7,3},{8,12},{12,8},{9,1... | collective-permute-start | bytes 1572872 | tf_op jit(solution)/shard_map/ppermute | solution.py:22
  264.1 0.8 copy-start.9
  270.3 1.4 copy-start.3
  271.7 12.4 %collective-permute-start.6 = (bf16[2,128,1024]{2,1,0:T(8,128)(2,1)S(1)}, bf16[2,128,1024]{2,1,0:T(8,128)(2,1)S(1)}, u32[]{:S(2)}, u32[]{:S(2)}) collective-permute-start(bf16[2,128,1024]{2,1,0:T(8,128)(2,1)S(1)} %fusion.15), channel_id=1, source_target_pairs={{0,8},{8,0},{1,9},{9,1},{2,10},{10,2},{3,11},{11,3},{4,12},{12,4},... | collective-permute-start | bytes 1572872 | tf_op jit(solution)/shard_map/ppermute | solution.py:22
  273.3 13.1 %copy-start.8 = (bf16[128,4,128]{0,2,1:T(8,128)(2,1)S(1)}, bf16[128,4,128]{0,2,1:T(8,128)(2,1)}, u32[]{:S(2)}) copy-start(bf16[128,4,128]{0,2,1:T(8,128)(2,1)} %get-tuple-element.124) | copy-start | bytes 393220
  273.3 13.9 %copy-start.11 = (bf16[4,128,128]{2,1,0:T(8,128)(2,1)S(1)}, bf16[4,128,128]{2,1,0:T(8,128)(2,1)}, u32[]{:S(2)}) copy-start(bf16[4,128,128]{2,1,0:T(8,128)(2,1)} %copy-done.10) | copy-start | bytes 393220
  286.0 11.8 %collective-permute-start.7 = (bf16[1,128,1024]{2,1,0:T(8,128)(2,1)S(1)}, bf16[1,128,1024]{2,1,0:T(8,128)(2,1)S(1)}, u32[]{:S(2)}, u32[]{:S(2)}) collective-permute-start(bf16[1,128,1024]{2,1,0:T(8,128)(2,1)S(1)} %fusion.20), channel_id=1, source_target_pairs={{0,16},{16,0},{1,17},{17,1},{2,18},{18,2},{3,19},{19,3},{4,20},{20... | collective-permute-start | bytes 786440 | tf_op jit(solution)/shard_map/ppermute | solution.py:22
  332.7 1.0 copy-start.7
Sparse Core Ops, SparseCore 0:
  11.5 80.1 all-gather.7
  94.5 76.0 all-gather.5
  179.7 97.6 all-gather.9
where the time goes:
time: 344 us; the launch traced here: 342 us
  waiting for transfers between devices  241 us (70%)
  other arithmetic  46.7 us (14%)
  between operations  14.1 us (4%)
  matrix products  13.7 us (4%)
  local copies, waits for them, and re-layouts  13.5 us (4%)
  starting transfers between devices  12.4 us (4%)
    all_gather x2, waiting for transfers between devices, prefix(): gathered = lax.all_gather(array.astype(jnp.bfloat16), axis)  81.3 us
    ppermute x8, waiting for transfers between devices, partner(): return lax.ppermute(block, axis, route)  80.2 us
    all_gather x1, waiting for transfers between devices, body(): lax.all_gather(w_query, 'ctx', axis=0, tiled=True)  78.9 us
    add x31, other arithmetic, add_states(): return earlier + later_one  33 us
    ppermute x8, starting transfers between devices, partner(): return lax.ppermute(block, axis, route)  12.3 us
  transfers between devices with their start and end apart: 11, of which 8 were waited for; matrix products, arithmetic and copies ran while one was open for 7% of the time, Pallas kernels for 0%

commit v1 on v0

v1 whole, which is shorter than its diff:
```python
import functools

import jax
import jax.numpy as jnp
from jax import lax
from jax.experimental import pallas as pl
from jax.experimental.pallas import tpu as pltpu
from jax.sharding import PartitionSpec as P

HEAD_DIM = 128
FEAT = 256
HEADS_GROUP = 4
CORES = 2
EPSILON = 1e-06

F32 = jnp.float32
BF16 = jnp.bfloat16
HALF = FEAT // 2


def dot(a, b, dims=((1,), (0,))):
    return lax.dot_general(a, b, (dims, ((), ())), preferred_element_type=F32)


def split(x):
    high = x.astype(BF16)
    return high, (x - high.astype(F32)).astype(BF16)


def call(kernel, outs, args, flops=0, scratch=(), mib=48):
    shapes = [jax.ShapeDtypeStruct(shape, dtype) for shape, dtype in outs]
    moved = sum(a.size * a.dtype.itemsize for a in args) + sum(s.size * s.dtype.itemsize for s in shapes)
    return pl.pallas_call(
        kernel,
        out_shape=shapes,
        in_specs=[pl.BlockSpec(memory_space=pltpu.SMEM)]
        + [pl.BlockSpec(memory_space=pltpu.VMEM)] * (len(args) - 1),
        out_specs=[pl.BlockSpec(memory_space=pltpu.VMEM)] * len(shapes),
        scratch_shapes=list(scratch),
        compiler_params=pltpu.CompilerParams(vmem_limit_bytes=mib << 20),
        cost_estimate=pl.CostEstimate(flops=flops, bytes_accessed=moved, transcendentals=0),
    )(*args)


def lanes(index, width):
    return pl.ds(pl.multiple_of(index * width, width), width)


def pack_kernel(place, w, key, val, cot, *outs):
    rows, depth = key.shape[0], w.shape[0]
    for k, out in enumerate(outs):
        head = place[0] ^ k
        out[:depth, :] = w[:, lanes(head, FEAT)]
        out[depth : depth + rows, :] = key[:, lanes(head, FEAT)]
        out[depth + rows :, :HEAD_DIM] = val[:, lanes(head, HEAD_DIM)]
        out[depth + rows :, HEAD_DIM:] = cot[:, lanes(head, HEAD_DIM)]


def state_kernel(rows, depth, place, p0, p1, p2, p3, pay, states):
    total = jnp.zeros((FEAT, HEAD_DIM), F32)
    for j, p in enumerate((p0, p1, p2, p3)):
        pay[j * depth : (j + 1) * depth, :] = p[:depth, :]
        keys = jnp.maximum(p[depth : depth + rows, :], 0)
        state = dot(keys, p[depth + rows :, :HEAD_DIM], ((0,), (0,)))
        states[j] = state.astype(BF16)
        total = total + state
    total = total.astype(BF16)
    pay[4 * depth :, :HEAD_DIM] = total[:HALF, :]
    pay[4 * depth :, HEAD_DIM:] = total[HALF:, :]


def hidden_columns(h, start, width):
    cols = pl.ds(start, width)
    return jnp.concatenate([ref[:, cols] for ref in h], axis=0)


def attend_kernel(rows, depth, outer, place, *refs):
    h, refs = refs[:7], refs[7:]
    p, refs = refs[:4], refs[4:]
    own_pay, refs = refs[:outer], refs[outer:]
    other_pay, refs = refs[:outer], refs[outer:]
    own_states, other_states, att, dq_t, grown, grown_sum, val_part, key_part, weights, proj = refs
    q, z, core = place[0], place[1], place[2]
    base = jnp.zeros((FEAT, HEAD_DIM), F32)
    for k in range(outer):
        for flip, pay in ((0, own_pay[k]), (1, other_pay[k])):
            for j in range(4):
                at = (((z ^ k) * 4 + (q ^ j)) * CORES + (core ^ flip)) * depth
                weights[pl.ds(pl.multiple_of(at, depth), depth), :] = pay[j * depth : (j + 1) * depth, :]
            if k:
                seen = ((z ^ k) < z).astype(jnp.int32).astype(F32)
                packed = pay[4 * depth :, :].astype(F32)
                base = base + seen * jnp.concatenate([packed[:, :HEAD_DIM], packed[:, HEAD_DIM:]], axis=0)
    width = h[0].shape[1]
    step = min(512, width)
    for at in range(0, width, step):
        part = dot(hidden_columns(h, at, step), weights[at : at + step, :])
        if at:
            proj[...] += part
        else:
            proj[...] = part
    own = [own_states[j].astype(F32) for j in range(4)]
    other = [other_states[j].astype(F32) for j in range(4)]
    causal = lax.broadcasted_iota(jnp.int32, (rows, rows), 0) >= lax.broadcasted_iota(
        jnp.int32, (rows, rows), 1
    )
    total = jnp.zeros((FEAT, HEAD_DIM), F32)
    for j in range(4):
        here = (q ^ j) * CORES + core
        prior = base
        for i in range(4):
            for flip, group in ((0, own), (1, other)):
                if flip == 0 and i == j:
                    continue
                there = (q ^ i) * CORES + (core ^ flip)
                prior = prior + (there < here).astype(jnp.int32).astype(F32) * group[i]
        prior_high, prior_low = split(prior)
        block = slice(j * rows, (j + 1) * rows)
        query = proj[block, :]
        feats = jnp.maximum(query, 0.0).astype(BF16)
        keys = jnp.maximum(p[j][depth : depth + rows, :], 0)
        vals = p[j][depth + rows :, :HEAD_DIM]
        grad = p[j][depth + rows :, HEAD_DIM:].astype(F32)
        scores = jnp.where(causal, dot(feats, keys, ((1,), (1,))), 0.0).astype(BF16)
        numer = dot(scores, vals) + dot(feats, prior_high) + dot(feats, prior_low)
        inv = lax.rsqrt(jnp.mean(numer * numer, axis=-1, keepdims=True) + EPSILON)
        normed = numer * inv
        att[j] = normed.astype(BF16)
        d_num = (inv * (grad - normed * jnp.mean(grad * normed, axis=-1, keepdims=True))).astype(BF16)
        mixed = jnp.where(causal, dot(d_num, vals, ((1,), (1,))), 0.0).astype(BF16)
        d_feat = dot(mixed, keys) + dot(d_num, prior_high, ((1,), (1,))) + dot(d_num, prior_low, ((1,), (1,)))
        d_query = jnp.where(query > 0, d_feat, 0.0)
        dq_t[:, block] = d_query.T.astype(BF16)
        grown_j = dot(feats, d_num, ((0,), (0,)))
        grown[j] = grown_j.astype(BF16)
        total = total + grown_j
        val_part[block, :] = dot(scores, d_num, ((0,), (0,)))
        key_part[block, :] = dot(mixed, feats, ((0,), (0,)))
    grown_sum[...] = total.astype(BF16)


def grad_kernel(depth, outer, place, *refs):
    h, dq_t, keep, give = refs[:7], refs[7], refs[8], refs[9:]
    z, core = place[1], place[2]
    pair = CORES * depth
    lhs = dq_t[...]
    for k in range(outer):
        for i in range(4):
            start = pl.multiple_of(((z ^ k) * 4 + i) * pair, pair)
            out = dot(lhs, hidden_columns(h, start, pair))
            even, odd = out[:, :depth], out[:, depth:]
            first = jnp.broadcast_to(core == 0, even.shape)
            keep[k, :, i * depth : (i + 1) * depth] = jnp.where(first, even, odd)
            give[k][:, i * depth : (i + 1) * depth] = jnp.where(first, odd, even).astype(BF16)


def add_kernel(outer, place, keep, *refs):
    gifts, own, outs = refs[:outer], refs[outer], refs[outer + 1 :]
    for k in range(outer):
        total = keep[k] + gifts[k][...].astype(F32)
        if k:
            outs[k - 1][...] = total.astype(BF16)
        else:
            own[...] = total


def sum_kernel(depth, place, own, *refs):
    arrived, (mine, *outs), blocks = refs[:-5], refs[-5:-1], refs[-1]
    total = own[...]
    for ref in arrived:
        total = total + ref[...].astype(F32)
    for i in range(4):
        blocks[place[0] ^ i] = total[:, i * depth : (i + 1) * depth]
    mine[...] = blocks[0]
    for k, out in enumerate(outs):
        out[...] = blocks[k + 1].astype(BF16)


def query_grad_kernel(place, *refs):
    out = refs[-1]
    for k, ref in enumerate(refs[:-1]):
        out[:, lanes(place[0] ^ k, FEAT)] = ref[...].astype(F32).T


def finish_kernel(rows, depth, outer, place, *refs):
    p, refs = refs[:4], refs[4:]
    att, val_part, key_part, own_grown, other_grown, own_rest, other_rest, *outs = refs
    q, core = place[0], place[2]
    base = own_rest[...].astype(F32) + other_rest[...].astype(F32)
    own = [own_grown[j].astype(F32) for j in range(4)]
    other = [other_grown[j].astype(F32) for j in range(4)]
    for j, out in enumerate(outs):
        here = (q ^ j) * CORES + core
        later = base
        for i in range(4):
            for flip, group in ((0, own), (1, other)):
                if flip == 0 and i == j:
                    continue
                there = (q ^ i) * CORES + (core ^ flip)
                later = later + (there > here).astype(jnp.int32).astype(F32) * group[i]
        high, low = split(later)
        block = slice(j * rows, (j + 1) * rows)
        raw = p[j][depth : depth + rows, :]
        keys = jnp.maximum(raw, 0)
        vals = p[j][depth + rows :, :HEAD_DIM]
        d_val = val_part[block, :] + dot(keys, high) + dot(keys, low)
        d_key = key_part[block, :] + dot(vals, high, ((1,), (1,))) + dot(vals, low, ((1,), (1,)))
        out[:, :HEAD_DIM] = att[j]
        out[:, HEAD_DIM : 2 * HEAD_DIM] = d_val.astype(BF16)
        out[:, 2 * HEAD_DIM :] = jnp.where(raw.astype(F32) > 0, d_key, 0.0).astype(BF16)


def place_kernel(place, *refs):
    att, key_grad, val_grad = refs[-3:]
    for k, ref in enumerate(refs[:-3]):
        head = place[0] ^ k
        att[:, lanes(head, HEAD_DIM)] = ref[:, :HEAD_DIM]
        val_grad[:, lanes(head, HEAD_DIM)] = ref[:, HEAD_DIM : 2 * HEAD_DIM]
        key_grad[:, lanes(head, FEAT)] = ref[:, 2 * HEAD_DIM :]


def body(hidden, w_query, key_input, values, cotangent):
    count = lax.axis_size("ctx")
    me = lax.axis_index("ctx")
    inner = CORES * HEADS_GROUP
    outer = count // inner
    rows, depth = key_input.shape[0], w_query.shape[0]
    if lax.axis_size("heads") > 1:
        hidden = lax.all_gather(hidden, "heads", axis=1, tiled=True)
    width = hidden.shape[1]
    place = jnp.stack([me // CORES % HEADS_GROUP, me // inner, me % CORES]).astype(jnp.int32)

    def swap(block, bits):
        return lax.ppermute(block, "ctx", [(i, i ^ bits) for i in range(count)])

    def core_swap(block):
        return swap(block, 1)

    def chip_swap(block, k):
        return swap(block, CORES * k)

    def plane_swap(block, k):
        return swap(block, inner * k)

    def down(block, k):
        return lax.ppermute(block, "ctx", [(i, i - inner * k) for i in range(inner * k, count)])

    packs = call(
        pack_kernel,
        [((depth + 2 * rows, FEAT), BF16)] * 4,
        [place, w_query, key_input, values, cotangent],
    )
    p = [packs[0]] + [chip_swap(packs[k], k) for k in (1, 2, 3)]
    top, bottom = hidden[: rows // 2], hidden[rows // 2 :]
    h1t = chip_swap(top, 1)
    h2b = chip_swap(bottom, 2)
    h3t = chip_swap(h1t, 2)
    h3b = chip_swap(h2b, 1)
    h1b = chip_swap(bottom, 1)
    h2t = chip_swap(top, 2)
    h = [hidden, h1t, h1b, h2t, h2b, h3t, h3b]
    pay, states = call(
        functools.partial(state_kernel, rows, depth),
        [((4 * depth + HALF, FEAT), BF16), ((4, FEAT, HEAD_DIM), BF16)],
        [place, *p],
        flops=2 * 4 * rows * FEAT * HEAD_DIM,
    )
    pays = [pay] + [None] * (outer - 1)
    for k in reversed(range(1, outer)):
        pays[k] = plane_swap(pay, k)
    other_pays = [core_swap(pays[k]) for k in range(outer)]
    other_states = core_swap(states)
    positions = 4 * rows
    att, dq_t, grown, grown_sum, val_part, key_part = call(
        functools.partial(attend_kernel, rows, depth, outer),
        [
            ((4, rows, HEAD_DIM), BF16),
            ((FEAT, positions), BF16),
            ((4, FEAT, HEAD_DIM), BF16),
            ((FEAT, HEAD_DIM), BF16),
            ((positions, HEAD_DIM), F32),
            ((positions, FEAT), F32),
        ],
        [place, *h, *p, *pays, *other_pays, states, other_states],
        flops=2 * positions * width * FEAT + 24 * positions * FEAT * HEAD_DIM,
        scratch=[pltpu.VMEM((width, FEAT), BF16), pltpu.VMEM((positions, FEAT), F32)],
    )
    other_grown = core_swap(grown)
    later = [down(grown_sum, k) for k in range(1, outer)]
    keep, *give = call(
        functools.partial(grad_kernel, depth, outer),
        [((outer, FEAT, 4 * depth), F32)] + [((FEAT, 4 * depth), BF16)] * outer,
        [place, *h, dq_t],
        flops=2 * positions * width * FEAT,
    )
    gifts = [core_swap(g) for g in give]
    own, *sent = call(
        functools.partial(add_kernel, outer),
        [((FEAT, 4 * depth), F32)] + [((FEAT, 4 * depth), BF16)] * (outer - 1),
        [place, keep, *gifts],
    )
    arrived = [plane_swap(sent[k - 1], k) for k in reversed(range(1, outer))]
    rest = sum((x.astype(F32) for x in later), jnp.zeros((FEAT, HEAD_DIM), F32)).astype(BF16)
    other_rest = core_swap(rest)
    outs = call(
        functools.partial(finish_kernel, rows, depth, outer),
        [((rows, 2 * HEAD_DIM + FEAT), BF16)] * 4,
        [place, *p, att, val_part, key_part, grown, other_grown, rest, other_rest],
        flops=16 * positions * FEAT * HEAD_DIM,
    )
    placed = [outs[0]] + [chip_swap(outs[k], k) for k in (1, 2, 3)]
    attended, key_grad, value_grad = call(
        place_kernel,
        [
            ((rows, HEADS_GROUP * HEAD_DIM), BF16),
            ((rows, HEADS_GROUP * FEAT), BF16),
            ((rows, HEADS_GROUP * HEAD_DIM), BF16),
        ],
        [place, *placed],
    )
    blocks = call(
        functools.partial(sum_kernel, depth),
        [((FEAT, depth), F32)] + [((FEAT, depth), BF16)] * 3,
        [place, own, *arrived],
        scratch=[pltpu.VMEM((4, FEAT, depth), F32)],
    )
    columns = [blocks[0]] + [chip_swap(blocks[k], k) for k in (1, 2, 3)]
    (query_grad,) = call(
        query_grad_kernel, [((depth, HEADS_GROUP * FEAT), F32)], [place, *columns]
    )
    return (attended, query_grad, key_grad, value_grad)


def solution(mesh):
    return jax.shard_map(
        body,
        mesh=mesh,
        in_specs=(P("ctx", "heads"),) * 5,
        out_specs=(P("ctx", "heads"),) * 4,
        check_vma=False,
    )
```

time: 344 us -> 129 us (0.38)
  waiting for transfers between devices: 241 us -> 63.4 us
  other arithmetic: 46.7 us -> 0.11 us
  starting transfers between devices: 12.4 us -> 35.5 us
  Pallas kernels: 0 us -> 17.2 us
  matrix products: 13.7 us -> 0 us
  between operations: 14.1 us -> 0.9 us
    all_gather x3 -> x0, waiting for transfers between devices: 160 us -> none  [the longest x2 81.3 us: prefix(): gathered = lax.all_gather(array.astype(jnp.bfloat16), axis)]
    add x31 -> x0, other arithmetic: 33 us -> none  [add_states(): return earlier + later_one]
    ppermute x8 -> x35, starting transfers between devices: 12.3 us -> 35.5 us  [the longest x32 31.6 us: swap(): return lax.ppermute(block, 'ctx', [(i, i ^ bits) for i in range(count)])]
    pallas_call x0 -> x9, Pallas kernels: none -> 17.2 us  [call(): pl.pallas_call(kernel, out_shape=shapes, in_specs=[pl.BlockSpec(memory_sp...]
    ppermute x8 -> x35, waiting for transfers between devices: 80.2 us -> 63.4 us  [the longest x32 63.4 us: swap(): return lax.ppermute(block, 'ctx', [(i, i ^ bits) for i in range(count)])]
    dot_general x14 -> x0, matrix products: 13.7 us -> none  [the longest x1 5.43 us: body(): jnp.dot(full_hidden, lax.all_gather(w_query, 'ctx', axis=0, tiled=True),...]
    unnamed x30 -> x34, local copies, waits for them, and re-layouts: 6.15 us -> 11.4 us
    rev x3 -> x0, local copies, waits for them, and re-layouts: 3.8 us -> none  [split_grad(): flipped = jnp.flip(shaped, axis=3).reshape(columns.shape)]
  transfers between devices with their start and end apart: 11 -> 35, of which waited for: 8 -> 15; matrix products, arithmetic and copies ran while one was open for 7% -> 0% of each run, Pallas kernels for 0% -> 3%
where the time goes in v1:
time: 129 us
  waiting for transfers between devices  63.4 us (49%)
  starting transfers between devices  35.5 us (28%)
  Pallas kernels  17.2 us (13%)
  local copies, waits for them, and re-layouts  11.4 us (9%)
    ppermute x32, waiting for transfers between devices, swap(): return lax.ppermute(block, 'ctx', [(i, i ^ bits) for i in range(count)])  63.4 us
    ppermute x32, starting transfers between devices, swap(): return lax.ppermute(block, 'ctx', [(i, i ^ bits) for i in range(count)])  31.6 us
    pallas_call x9, Pallas kernels, call(): pl.pallas_call(kernel, out_shape=shapes, in_specs=[pl.BlockSpec(memory_sp...  17.2 us
    unnamed x34, local copies, waits for them, and re-layouts  11.4 us
    ppermute x3, starting transfers between devices, down(): lax.ppermute(block, 'ctx', [(i, i - inner * k) for i in range(inner * k,...  3.86 us
  transfers between devices with their start and end apart: 35, of which 15 were waited for; matrix products, arithmetic and copies ran while one was open for 0% of the time, Pallas kernels for 3%

profile of v1, /device:TPU:0, one launch (start us, length us, event | category | flops | bytes accessed | tf_op | source)
XLA Modules:
  0.0 128.5 jit_solution(14937069092431579827)
XLA Ops:
  5.2 3.0 %collective-permute-start = (bf16[384,256]{1,0:T(8,128)(2,1)S(1)}, bf16[384,256]{1,0:T(8,128)(2,1)S(1)}, u32[]{:S(2)}, u32[]{:S(2)}) collective-permute-start(bf16[384,256]{1,0:T(8,128)(2,1)S(1)} %get-tuple-element.37), channel_id=1, source_target_pairs={{0,2},{1,3},{2,0},{3,1},{4,6},{5,7},{6,4},{7,5},{8,10},{9,11},{10,... | collective-permute-start | bytes 589832 | tf_op jit(solution)/shard_map/ppermute | solution.py:234
  8.2 1.5 %collective-permute-start.1 = (bf16[384,256]{1,0:T(8,128)(2,1)S(1)}, bf16[384,256]{1,0:T(8,128)(2,1)S(1)}, u32[]{:S(2)}, u32[]{:S(2)}) collective-permute-start(bf16[384,256]{1,0:T(8,128)(2,1)S(1)} %get-tuple-element.38), channel_id=1, source_target_pairs={{0,4},{1,5},{2,6},{3,7},{4,0},{5,1},{6,2},{7,3},{8,12},{9,13},{10,... | collective-permute-start | bytes 589832 | tf_op jit(solution)/shard_map/ppermute | solution.py:234
  9.7 4.2 %collective-permute-done.p1.refs_8_.refs_1_ = bf16[384,256]{1,0:T(8,128)(2,1)S(1)} collective-permute-done((bf16[384,256]{1,0:T(8,128)(2,1)S(1)}, bf16[384,256]{1,0:T(8,128)(2,1)S(1)}, u32[]{:S(2)}, u32[]{:S(2)}) %collective-permute-start) | collective-permute-done | bytes 196640 | tf_op jit(solution)/shard_map/ppermute | solution.py:234
  13.9 4.8 %collective-permute-done.1.p2.refs_9_.refs_2_ = bf16[384,256]{1,0:T(8,128)(2,1)S(1)} collective-permute-done((bf16[384,256]{1,0:T(8,128)(2,1)S(1)}, bf16[384,256]{1,0:T(8,128)(2,1)S(1)}, u32[]{:S(2)}, u32[]{:S(2)}) %collective-permute-start.1) | collective-permute-done | bytes 196640 | tf_op jit(solution)/shard_map/ppermute | solution.py:234
  19.7 3.7 %collective-permute-start.11 = (bf16[640,256]{1,0:T(8,128)(2,1)S(1)}, bf16[640,256]{1,0:T(8,128)(2,1)S(1)}, u32[]{:S(2)}, u32[]{:S(2)}) collective-permute-start(bf16[640,256]{1,0:T(8,128)(2,1)S(1)} %get-tuple-element.40.refs_11_), channel_id=1, source_target_pairs={{0,24},{1,25},{2,26},{3,27},{4,28},{5,29},{6,30},{7,31},{8,16},{9,... | collective-permute-start | bytes 983048 | tf_op jit(solution)/shard_map/ppermute | solution.py:234
  23.6 1.6 %collective-permute-start.6 = (bf16[64,4096]{1,0:T(8,128)(2,1)S(1)}, bf16[64,4096]{1,0:T(8,128)(2,1)S(1)}, u32[]{:S(2)}, u32[]{:S(2)}) collective-permute-start(bf16[64,4096]{1,0:T(8,128)(2,1)S(1)} %get-tuple-element.68), channel_id=1, source_target_pairs={{0,4},{1,5},{2,6},{3,7},{4,0},{5,1},{6,2},{7,3},{8,12},{9,13},{10,... | collective-permute-start | bytes 1572872 | tf_op jit(solution)/shard_map/ppermute | solution.py:234
  25.7 1.6 %collective-permute-start.4 = (bf16[64,4096]{1,0:T(8,128)(2,1)S(1)}, bf16[64,4096]{1,0:T(8,128)(2,1)S(1)}, u32[]{:S(2)}, u32[]{:S(2)}) collective-permute-start(bf16[64,4096]{1,0:T(8,128)(2,1)S(1)} %get-tuple-element.68), channel_id=1, source_target_pairs={{0,2},{1,3},{2,0},{3,1},{4,6},{5,7},{6,4},{7,5},{8,10},{9,11},{10,... | collective-permute-start | bytes 1572872 | tf_op jit(solution)/shard_map/ppermute | solution.py:234
  27.3 4.8 %collective-permute-done.11.refs_14_ = bf16[640,256]{1,0:T(8,128)(2,1)S(1)} collective-permute-done((bf16[640,256]{1,0:T(8,128)(2,1)S(1)}, bf16[640,256]{1,0:T(8,128)(2,1)S(1)}, u32[]{:S(2)}, u32[]{:S(2)}) %collective-permute-start.11) | collective-permute-done | bytes 327712 | tf_op jit(solution)/shard_map/ppermute | solution.py:234
  32.1 1.5 %collective-permute-start.5 = (bf16[64,4096]{1,0:T(8,128)(2,1)S(1)}, bf16[64,4096]{1,0:T(8,128)(2,1)S(1)}, u32[]{:S(2)}, u32[]{:S(2)}) collective-permute-start(bf16[64,4096]{1,0:T(8,128)(2,1)S(1)} %get-tuple-element.69), channel_id=1, source_target_pairs={{0,4},{1,5},{2,6},{3,7},{4,0},{5,1},{6,2},{7,3},{8,12},{9,13},{10,... | collective-permute-start | bytes 1572872 | tf_op jit(solution)/shard_map/ppermute | solution.py:234
  33.7 18.2 %collective-permute-done.10.refs_13_ = bf16[640,256]{1,0:T(8,128)(2,1)S(1)} collective-permute-done((bf16[640,256]{1,0:T(8,128)(2,1)S(1)}, bf16[640,256]{1,0:T(8,128)(2,1)S(1)}, u32[]{:S(2)}, u32[]{:S(2)}) %collective-permute-start.10) | collective-permute-done | bytes 327712 | tf_op jit(solution)/shard_map/ppermute | solution.py:234
  51.9 1.3 %collective-permute-start.8 = (bf16[64,4096]{1,0:T(8,128)(2,1)S(1)}, bf16[64,4096]{1,0:T(8,128)(2,1)S(1)}, u32[]{:S(2)}, u32[]{:S(2)}) collective-permute-start(bf16[64,4096]{1,0:T(8,128)(2,1)S(1)} %collective-permute-done.6.refs_4_), channel_id=1, source_target_pairs={{0,2},{1,3},{2,0},{3,1},{4,6},{5,7},{6,4},{7,5},{8,10},{9,11},{10,... | collective-permute-start | bytes 1572872 | tf_op jit(solution)/shard_map/ppermute | solution.py:234
  54.0 7.1 %collective-permute-done.9.refs_12_ = bf16[640,256]{1,0:T(8,128)(2,1)S(1)} collective-permute-done((bf16[640,256]{1,0:T(8,128)(2,1)S(1)}, bf16[640,256]{1,0:T(8,128)(2,1)S(1)}, u32[]{:S(2)}, u32[]{:S(2)}) %collective-permute-start.9) | collective-permute-done | bytes 327712 | tf_op jit(solution)/shard_map/ppermute | solution.py:234
  63.7 1.7 %collective-permute-done.8.refs_6_ = bf16[64,4096]{1,0:T(8,128)(2,1)S(1)} collective-permute-done((bf16[64,4096]{1,0:T(8,128)(2,1)S(1)}, bf16[64,4096]{1,0:T(8,128)(2,1)S(1)}, u32[]{:S(2)}, u32[]{:S(2)}) %collective-permute-start.8) | collective-permute-done | bytes 524320 | tf_op jit(solution)/shard_map/ppermute | solution.py:234
  67.2 6.9 %shard_map.86 = (bf16[4,128,128]{2,1,0:T(8,128)(2,1)S(1)}, bf16[256,512]{1,0:T(8,128)(2,1)S(1)}, bf16[4,256,128]{2,1,0:T(8,128)(2,1)S(1)}, bf16[256,128]{1,0:T(8...) custom-call(s32[3]{0:T(128)S(1)} %pad_add_fusion.place, bf16[128,4096]{1,0:T(8,128)(2,1)} %refs_0_.3, ...), custom_call_target="tpu_custom_call" | custom-call | flops 1476395008 | bytes 9633804 | tf_op jit(solution)/shard_map/pallas_call | solution.py:33
  75.2 1.0 copy-done.5
  79.4 3.2 %shard_map.89 = (f32[4,256,512]{2,1,0:T(8,128)}, bf16[256,512]{1,0:T(8,128)(2,1)S(1)}, bf16[256,512]{1,0:T(8,128)(2,1)S(1)}, bf16[256,512]{1,0:T(8,128)(2,1)S(1)}, bf16[256,512]{1,0:T(8,128)(2,1)S(1)}) custom-call(s32[3]{0:T(128)S(1)} %pad_add_fusion.place, bf16[128,4096]{1,0:T(8,128)(2,1)S(1)} %copy-done.1, ...), custom_call_target="tpu_custom_call" | custom-call | flops 1073741824 | bytes 7602188 | tf_op jit(solution)/shard_map/pallas_call | solution.py:33
  83.6 1.3 collective-permute-start.20
  84.9 1.3 %collective-permute-start.19 = (bf16[256,128]{1,0:T(8,128)(2,1)S(1)}, bf16[256,128]{1,0:T(8,128)(2,1)S(1)}, u32[]{:S(2)}, u32[]{:S(2)}) collective-permute-start(bf16[256,128]{1,0:T(8,128)(2,1)S(1)} %get-tuple-element.46), channel_id=1, source_target_pairs={{16,0},{17,1},{18,2},{19,3},{20,4},{21,5},{22,6},{23,7},{24,8},{25... | collective-permute-start | bytes 196616 | tf_op jit(solution)/shard_map/ppermute | solution.py:246
  86.2 1.3 %collective-permute-start.18 = (bf16[256,128]{1,0:T(8,128)(2,1)S(1)}, bf16[256,128]{1,0:T(8,128)(2,1)S(1)}, u32[]{:S(2)}, u32[]{:S(2)}) collective-permute-start(bf16[256,128]{1,0:T(8,128)(2,1)S(1)} %get-tuple-element.46), channel_id=1, source_target_pairs={{8,0},{9,1},{10,2},{11,3},{12,4},{13,5},{14,6},{15,7},{16,8},{17,9... | collective-permute-start | bytes 196616 | tf_op jit(solution)/shard_map/ppermute | solution.py:246
  87.6 1.6 %copy-done.12 = f32[4,256,512]{2,1,0:T(8,128)S(1)} copy-done((f32[4,256,512]{2,1,0:T(8,128)S(1)}, f32[4,256,512]{2,1,0:T(8,128)}, u32[]{:S(2)}) %copy-start.12) | copy-done | bytes 2097176
  89.9 6.3 %collective-permute-start.29 = (bf16[256,512]{1,0:T(8,128)(2,1)S(1)}, bf16[256,512]{1,0:T(8,128)(2,1)S(1)}, u32[]{:S(2)}, u32[]{:S(2)}) collective-permute-start(bf16[256,512]{1,0:T(8,128)(2,1)S(1)} %get-tuple-element.59), channel_id=1, source_target_pairs={{0,24},{1,25},{2,26},{3,27},{4,28},{5,29},{6,30},{7,31},{8,16},{9,... | collective-permute-start | bytes 786440 | tf_op jit(solution)/shard_map/ppermute | solution.py:234
  96.9 1.2 collective-permute-done.21.refs_10_
  98.2 1.2 shard_map.87
  99.4 1.3 %collective-permute-start.22 = (bf16[128,512]{1,0:T(8,128)(2,1)S(1)}, bf16[128,512]{1,0:T(8,128)(2,1)S(1)}, u32[]{:S(2)}, u32[]{:S(2)}) collective-permute-start(bf16[128,512]{1,0:T(8,128)(2,1)S(1)} %get-tuple-element.48), channel_id=1, source_target_pairs={{0,2},{1,3},{2,0},{3,1},{4,6},{5,7},{6,4},{7,5},{8,10},{9,11},{10,... | collective-permute-start | bytes 393224 | tf_op jit(solution)/shard_map/ppermute | solution.py:234
  101.5 1.9 %collective-permute-done.29.refs_0_ = bf16[256,512]{1,0:T(8,128)(2,1)S(1)} collective-permute-done((bf16[256,512]{1,0:T(8,128)(2,1)S(1)}, bf16[256,512]{1,0:T(8,128)(2,1)S(1)}, u32[]{:S(2)}, u32[]{:S(2)}) %collective-permute-start.29) | collective-permute-done | bytes 262176 | tf_op jit(solution)/shard_map/ppermute | solution.py:234
  103.5 1.5 %collective-permute-start.24 = (bf16[128,512]{1,0:T(8,128)(2,1)S(1)}, bf16[128,512]{1,0:T(8,128)(2,1)S(1)}, u32[]{:S(2)}, u32[]{:S(2)}) collective-permute-start(bf16[128,512]{1,0:T(8,128)(2,1)S(1)} %get-tuple-element.50), channel_id=1, source_target_pairs={{0,6},{1,7},{2,4},{3,5},{4,2},{5,3},{6,0},{7,1},{8,14},{9,15},{10,... | collective-permute-start | bytes 393224 | tf_op jit(solution)/shard_map/ppermute | solution.py:234
  105.0 14.0 %collective-permute-done.30.refs_1_ = bf16[256,512]{1,0:T(8,128)(2,1)S(1)} collective-permute-done((bf16[256,512]{1,0:T(8,128)(2,1)S(1)}, bf16[256,512]{1,0:T(8,128)(2,1)S(1)}, u32[]{:S(2)}, u32[]{:S(2)}) %collective-permute-start.30) | collective-permute-done | bytes 262176 | tf_op jit(solution)/shard_map/ppermute | solution.py:234
  119.7 1.3 %collective-permute-start.32 = (bf16[256,128]{1,0:T(8,128)(2,1)S(1)}, bf16[256,128]{1,0:T(8,128)(2,1)S(1)}, u32[]{:S(2)}, u32[]{:S(2)}) collective-permute-start(bf16[256,128]{1,0:T(8,128)(2,1)S(1)} %get-tuple-element.63), channel_id=1, source_target_pairs={{0,2},{1,3},{2,0},{3,1},{4,6},{5,7},{6,4},{7,5},{8,10},{9,11},{10,... | collective-permute-start | bytes 196616 | tf_op jit(solution)/shard_map/ppermute | solution.py:234
  121.9 1.4 %collective-permute-start.34 = (bf16[256,128]{1,0:T(8,128)(2,1)S(1)}, bf16[256,128]{1,0:T(8,128)(2,1)S(1)}, u32[]{:S(2)}, u32[]{:S(2)}) collective-permute-start(bf16[256,128]{1,0:T(8,128)(2,1)S(1)} %get-tuple-element.65), channel_id=1, source_target_pairs={{0,6},{1,7},{2,4},{3,5},{4,2},{5,3},{6,0},{7,1},{8,14},{9,15},{10,... | collective-permute-start | bytes 196616 | tf_op jit(solution)/shard_map/ppermute | solution.py:234
  123.3 1.4 %shard_map.88 = (bf16[128,512]{1,0:T(8,128)(2,1)}, bf16[128,1024]{1,0:T(8,128)(2,1)}, bf16[128,512]{1,0:T(8,128)(2,1)}) custom-call(s32[3]{0:T(128)S(1)} %pad_add_fusion.place, bf16[128,512]{1,0:T(8,128)(2,1)S(1)} %get-tuple-element.47.refs_0_, bf16[128,512]{1,0:T(8,128)(2,1)S(1)} %collective-permute-done.22.refs_1_, ...), custom_call_target="tpu_custom_call" | custom-call | bytes 1048588 | tf_op jit(solution)/shard_map/pallas_call | solution.py:33
  124.7 1.3 %collective-permute-done.33.refs_2_ = bf16[256,128]{1,0:T(8,128)(2,1)S(1)} collective-permute-done((bf16[256,128]{1,0:T(8,128)(2,1)S(1)}, bf16[256,128]{1,0:T(8,128)(2,1)S(1)}, u32[]{:S(2)}, u32[]{:S(2)}) %collective-permute-start.33) | collective-permute-done | bytes 65568 | tf_op jit(solution)/shard_map/ppermute | solution.py:234
  127.0 1.5 %shard_map.92 = f32[128,1024]{1,0:T(8,128)} custom-call(s32[3]{0:T(128)S(1)} %pad_add_fusion.place, f32[256,128]{1,0:T(8,128)S(1)} %get-tuple-element.62.refs_0_, bf16[256,128]{1,0:T(8,128)(2,1)S(1)} %collective-permute-done.32.refs_1_, bf16[256,128]{1,0:T(8,128)(2,1)S(1)} %collective-permute-done.33.refs_2_, ...), custom_call_target="tpu_custom_call" | custom-call | bytes 851980 | tf_op jit(solution)/shard_map/pallas_call | solution.py:33
  (84 shorter events, 21.5 us)
Async XLA Ops:
  5.2 8.7 %collective-permute-start = (bf16[384,256]{1,0:T(8,128)(2,1)S(1)}, bf16[384,256]{1,0:T(8,128)(2,1)S(1)}, u32[]{:S(2)}, u32[]{:S(2)}) collective-permute-start(bf16[384,256]{1,0:T(8,128)(2,1)S(1)} %get-tuple-element.37), channel_id=1, source_target_pairs={{0,2},{1,3},{2,0},{3,1},{4,6},{5,7},{6,4},{7,5},{8,10},{9,11},{10,... | collective-permute-start | bytes 589832 | tf_op jit(solution)/shard_map/ppermute | solution.py:234
  8.2 10.6 %collective-permute-start.1 = (bf16[384,256]{1,0:T(8,128)(2,1)S(1)}, bf16[384,256]{1,0:T(8,128)(2,1)S(1)}, u32[]{:S(2)}, u32[]{:S(2)}) collective-permute-start(bf16[384,256]{1,0:T(8,128)(2,1)S(1)} %get-tuple-element.38), channel_id=1, source_target_pairs={{0,4},{1,5},{2,6},{3,7},{4,0},{5,1},{6,2},{7,3},{8,12},{9,13},{10,... | collective-permute-start | bytes 589832 | tf_op jit(solution)/shard_map/ppermute | solution.py:234
  9.7 9.1 %collective-permute-start.2 = (bf16[384,256]{1,0:T(8,128)(2,1)S(1)}, bf16[384,256]{1,0:T(8,128)(2,1)S(1)}, u32[]{:S(2)}, u32[]{:S(2)}) collective-permute-start(bf16[384,256]{1,0:T(8,128)(2,1)S(1)} %get-tuple-element.39), channel_id=1, source_target_pairs={{0,6},{1,7},{2,4},{3,5},{4,2},{5,3},{6,0},{7,1},{8,14},{9,15},{10,... | collective-permute-start | bytes 589832 | tf_op jit(solution)/shard_map/ppermute | solution.py:234
  19.6 6.1 %collective-permute-start.12 = (bf16[640,256]{1,0:T(8,128)(2,1)S(1)}, bf16[640,256]{1,0:T(8,128)(2,1)S(1)}, u32[]{:S(2)}, u32[]{:S(2)}) collective-permute-start(bf16[640,256]{1,0:T(8,128)(2,1)S(1)} %get-tuple-element.40.refs_11_), channel_id=1, source_target_pairs={{0,1},{1,0},{2,3},{3,2},{4,5},{5,4},{6,7},{7,6},{8,9},{9,8},{10,11... | collective-permute-start | bytes 983048 | tf_op jit(solution)/shard_map/ppermute | solution.py:234
  19.7 12.5 %collective-permute-start.11 = (bf16[640,256]{1,0:T(8,128)(2,1)S(1)}, bf16[640,256]{1,0:T(8,128)(2,1)S(1)}, u32[]{:S(2)}, u32[]{:S(2)}) collective-permute-start(bf16[640,256]{1,0:T(8,128)(2,1)S(1)} %get-tuple-element.40.refs_11_), channel_id=1, source_target_pairs={{0,24},{1,25},{2,26},{3,27},{4,28},{5,29},{6,30},{7,31},{8,16},{9,... | collective-permute-start | bytes 983048 | tf_op jit(solution)/shard_map/ppermute | solution.py:234
  23.3 2.4 %collective-permute-start.16 = (bf16[4,256,128]{2,1,0:T(8,128)(2,1)S(1)}, bf16[4,256,128]{2,1,0:T(8,128)(2,1)S(1)}, u32[]{:S(2)}, u32[]{:S(2)}) collective-permute-start(bf16[4,256,128]{2,1,0:T(8,128)(2,1)S(1)} %get-tuple-element.41.refs_19_), channel_id=1, source_target_pairs={{0,1},{1,0},{2,3},{3,2},{4,5},{5,4},{6,7},{7,6},{8,9},{9,8},{10,11... | collective-permute-start | bytes 786440 | tf_op jit(solution)/shard_map/ppermute | solution.py:234
  23.6 28.3 %collective-permute-start.6 = (bf16[64,4096]{1,0:T(8,128)(2,1)S(1)}, bf16[64,4096]{1,0:T(8,128)(2,1)S(1)}, u32[]{:S(2)}, u32[]{:S(2)}) collective-permute-start(bf16[64,4096]{1,0:T(8,128)(2,1)S(1)} %get-tuple-element.68), channel_id=1, source_target_pairs={{0,4},{1,5},{2,6},{3,7},{4,0},{5,1},{6,2},{7,3},{8,12},{9,13},{10,... | collective-permute-start | bytes 1572872 | tf_op jit(solution)/shard_map/ppermute | solution.py:234
  25.2 28.0 %collective-permute-start.3 = (bf16[64,4096]{1,0:T(8,128)(2,1)S(1)}, bf16[64,4096]{1,0:T(8,128)(2,1)S(1)}, u32[]{:S(2)}, u32[]{:S(2)}) collective-permute-start(bf16[64,4096]{1,0:T(8,128)(2,1)S(1)} %get-tuple-element.69), channel_id=1, source_target_pairs={{0,2},{1,3},{2,0},{3,1},{4,6},{5,7},{6,4},{7,5},{8,10},{9,11},{10,... | collective-permute-start | bytes 1572872 | tf_op jit(solution)/shard_map/ppermute | solution.py:234
  25.7 26.2 %collective-permute-start.10 = (bf16[640,256]{1,0:T(8,128)(2,1)S(1)}, bf16[640,256]{1,0:T(8,128)(2,1)S(1)}, u32[]{:S(2)}, u32[]{:S(2)}) collective-permute-start(bf16[640,256]{1,0:T(8,128)(2,1)S(1)} %get-tuple-element.40.refs_11_), channel_id=1, source_target_pairs={{0,16},{1,17},{2,18},{3,19},{4,20},{5,21},{6,22},{7,23},{8,24},{9,... | collective-permute-start | bytes 983048 | tf_op jit(solution)/shard_map/ppermute | solution.py:234
  25.7 35.4 %collective-permute-start.4 = (bf16[64,4096]{1,0:T(8,128)(2,1)S(1)}, bf16[64,4096]{1,0:T(8,128)(2,1)S(1)}, u32[]{:S(2)}, u32[]{:S(2)}) collective-permute-start(bf16[64,4096]{1,0:T(8,128)(2,1)S(1)} %get-tuple-element.68), channel_id=1, source_target_pairs={{0,2},{1,3},{2,0},{3,1},{4,6},{5,7},{6,4},{7,5},{8,10},{9,11},{10,... | collective-permute-start | bytes 1572872 | tf_op jit(solution)/shard_map/ppermute | solution.py:234
  32.1 29.5 %collective-permute-start.5 = (bf16[64,4096]{1,0:T(8,128)(2,1)S(1)}, bf16[64,4096]{1,0:T(8,128)(2,1)S(1)}, u32[]{:S(2)}, u32[]{:S(2)}) collective-permute-start(bf16[64,4096]{1,0:T(8,128)(2,1)S(1)} %get-tuple-element.69), channel_id=1, source_target_pairs={{0,4},{1,5},{2,6},{3,7},{4,0},{5,1},{6,2},{7,3},{8,12},{9,13},{10,... | collective-permute-start | bytes 1572872 | tf_op jit(solution)/shard_map/ppermute | solution.py:234
  51.9 9.3 %collective-permute-start.9 = (bf16[640,256]{1,0:T(8,128)(2,1)S(1)}, bf16[640,256]{1,0:T(8,128)(2,1)S(1)}, u32[]{:S(2)}, u32[]{:S(2)}) collective-permute-start(bf16[640,256]{1,0:T(8,128)(2,1)S(1)} %get-tuple-element.40.refs_11_), channel_id=1, source_target_pairs={{0,8},{1,9},{2,10},{3,11},{4,12},{5,13},{6,14},{7,15},{8,0},{9,1},... | collective-permute-start | bytes 983048 | tf_op jit(solution)/shard_map/ppermute | solution.py:234
  51.9 13.6 %collective-permute-start.8 = (bf16[64,4096]{1,0:T(8,128)(2,1)S(1)}, bf16[64,4096]{1,0:T(8,128)(2,1)S(1)}, u32[]{:S(2)}, u32[]{:S(2)}) collective-permute-start(bf16[64,4096]{1,0:T(8,128)(2,1)S(1)} %collective-permute-done.6.refs_4_), channel_id=1, source_target_pairs={{0,2},{1,3},{2,0},{3,1},{4,6},{5,7},{6,4},{7,5},{8,10},{9,11},{10,... | collective-permute-start | bytes 1572872 | tf_op jit(solution)/shard_map/ppermute | solution.py:234
  53.2 13.2 %collective-permute-start.7 = (bf16[64,4096]{1,0:T(8,128)(2,1)S(1)}, bf16[64,4096]{1,0:T(8,128)(2,1)S(1)}, u32[]{:S(2)}, u32[]{:S(2)}) collective-permute-start(bf16[64,4096]{1,0:T(8,128)(2,1)S(1)} %collective-permute-done.3.refs_1_), channel_id=1, source_target_pairs={{0,4},{1,5},{2,6},{3,7},{4,0},{5,1},{6,2},{7,3},{8,12},{9,13},{10,... | collective-permute-start | bytes 1572872 | tf_op jit(solution)/shard_map/ppermute | solution.py:234
  61.2 2.1 %collective-permute-start.14 = (bf16[640,256]{1,0:T(8,128)(2,1)S(1)}, bf16[640,256]{1,0:T(8,128)(2,1)S(1)}, u32[]{:S(2)}, u32[]{:S(2)}) collective-permute-start(bf16[640,256]{1,0:T(8,128)(2,1)S(1)} %collective-permute-done.10.refs_13_), channel_id=1, source_target_pairs={{0,1},{1,0},{2,3},{3,2},{4,5},{5,4},{6,7},{7,6},{8,9},{9,8},{10,11... | collective-permute-start | bytes 983048 | tf_op jit(solution)/shard_map/ppermute | solution.py:234
  82.6 2.3 %collective-permute-start.25 = (bf16[256,512]{1,0:T(8,128)(2,1)S(1)}, bf16[256,512]{1,0:T(8,128)(2,1)S(1)}, u32[]{:S(2)}, u32[]{:S(2)}) collective-permute-start(bf16[256,512]{1,0:T(8,128)(2,1)S(1)} %get-tuple-element.54), channel_id=1, source_target_pairs={{0,1},{1,0},{2,3},{3,2},{4,5},{5,4},{6,7},{7,6},{8,9},{9,8},{10,11... | collective-permute-start | bytes 786440 | tf_op jit(solution)/shard_map/ppermute | solution.py:234
  82.6 3.6 %collective-permute-start.26 = (bf16[256,512]{1,0:T(8,128)(2,1)S(1)}, bf16[256,512]{1,0:T(8,128)(2,1)S(1)}, u32[]{:S(2)}, u32[]{:S(2)}) collective-permute-start(bf16[256,512]{1,0:T(8,128)(2,1)S(1)} %get-tuple-element.55), channel_id=1, source_target_pairs={{0,1},{1,0},{2,3},{3,2},{4,5},{5,4},{6,7},{7,6},{8,9},{9,8},{10,11... | collective-permute-start | bytes 786440 | tf_op jit(solution)/shard_map/ppermute | solution.py:234
  83.1 4.4 %collective-permute-start.27 = (bf16[256,512]{1,0:T(8,128)(2,1)S(1)}, bf16[256,512]{1,0:T(8,128)(2,1)S(1)}, u32[]{:S(2)}, u32[]{:S(2)}) collective-permute-start(bf16[256,512]{1,0:T(8,128)(2,1)S(1)} %get-tuple-element.56), channel_id=1, source_target_pairs={{0,1},{1,0},{2,3},{3,2},{4,5},{5,4},{6,7},{7,6},{8,9},{9,8},{10,11... | collective-permute-start | bytes 786440 | tf_op jit(solution)/shard_map/ppermute | solution.py:234
  83.1 4.5 %collective-permute-start.28 = (bf16[256,512]{1,0:T(8,128)(2,1)S(1)}, bf16[256,512]{1,0:T(8,128)(2,1)S(1)}, u32[]{:S(2)}, u32[]{:S(2)}) collective-permute-start(bf16[256,512]{1,0:T(8,128)(2,1)S(1)} %get-tuple-element.57), channel_id=1, source_target_pairs={{0,1},{1,0},{2,3},{3,2},{4,5},{5,4},{6,7},{7,6},{8,9},{9,8},{10,11... | collective-permute-start | bytes 786440 | tf_op jit(solution)/shard_map/ppermute | solution.py:234
  83.6 12.6 %collective-permute-start.20 = (bf16[256,128]{1,0:T(8,128)(2,1)S(1)}, bf16[256,128]{1,0:T(8,128)(2,1)S(1)}, u32[]{:S(2)}, u32[]{:S(2)}) collective-permute-start(bf16[256,128]{1,0:T(8,128)(2,1)S(1)} %get-tuple-element.46), channel_id=1, source_target_pairs={{24,0},{25,1},{26,2},{27,3},{28,4},{29,5},{30,6},{31,7}} | collective-permute-start | bytes 196616 | tf_op jit(solution)/shard_map/ppermute | solution.py:246
  84.9 11.3 %collective-permute-start.19 = (bf16[256,128]{1,0:T(8,128)(2,1)S(1)}, bf16[256,128]{1,0:T(8,128)(2,1)S(1)}, u32[]{:S(2)}, u32[]{:S(2)}) collective-permute-start(bf16[256,128]{1,0:T(8,128)(2,1)S(1)} %get-tuple-element.46), channel_id=1, source_target_pairs={{16,0},{17,1},{18,2},{19,3},{20,4},{21,5},{22,6},{23,7},{24,8},{25... | collective-permute-start | bytes 196616 | tf_op jit(solution)/shard_map/ppermute | solution.py:246
  86.2 10.6 %collective-permute-start.18 = (bf16[256,128]{1,0:T(8,128)(2,1)S(1)}, bf16[256,128]{1,0:T(8,128)(2,1)S(1)}, u32[]{:S(2)}, u32[]{:S(2)}) collective-permute-start(bf16[256,128]{1,0:T(8,128)(2,1)S(1)} %get-tuple-element.46), channel_id=1, source_target_pairs={{8,0},{9,1},{10,2},{11,3},{12,4},{13,5},{14,6},{15,7},{16,8},{17,9... | collective-permute-start | bytes 196616 | tf_op jit(solution)/shard_map/ppermute | solution.py:246
  87.5 10.7 %collective-permute-start.17 = (bf16[4,256,128]{2,1,0:T(8,128)(2,1)S(1)}, bf16[4,256,128]{2,1,0:T(8,128)(2,1)S(1)}, u32[]{:S(2)}, u32[]{:S(2)}) collective-permute-start(bf16[4,256,128]{2,1,0:T(8,128)(2,1)S(1)} %get-tuple-element.45.refs_7_), channel_id=1, source_target_pairs={{0,1},{1,0},{2,3},{3,2},{4,5},{5,4},{6,7},{7,6},{8,9},{9,8},{10,11... | collective-permute-start | bytes 786440 | tf_op jit(solution)/shard_map/ppermute | solution.py:234
  89.9 13.6 %collective-permute-start.29 = (bf16[256,512]{1,0:T(8,128)(2,1)S(1)}, bf16[256,512]{1,0:T(8,128)(2,1)S(1)}, u32[]{:S(2)}, u32[]{:S(2)}) collective-permute-start(bf16[256,512]{1,0:T(8,128)(2,1)S(1)} %get-tuple-element.59), channel_id=1, source_target_pairs={{0,24},{1,25},{2,26},{3,27},{4,28},{5,29},{6,30},{7,31},{8,16},{9,... | collective-permute-start | bytes 786440 | tf_op jit(solution)/shard_map/ppermute | solution.py:234
  96.2 22.8 %collective-permute-start.30 = (bf16[256,512]{1,0:T(8,128)(2,1)S(1)}, bf16[256,512]{1,0:T(8,128)(2,1)S(1)}, u32[]{:S(2)}, u32[]{:S(2)}) collective-permute-start(bf16[256,512]{1,0:T(8,128)(2,1)S(1)} %get-tuple-element.60), channel_id=1, source_target_pairs={{0,16},{1,17},{2,18},{3,19},{4,20},{5,21},{6,22},{7,23},{8,24},{9,... | collective-permute-start | bytes 786440 | tf_op jit(solution)/shard_map/ppermute | solution.py:234
  96.2 22.8 %collective-permute-start.31 = (bf16[256,512]{1,0:T(8,128)(2,1)S(1)}, bf16[256,512]{1,0:T(8,128)(2,1)S(1)}, u32[]{:S(2)}, u32[]{:S(2)}) collective-permute-start(bf16[256,512]{1,0:T(8,128)(2,1)S(1)} %get-tuple-element.61), channel_id=1, source_target_pairs={{0,8},{1,9},{2,10},{3,11},{4,12},{5,13},{6,14},{7,15},{8,0},{9,1},... | collective-permute-start | bytes 786440 | tf_op jit(solution)/shard_map/ppermute | solution.py:234
  99.4 22.4 %collective-permute-start.22 = (bf16[128,512]{1,0:T(8,128)(2,1)S(1)}, bf16[128,512]{1,0:T(8,128)(2,1)S(1)}, u32[]{:S(2)}, u32[]{:S(2)}) collective-permute-start(bf16[128,512]{1,0:T(8,128)(2,1)S(1)} %get-tuple-element.48), channel_id=1, source_target_pairs={{0,2},{1,3},{2,0},{3,1},{4,6},{5,7},{6,4},{7,5},{8,10},{9,11},{10,... | collective-permute-start | bytes 393224 | tf_op jit(solution)/shard_map/ppermute | solution.py:234
  100.7 22.6 %collective-permute-start.23 = (bf16[128,512]{1,0:T(8,128)(2,1)S(1)}, bf16[128,512]{1,0:T(8,128)(2,1)S(1)}, u32[]{:S(2)}, u32[]{:S(2)}) collective-permute-start(bf16[128,512]{1,0:T(8,128)(2,1)S(1)} %get-tuple-element.49), channel_id=1, source_target_pairs={{0,4},{1,5},{2,6},{3,7},{4,0},{5,1},{6,2},{7,3},{8,12},{9,13},{10,... | collective-permute-start | bytes 393224 | tf_op jit(solution)/shard_map/ppermute | solution.py:234
  103.5 19.8 %collective-permute-start.24 = (bf16[128,512]{1,0:T(8,128)(2,1)S(1)}, bf16[128,512]{1,0:T(8,128)(2,1)S(1)}, u32[]{:S(2)}, u32[]{:S(2)}) collective-permute-start(bf16[128,512]{1,0:T(8,128)(2,1)S(1)} %get-tuple-element.50), channel_id=1, source_target_pairs={{0,6},{1,7},{2,4},{3,5},{4,2},{5,3},{6,0},{7,1},{8,14},{9,15},{10,... | collective-permute-start | bytes 393224 | tf_op jit(solution)/shard_map/ppermute | solution.py:234
  119.7 5.0 %collective-permute-start.32 = (bf16[256,128]{1,0:T(8,128)(2,1)S(1)}, bf16[256,128]{1,0:T(8,128)(2,1)S(1)}, u32[]{:S(2)}, u32[]{:S(2)}) collective-permute-start(bf16[256,128]{1,0:T(8,128)(2,1)S(1)} %get-tuple-element.63), channel_id=1, source_target_pairs={{0,2},{1,3},{2,0},{3,1},{4,6},{5,7},{6,4},{7,5},{8,10},{9,11},{10,... | collective-permute-start | bytes 196616 | tf_op jit(solution)/shard_map/ppermute | solution.py:234
  121.0 5.0 %collective-permute-start.33 = (bf16[256,128]{1,0:T(8,128)(2,1)S(1)}, bf16[256,128]{1,0:T(8,128)(2,1)S(1)}, u32[]{:S(2)}, u32[]{:S(2)}) collective-permute-start(bf16[256,128]{1,0:T(8,128)(2,1)S(1)} %get-tuple-element.64), channel_id=1, source_target_pairs={{0,4},{1,5},{2,6},{3,7},{4,0},{5,1},{6,2},{7,3},{8,12},{9,13},{10,... | collective-permute-start | bytes 196616 | tf_op jit(solution)/shard_map/ppermute | solution.py:234
  121.9 5.2 %collective-permute-start.34 = (bf16[256,128]{1,0:T(8,128)(2,1)S(1)}, bf16[256,128]{1,0:T(8,128)(2,1)S(1)}, u32[]{:S(2)}, u32[]{:S(2)}) collective-permute-start(bf16[256,128]{1,0:T(8,128)(2,1)S(1)} %get-tuple-element.65), channel_id=1, source_target_pairs={{0,6},{1,7},{2,4},{3,5},{4,2},{5,3},{6,0},{7,1},{8,14},{9,15},{10,... | collective-permute-start | bytes 196616 | tf_op jit(solution)/shard_map/ppermute | solution.py:234
  (20 other events, 113.7 us)

commit v2 on v1

v2 whole, which is shorter than its diff:
```python
import functools

import jax
import jax.numpy as jnp
from jax import lax
from jax.experimental import pallas as pl
from jax.experimental.pallas import tpu as pltpu
from jax.sharding import PartitionSpec as P

HEAD_DIM = 128
FEAT = 256
HEADS_GROUP = 4
CORES = 2
EPSILON = 1e-06

F32 = jnp.float32
BF16 = jnp.bfloat16
HALF = FEAT // 2
URGENT = 1 << 35


def dot(a, b, dims=((1,), (0,))):
    return lax.dot_general(a, b, (dims, ((), ())), preferred_element_type=F32)


def split(x):
    high = x.astype(BF16)
    return high, (x - high.astype(F32)).astype(BF16)


def seat(place):
    me = place[0]
    low, high = CORES.bit_length() - 1, (CORES * HEADS_GROUP).bit_length() - 1
    return me >> low & HEADS_GROUP - 1, me >> high, me & CORES - 1


def call(kernel, outs, args, flops=0, scratch=(), mib=16, space=pltpu.VMEM, urgent=False):
    shapes = [jax.ShapeDtypeStruct(shape, dtype) for shape, dtype in outs]
    moved = sum(a.size * a.dtype.itemsize for a in args) + sum(s.size * s.dtype.itemsize for s in shapes)
    return pl.pallas_call(
        kernel,
        out_shape=shapes,
        in_specs=[pl.BlockSpec(memory_space=pltpu.SMEM)]
        + [pl.BlockSpec(memory_space=space)] * (len(args) - 1),
        out_specs=[pl.BlockSpec(memory_space=pltpu.VMEM)] * len(shapes),
        scratch_shapes=list(scratch),
        compiler_params=pltpu.CompilerParams(vmem_limit_bytes=mib << 20),
        cost_estimate=pl.CostEstimate(flops=URGENT if urgent else flops, bytes_accessed=moved, transcendentals=0),
    )(*args)


def lanes(index, width):
    return pl.ds(pl.multiple_of(index * width, width), width)


def pack_kernel(place, w, key, val, cot, *refs):
    outs, sems = refs[:4], refs[4]
    rows, depth = key.shape[0], w.shape[0]
    q, _, _ = seat(place)
    copies = []
    for k in (3, 1, 2, 0):
        head, out = q ^ k, outs[k]
        low, high = pl.ds(depth, rows), pl.ds(depth + rows, rows)
        moves = (
            (w.at[:, lanes(head, FEAT)], out.at[pl.ds(0, depth), :]),
            (key.at[:, lanes(head, FEAT)], out.at[low, :]),
            (val.at[:, lanes(head, HEAD_DIM)], out.at[high, pl.ds(0, HEAD_DIM)]),
            (cot.at[:, lanes(head, HEAD_DIM)], out.at[high, pl.ds(HEAD_DIM, HEAD_DIM)]),
        )
        for source, target in moves:
            copies.append(pltpu.make_async_copy(source, target, sems.at[len(copies)]))
            copies[-1].start()
    for copy in copies:
        copy.wait()


def state_kernel(rows, depth, place, p0, p1, p2, p3, pay, states):
    total = jnp.zeros((FEAT, HEAD_DIM), F32)
    for j, p in enumerate((p0, p1, p2, p3)):
        pay[j * depth : (j + 1) * depth, :] = p[:depth, :]
        keys = jnp.maximum(p[depth : depth + rows, :], 0)
        state = dot(keys, p[depth + rows :, :HEAD_DIM], ((0,), (0,)))
        states[j] = state.astype(BF16)
        total = total + state
    total = total.astype(BF16)
    pay[4 * depth :, :HEAD_DIM] = total[:HALF, :]
    pay[4 * depth :, HEAD_DIM:] = total[HALF:, :]


def hidden_columns(h, start, width):
    cols = pl.ds(start, width)
    return jnp.concatenate([ref[:, cols] for ref in h], axis=0)


def before(there, here):
    return (there < here).astype(jnp.int32).astype(F32)


def attend_kernel(rows, depth, outer, place, *refs):
    h, refs = refs[:5], refs[5:]
    p, refs = refs[:4], refs[4:]
    own_pay, refs = refs[:outer], refs[outer:]
    other_pay, refs = refs[:outer], refs[outer:]
    own_states, other_states, att, dq_t, grown, feats_out, d_num_out, scores_out, mixed_out, weights, proj = refs
    q, z, core = seat(place)
    base = jnp.zeros((FEAT, HEAD_DIM), F32)
    for k in range(outer):
        for flip, pay in ((0, own_pay[k]), (1, other_pay[k])):
            for j in range(4):
                at = (((z ^ k) * 4 + (q ^ j)) * CORES + (core ^ flip)) * depth
                weights[pl.ds(pl.multiple_of(at, depth), depth), :] = pay[j * depth : (j + 1) * depth, :]
            if k:
                packed = pay[4 * depth :, :].astype(F32)
                base = base + before(z ^ k, z) * jnp.concatenate(
                    [packed[:, :HEAD_DIM], packed[:, HEAD_DIM:]], axis=0
                )
    width = h[0].shape[1]
    step = min(512, width)
    for at in range(0, width, step):
        part = dot(hidden_columns(h, at, step), weights[at : at + step, :])
        if at:
            proj[...] += part
        else:
            proj[...] = part
    own = [own_states[j].astype(F32) for j in range(4)]
    other = [other_states[j].astype(F32) for j in range(4)]
    causal = lax.broadcasted_iota(jnp.int32, (rows, rows), 0) >= lax.broadcasted_iota(
        jnp.int32, (rows, rows), 1
    )
    for j in range(4):
        here = (q ^ j) * CORES + core
        prior = base
        for i in range(4):
            for flip, group in ((0, own), (1, other)):
                if flip == 0 and i == j:
                    continue
                prior = prior + before((q ^ i) * CORES + (core ^ flip), here) * group[i]
        prior_high, prior_low = split(prior)
        block = slice(j * rows, (j + 1) * rows)
        query = proj[block, :]
        feats = jnp.maximum(query, 0.0).astype(BF16)
        keys = jnp.maximum(p[j][depth : depth + rows, :], 0)
        vals = p[j][depth + rows :, :HEAD_DIM]
        grad = p[j][depth + rows :, HEAD_DIM:].astype(F32)
        scores = jnp.where(causal, dot(feats, keys, ((1,), (1,))), 0.0).astype(BF16)
        numer = dot(scores, vals) + dot(feats, prior_high) + dot(feats, prior_low)
        inv = lax.rsqrt(jnp.mean(numer * numer, axis=-1, keepdims=True) + EPSILON)
        normed = numer * inv
        att[j] = normed.astype(BF16)
        d_num = (inv * (grad - normed * jnp.mean(grad * normed, axis=-1, keepdims=True))).astype(BF16)
        mixed = jnp.where(causal, dot(d_num, vals, ((1,), (1,))), 0.0).astype(BF16)
        d_feat = dot(mixed, keys) + dot(d_num, prior_high, ((1,), (1,))) + dot(d_num, prior_low, ((1,), (1,)))
        d_query = jnp.where(query > 0, d_feat, 0.0)
        dq_t[:, block] = d_query.T.astype(BF16)
        grown[j] = dot(feats, d_num, ((0,), (0,))).astype(BF16)
        feats_out[j] = feats
        d_num_out[j] = d_num
        scores_out[j] = scores
        mixed_out[j] = mixed


def half_kernel(place, own, other, half, total):
    _, _, core = seat(place)
    total[...] = sum(ref[j].astype(F32) for ref in (own, other) for j in range(4))
    half[...] = total[pl.ds(pl.multiple_of(core * HALF, HALF), HALF), :].astype(BF16)


def side_kernel(rows, place, feats, d_num, scores, mixed, val_part, key_part):
    for j in range(4):
        block = slice(j * rows, (j + 1) * rows)
        val_part[block, :] = dot(scores[j], d_num[j], ((0,), (0,)))
        key_part[block, :] = dot(mixed[j], feats[j], ((0,), (0,)))


def grad_kernel(depth, k, place, *refs):
    *h, dq_t, keep, give = refs
    _, z, core = seat(place)
    pair = CORES * depth
    lhs = dq_t[...]
    for i in range(4):
        start = pl.multiple_of(((z ^ k) * 4 + i) * pair, pair)
        out = dot(lhs, hidden_columns(h, start, pair))
        even, odd = out[:, :depth], out[:, depth:]
        first = jnp.broadcast_to(core == 0, even.shape)
        keep[:, i * depth : (i + 1) * depth] = jnp.where(first, even, odd)
        give[:, i * depth : (i + 1) * depth] = jnp.where(first, odd, even).astype(BF16)


def sum_kernel(depth, place, own, *refs):
    arrived, (mine, *outs), blocks = refs[:-5], refs[-5:-1], refs[-1]
    total = own[...]
    for ref in arrived:
        total = total + ref[...].astype(F32)
    q, _, _ = seat(place)
    for i in range(4):
        blocks[q ^ i] = total[:, i * depth : (i + 1) * depth]
    mine[...] = blocks[0]
    for k, out in enumerate(outs):
        out[...] = blocks[k + 1].astype(BF16)


def query_grad_kernel(place, *refs):
    out = refs[-1]
    q, _, _ = seat(place)
    for k, ref in enumerate(refs[:-1]):
        out[:, lanes(q ^ k, FEAT)] = ref[...].astype(F32).T


def finish_kernel(rows, depth, outer, place, *refs):
    p, refs = refs[:4], refs[4:]
    att, val_part, key_part, own_grown, other_grown, own_rest, other_rest, *outs, rest = refs
    q, _, core = seat(place)
    for flip, ref in ((0, own_rest), (1, other_rest)):
        rest[pl.ds(pl.multiple_of((core ^ flip) * HALF, HALF), HALF), :] = ref[...].astype(F32)
    base = rest[...]
    own = [own_grown[j].astype(F32) for j in range(4)]
    other = [other_grown[j].astype(F32) for j in range(4)]
    for j, out in enumerate(outs):
        here = (q ^ j) * CORES + core
        later = base
        for i in range(4):
            for flip, group in ((0, own), (1, other)):
                if flip == 0 and i == j:
                    continue
                later = later + before(here, (q ^ i) * CORES + (core ^ flip)) * group[i]
        high, low = split(later)
        block = slice(j * rows, (j + 1) * rows)
        raw = p[j][depth : depth + rows, :]
        keys = jnp.maximum(raw, 0)
        vals = p[j][depth + rows :, :HEAD_DIM]
        d_val = val_part[block, :] + dot(keys, high) + dot(keys, low)
        d_key = key_part[block, :] + dot(vals, high, ((1,), (1,))) + dot(vals, low, ((1,), (1,)))
        out[:, :HEAD_DIM] = att[j]
        out[:, HEAD_DIM : 2 * HEAD_DIM] = d_val.astype(BF16)
        out[:, 2 * HEAD_DIM :] = jnp.where(raw.astype(F32) > 0, d_key, 0.0).astype(BF16)


def place_kernel(place, *refs):
    att, key_grad, val_grad = refs[-3:]
    q, _, _ = seat(place)
    for k, ref in enumerate(refs[:-3]):
        head = q ^ k
        att[:, lanes(head, HEAD_DIM)] = ref[:, :HEAD_DIM]
        val_grad[:, lanes(head, HEAD_DIM)] = ref[:, HEAD_DIM : 2 * HEAD_DIM]
        key_grad[:, lanes(head, FEAT)] = ref[:, 2 * HEAD_DIM :]


def body(hidden, w_query, key_input, values, cotangent):
    count = lax.axis_size("ctx")
    me = lax.axis_index("ctx")
    inner = CORES * HEADS_GROUP
    outer = count // inner
    rows, depth = key_input.shape[0], w_query.shape[0]
    if lax.axis_size("heads") > 1:
        hidden = lax.all_gather(hidden, "heads", axis=1, tiled=True)
    width = hidden.shape[1]
    place = me.astype(jnp.int32).reshape(1)

    def swap(block, bits):
        return lax.ppermute(block, "ctx", [(i, i ^ bits) for i in range(count)])

    def core_swap(block):
        return swap(block, 1)

    def chip_swap(block, k):
        return swap(block, CORES * k)

    def plane_swap(block, k):
        return swap(block, inner * k)

    def down(block, k):
        return lax.ppermute(block, "ctx", [(i, i - inner * k) for i in range(inner * k, count)])

    packs = call(
        pack_kernel,
        [((depth + 2 * rows, FEAT), BF16)] * 4,
        [place, w_query, key_input, values, cotangent],
        scratch=[pltpu.SemaphoreType.DMA((16,))],
        space=pltpu.HBM,
        mib=62,
    )
    hidden, packs = lax.optimization_barrier((hidden, packs))
    p = [packs[0]] + [chip_swap(packs[k], k) for k in (1, 2, 3)]
    h1, h2 = chip_swap(hidden, 1), chip_swap(hidden, 2)
    pay, states = call(
        functools.partial(state_kernel, rows, depth),
        [((4 * depth + HALF, FEAT), BF16), ((4, FEAT, HEAD_DIM), BF16)],
        [place, *p],
        urgent=True,
    )
    pays = [pay] + [None] * (outer - 1)
    for k in reversed(range(1, outer)):
        pays[k] = plane_swap(pay, k)
    h1, h2, pays[-1], late_pay, late_states = lax.optimization_barrier((h1, h2, pays[-1], pay, states))
    h3 = [chip_swap(h1[: rows // 2], 2), chip_swap(h2[rows // 2 :], 1)]
    h = [hidden, h1, h2, *h3]
    other_pays = [core_swap(late_pay)] + [core_swap(pays[k]) for k in range(1, outer)]
    other_states = core_swap(late_states)
    positions = 4 * rows
    att, dq_t, grown, *kept = call(
        functools.partial(attend_kernel, rows, depth, outer),
        [
            ((4, rows, HEAD_DIM), BF16),
            ((FEAT, positions), BF16),
            ((4, FEAT, HEAD_DIM), BF16),
            ((4, rows, FEAT), BF16),
            ((4, rows, HEAD_DIM), BF16),
            ((4, rows, rows), BF16),
            ((4, rows, rows), BF16),
        ],
        [place, *h, *p, *pays, *other_pays, states, other_states],
        flops=2 * positions * width * FEAT + 24 * positions * FEAT * HEAD_DIM,
        scratch=[pltpu.VMEM((width, FEAT), BF16), pltpu.VMEM((positions, FEAT), F32)],
    )
    other_grown = core_swap(grown)
    (half,) = call(
        half_kernel,
        [((HALF, HEAD_DIM), BF16)],
        [place, grown, other_grown],
        scratch=[pltpu.VMEM((FEAT, HEAD_DIM), F32)],
    )
    later = [down(half, k) for k in range(1, outer)]
    sums = [None] * outer
    for k in reversed(range(outer)):
        keep, give = call(
            functools.partial(grad_kernel, depth, k),
            [((FEAT, 4 * depth), F32), ((FEAT, 4 * depth), BF16)],
            [place, *h, dq_t],
            flops=2 * positions * width * FEAT // outer,
        )
        sums[k] = keep + core_swap(give).astype(F32)
    own = sums[0]
    arrived = [plane_swap(sums[k].astype(BF16), k) for k in reversed(range(1, outer))]
    val_part, key_part = call(
        functools.partial(side_kernel, rows),
        [((positions, HEAD_DIM), F32), ((positions, FEAT), F32)],
        [place, *kept],
        flops=6 * positions * FEAT * HEAD_DIM,
    )
    rest = sum((x.astype(F32) for x in later), jnp.zeros((HALF, HEAD_DIM), F32)).astype(BF16)
    other_rest = core_swap(rest)
    outs = call(
        functools.partial(finish_kernel, rows, depth, outer),
        [((rows, 2 * HEAD_DIM + FEAT), BF16)] * 4,
        [place, *p, att, val_part, key_part, grown, other_grown, rest, other_rest],
        flops=16 * positions * FEAT * HEAD_DIM,
        scratch=[pltpu.VMEM((FEAT, HEAD_DIM), F32)],
    )
    placed = [outs[0]] + [chip_swap(outs[k], k) for k in (1, 2, 3)]
    attended, key_grad, value_grad = call(
        place_kernel,
        [
            ((rows, HEADS_GROUP * HEAD_DIM), BF16),
            ((rows, HEADS_GROUP * FEAT), BF16),
            ((rows, HEADS_GROUP * HEAD_DIM), BF16),
        ],
        [place, *placed],
    )
    blocks = call(
        functools.partial(sum_kernel, depth),
        [((FEAT, depth), F32)] + [((FEAT, depth), BF16)] * 3,
        [place, own, *arrived],
        scratch=[pltpu.VMEM((4, FEAT, depth), F32)],
        urgent=True,
    )
    columns = [blocks[0]] + [chip_swap(blocks[k], k) for k in (1, 2, 3)]
    (query_grad,) = call(
        query_grad_kernel, [((depth, HEADS_GROUP * FEAT), F32)], [place, *columns]
    )
    return (attended, query_grad, key_grad, value_grad)


def solution(mesh):
    return jax.shard_map(
        body,
        mesh=mesh,
        in_specs=(P("ctx", "heads"),) * 5,
        out_specs=(P("ctx", "heads"),) * 4,
        check_vma=False,
    )
```

time: 129 us -> 109 us (0.84)
  the two profiles are of different devices: /device:TPU:0 before, /device:TPU:14 now
where the time goes in v2:
time: 109 us
  waiting for transfers between devices  64 us (59%)
  starting transfers between devices  30.7 us (28%)
  Pallas kernels  12.1 us (11%)
    ppermute x30, waiting for transfers between devices, swap(): return lax.ppermute(block, 'ctx', [(i, i ^ bits) for i in range(count)])  64 us
    ppermute x30, starting transfers between devices, swap(): return lax.ppermute(block, 'ctx', [(i, i ^ bits) for i in range(count)])  26.8 us
    pallas_call x13, Pallas kernels, call(): pl.pallas_call(kernel, out_shape=shapes, in_specs=[pl.BlockSpec(memory_sp...  12.1 us
    ppermute x3, starting transfers between devices, down(): lax.ppermute(block, 'ctx', [(i, i - inner * k) for i in range(inner * k,...  3.88 us
  transfers between devices with their start and end apart: 33, of which 14 were waited for; matrix products, arithmetic and copies ran while one was open for 0% of the time, Pallas kernels for 4%

profile of v2, /device:TPU:14, one launch (start us, length us, event | category | flops | bytes accessed | tf_op | source)
XLA Modules:
  0.0 109.0 jit_solution(15315989249726136032)
XLA Ops:
  0.6 2.2 %shard_map.84 = (bf16[384,256]{1,0:T(8,128)(2,1)}, bf16[384,256]{1,0:T(8,128)(2,1)}, bf16[384,256]{1,0:T(8,128)(2,1)}, bf16[384,256]{1,0:T(8,128)(2,1)}) custom-call(s32[1]{0:T(128)} %bitcast.place, bf16[128,1024]{1,0:T(8,128)(2,1)} %w.1, bf16[128,1024]{1,0:T(8,128)(2,1)} %key.1, bf16[128,512]{1,0:T(8,128)(2,1)} %val.1, bf16[128,512]{1,0:T(8,128)(2,1)} %cot.1), custom_call_target="tpu_custom_call" | custom-call | bytes 1572868 | tf_op jit(solution)/shard_map/pallas_call | solution.py:40
  3.9 2.4 %collective-permute-start.2 = (bf16[384,256]{1,0:T(8,128)(2,1)}, bf16[384,256]{1,0:T(8,128)(2,1)S(1)}, u32[]{:S(2)}, u32[]{:S(2)}) collective-permute-start(bf16[384,256]{1,0:T(8,128)(2,1)} %get-tuple-element.55), channel_id=1, source_target_pairs={{0,6},{1,7},{2,4},{3,5},{4,2},{5,3},{6,0},{7,1},{8,14},{9,15},{10,... | collective-permute-start | bytes 589832 | tf_op jit(solution)/shard_map/ppermute | solution.py:260
  7.4 3.5 %collective-permute-done.p1.refs_6_.refs_1_ = bf16[384,256]{1,0:T(8,128)(2,1)S(1)} collective-permute-done((bf16[384,256]{1,0:T(8,128)(2,1)}, bf16[384,256]{1,0:T(8,128)(2,1)S(1)}, u32[]{:S(2)}, u32[]{:S(2)}) %collective-permute-start) | collective-permute-done | bytes 196640 | tf_op jit(solution)/shard_map/ppermute | solution.py:260
  10.9 4.8 %collective-permute-done.1.p2.refs_7_.refs_2_ = bf16[384,256]{1,0:T(8,128)(2,1)S(1)} collective-permute-done((bf16[384,256]{1,0:T(8,128)(2,1)}, bf16[384,256]{1,0:T(8,128)(2,1)S(1)}, u32[]{:S(2)}, u32[]{:S(2)}) %collective-permute-start.1) | collective-permute-done | bytes 196640 | tf_op jit(solution)/shard_map/ppermute | solution.py:260
  15.7 0.9 copy-done.1
  16.9 2.7 %collective-permute-start.9 = (bf16[640,256]{1,0:T(8,128)(2,1)S(1)}, bf16[640,256]{1,0:T(8,128)(2,1)S(1)}, u32[]{:S(2)}, u32[]{:S(2)}) collective-permute-start(bf16[640,256]{1,0:T(8,128)(2,1)S(1)} %get-tuple-element.62.refs_9_), channel_id=1, source_target_pairs={{0,16},{1,17},{2,18},{3,19},{4,20},{5,21},{6,22},{7,23},{8,24},{9,... | collective-permute-start | bytes 983048 | tf_op jit(solution)/shard_map/ppermute | solution.py:260
  20.4 14.1 %collective-permute-done.9.refs_11_ = bf16[640,256]{1,0:T(8,128)(2,1)S(1)} collective-permute-done((bf16[640,256]{1,0:T(8,128)(2,1)S(1)}, bf16[640,256]{1,0:T(8,128)(2,1)S(1)}, u32[]{:S(2)}, u32[]{:S(2)}) %collective-permute-start.9) | collective-permute-done | bytes 327712 | tf_op jit(solution)/shard_map/ppermute | solution.py:260
  34.5 0.9 collective-permute-done.8.refs_10_
  35.4 9.5 %collective-permute-done.5.refs_12_ = bf16[640,256]{1,0:T(8,128)(2,1)S(1)} collective-permute-done((bf16[640,256]{1,0:T(8,128)(2,1)S(1)}, bf16[640,256]{1,0:T(8,128)(2,1)S(1)}, u32[]{:S(2)}, u32[]{:S(2)}) %collective-permute-start.5) | collective-permute-done | bytes 327712 | tf_op jit(solution)/shard_map/ppermute | solution.py:260
  45.5 1.5 %collective-permute-start.6 = (bf16[64,4096]{1,0:T(8,128)(2,1)S(1)}, bf16[64,4096]{1,0:T(8,128)(2,1)S(1)}, u32[]{:S(2)}, u32[]{:S(2)}) collective-permute-start(bf16[64,4096]{1,0:T(8,128)(2,1)S(1)} %slice.6), channel_id=1, source_target_pairs={{0,4},{1,5},{2,6},{3,7},{4,0},{5,1},{6,2},{7,3},{8,12},{9,13},{10,... | collective-permute-start | bytes 1572872 | tf_op jit(solution)/shard_map/ppermute | solution.py:260
  47.6 1.9 %collective-permute-done.14.refs_18_ = bf16[4,256,128]{2,1,0:T(8,128)(2,1)S(1)} collective-permute-done((bf16[4,256,128]{2,1,0:T(8,128)(2,1)S(1)}, bf16[4,256,128]{2,1,0:T(8,128)(2,1)S(1)}, u32[]{:S(2)}, u32[]{:S(2)}) %collective-permute-start.14) | collective-permute-done | bytes 262176 | tf_op jit(solution)/shard_map/ppermute | solution.py:260
  49.5 9.1 %collective-permute-done.7.refs_4_ = bf16[64,4096]{1,0:T(8,128)(2,1)S(1)} collective-permute-done((bf16[64,4096]{1,0:T(8,128)(2,1)S(1)}, bf16[64,4096]{1,0:T(8,128)(2,1)S(1)}, u32[]{:S(2)}, u32[]{:S(2)}) %collective-permute-start.7) | collective-permute-done | bytes 524320 | tf_op jit(solution)/shard_map/ppermute | solution.py:260
  58.7 4.7 %shard_map.86 = (bf16[4,128,128]{2,1,0:T(8,128)(2,1)S(1)}, bf16[256,512]{1,0:T(8,128)(2,1)S(1)}, bf16[4,256,128]{2,1,0:T(8,128)(2,1)S(1)}, bf16[4,128,256]{2,1,0...) custom-call(s32[1]{0:T(128)} %bitcast.place, ...), custom_call_target="tpu_custom_call" | custom-call | flops 1476395008 | bytes 9437188 | tf_op jit(solution)/shard_map/pallas_call | solution.py:40
  67.1 0.7 collective-permute-start.18
  67.8 1.3 %collective-permute-start.17 = (bf16[128,128]{1,0:T(8,128)(2,1)S(1)}, bf16[128,128]{1,0:T(8,128)(2,1)S(1)}, u32[]{:S(2)}, u32[]{:S(2)}) collective-permute-start(bf16[128,128]{1,0:T(8,128)(2,1)S(1)} %shard_map.88), channel_id=1, source_target_pairs={{16,0},{17,1},{18,2},{19,3},{20,4},{21,5},{22,6},{23,7},{24,8},{25... | collective-permute-start | bytes 98312 | tf_op jit(solution)/shard_map/ppermute | solution.py:272
  69.1 1.9 %collective-permute-start.16 = (bf16[128,128]{1,0:T(8,128)(2,1)S(1)}, bf16[128,128]{1,0:T(8,128)(2,1)S(1)}, u32[]{:S(2)}, u32[]{:S(2)}) collective-permute-start(bf16[128,128]{1,0:T(8,128)(2,1)S(1)} %shard_map.88), channel_id=1, source_target_pairs={{8,0},{9,1},{10,2},{11,3},{12,4},{13,5},{14,6},{15,7},{16,8},{17,9... | collective-permute-start | bytes 98312 | tf_op jit(solution)/shard_map/ppermute | solution.py:272
  71.3 4.0 %collective-permute-start.27 = (bf16[256,512]{1,0:T(8,128)(2,1)S(1)}, bf16[256,512]{1,0:T(8,128)(2,1)S(1)}, u32[]{:S(2)}, u32[]{:S(2)}) collective-permute-start(bf16[256,512]{1,0:T(8,128)(2,1)S(1)} %add_convert_fusion.1), channel_id=1, source_target_pairs={{0,16},{1,17},{2,18},{3,19},{4,20},{5,21},{6,22},{7,23},{8,24},{9,... | collective-permute-start | bytes 786440 | tf_op jit(solution)/shard_map/ppermute | solution.py:260
  75.3 0.6 collective-permute-start.25
  76.2 1.1 %collective-permute-done.19.refs_10_ = bf16[128,128]{1,0:T(8,128)(2,1)S(1)} collective-permute-done((bf16[128,128]{1,0:T(8,128)(2,1)S(1)}, bf16[128,128]{1,0:T(8,128)(2,1)S(1)}, u32[]{:S(2)}, u32[]{:S(2)}) %collective-permute-start.19) | collective-permute-done | bytes 32800 | tf_op jit(solution)/shard_map/ppermute | solution.py:260
  77.3 0.7 shard_map.89
  77.9 1.7 %collective-permute-start.20 = (bf16[128,512]{1,0:T(8,128)(2,1)S(1)}, bf16[128,512]{1,0:T(8,128)(2,1)S(1)}, u32[]{:S(2)}, u32[]{:S(2)}) collective-permute-start(bf16[128,512]{1,0:T(8,128)(2,1)S(1)} %get-tuple-element.73), channel_id=1, source_target_pairs={{0,2},{1,3},{2,0},{3,1},{4,6},{5,7},{6,4},{7,5},{8,10},{9,11},{10,... | collective-permute-start | bytes 393224 | tf_op jit(solution)/shard_map/ppermute | solution.py:260
  79.7 1.7 %collective-permute-start.21 = (bf16[128,512]{1,0:T(8,128)(2,1)S(1)}, bf16[128,512]{1,0:T(8,128)(2,1)S(1)}, u32[]{:S(2)}, u32[]{:S(2)}) collective-permute-start(bf16[128,512]{1,0:T(8,128)(2,1)S(1)} %get-tuple-element.74), channel_id=1, source_target_pairs={{0,4},{1,5},{2,6},{3,7},{4,0},{5,1},{6,2},{7,3},{8,12},{9,13},{10,... | collective-permute-start | bytes 393224 | tf_op jit(solution)/shard_map/ppermute | solution.py:260
  81.4 2.8 %collective-permute-done.29.refs_2_ = bf16[256,512]{1,0:T(8,128)(2,1)S(1)} collective-permute-done((bf16[256,512]{1,0:T(8,128)(2,1)S(1)}, bf16[256,512]{1,0:T(8,128)(2,1)S(1)}, u32[]{:S(2)}, u32[]{:S(2)}) %collective-permute-start.29) | collective-permute-done | bytes 262176 | tf_op jit(solution)/shard_map/ppermute | solution.py:260
  84.2 2.8 %collective-permute-start.22 = (bf16[128,512]{1,0:T(8,128)(2,1)S(1)}, bf16[128,512]{1,0:T(8,128)(2,1)S(1)}, u32[]{:S(2)}, u32[]{:S(2)}) collective-permute-start(bf16[128,512]{1,0:T(8,128)(2,1)S(1)} %get-tuple-element.75), channel_id=1, source_target_pairs={{0,6},{1,7},{2,4},{3,5},{4,2},{5,3},{6,0},{7,1},{8,14},{9,15},{10,... | collective-permute-start | bytes 393224 | tf_op jit(solution)/shard_map/ppermute | solution.py:260
  87.0 6.3 %collective-permute-done.27.refs_1_ = bf16[256,512]{1,0:T(8,128)(2,1)S(1)} collective-permute-done((bf16[256,512]{1,0:T(8,128)(2,1)S(1)}, bf16[256,512]{1,0:T(8,128)(2,1)S(1)}, u32[]{:S(2)}, u32[]{:S(2)}) %collective-permute-start.27) | collective-permute-done | bytes 262176 | tf_op jit(solution)/shard_map/ppermute | solution.py:260
  93.3 5.9 %collective-permute-done.25.refs_0_ = bf16[256,512]{1,0:T(8,128)(2,1)S(1)} collective-permute-done((bf16[256,512]{1,0:T(8,128)(2,1)S(1)}, bf16[256,512]{1,0:T(8,128)(2,1)S(1)}, u32[]{:S(2)}, u32[]{:S(2)}) %collective-permute-start.25) | collective-permute-done | bytes 262176 | tf_op jit(solution)/shard_map/ppermute | solution.py:260
  99.4 1.7 %collective-permute-start.30 = (bf16[256,128]{1,0:T(8,128)(2,1)S(1)}, bf16[256,128]{1,0:T(8,128)(2,1)S(1)}, u32[]{:S(2)}, u32[]{:S(2)}) collective-permute-start(bf16[256,128]{1,0:T(8,128)(2,1)S(1)} %get-tuple-element.87), channel_id=1, source_target_pairs={{0,2},{1,3},{2,0},{3,1},{4,6},{5,7},{6,4},{7,5},{8,10},{9,11},{10,... | collective-permute-start | bytes 196616 | tf_op jit(solution)/shard_map/ppermute | solution.py:260
  101.1 1.7 %collective-permute-start.31 = (bf16[256,128]{1,0:T(8,128)(2,1)S(1)}, bf16[256,128]{1,0:T(8,128)(2,1)S(1)}, u32[]{:S(2)}, u32[]{:S(2)}) collective-permute-start(bf16[256,128]{1,0:T(8,128)(2,1)S(1)} %get-tuple-element.88), channel_id=1, source_target_pairs={{0,4},{1,5},{2,6},{3,7},{4,0},{5,1},{6,2},{7,3},{8,12},{9,13},{10,... | collective-permute-start | bytes 196616 | tf_op jit(solution)/shard_map/ppermute | solution.py:260
  102.9 0.9 shard_map.90
  103.8 2.3 %collective-permute-done.31.refs_2_ = bf16[256,128]{1,0:T(8,128)(2,1)S(1)} collective-permute-done((bf16[256,128]{1,0:T(8,128)(2,1)S(1)}, bf16[256,128]{1,0:T(8,128)(2,1)S(1)}, u32[]{:S(2)}, u32[]{:S(2)}) %collective-permute-start.31) | collective-permute-done | bytes 65568 | tf_op jit(solution)/shard_map/ppermute | solution.py:260
  106.1 1.9 %collective-permute-done.32.refs_3_ = bf16[256,128]{1,0:T(8,128)(2,1)S(1)} collective-permute-done((bf16[256,128]{1,0:T(8,128)(2,1)S(1)}, bf16[256,128]{1,0:T(8,128)(2,1)S(1)}, u32[]{:S(2)}, u32[]{:S(2)}) %collective-permute-start.32) | collective-permute-done | bytes 65568 | tf_op jit(solution)/shard_map/ppermute | solution.py:260
  108.0 1.0 shard_map.96
  (60 shorter events, 9.1 us)
Async XLA Ops:
  2.8 8.1 %collective-permute-start = (bf16[384,256]{1,0:T(8,128)(2,1)}, bf16[384,256]{1,0:T(8,128)(2,1)S(1)}, u32[]{:S(2)}, u32[]{:S(2)}) collective-permute-start(bf16[384,256]{1,0:T(8,128)(2,1)} %get-tuple-element.53), channel_id=1, source_target_pairs={{0,2},{1,3},{2,0},{3,1},{4,6},{5,7},{6,4},{7,5},{8,10},{9,11},{10,... | collective-permute-start | bytes 589832 | tf_op jit(solution)/shard_map/ppermute | solution.py:260
  3.4 12.2 %collective-permute-start.1 = (bf16[384,256]{1,0:T(8,128)(2,1)}, bf16[384,256]{1,0:T(8,128)(2,1)S(1)}, u32[]{:S(2)}, u32[]{:S(2)}) collective-permute-start(bf16[384,256]{1,0:T(8,128)(2,1)} %get-tuple-element.54), channel_id=1, source_target_pairs={{0,4},{1,5},{2,6},{3,7},{4,0},{5,1},{6,2},{7,3},{8,12},{9,13},{10,... | collective-permute-start | bytes 589832 | tf_op jit(solution)/shard_map/ppermute | solution.py:260
  3.9 11.7 %collective-permute-start.2 = (bf16[384,256]{1,0:T(8,128)(2,1)}, bf16[384,256]{1,0:T(8,128)(2,1)S(1)}, u32[]{:S(2)}, u32[]{:S(2)}) collective-permute-start(bf16[384,256]{1,0:T(8,128)(2,1)} %get-tuple-element.55), channel_id=1, source_target_pairs={{0,6},{1,7},{2,4},{3,5},{4,2},{5,3},{6,0},{7,1},{8,14},{9,15},{10,... | collective-permute-start | bytes 589832 | tf_op jit(solution)/shard_map/ppermute | solution.py:260
  6.4 38.5 %collective-permute-start.4 = (bf16[128,4096]{1,0:T(8,128)(2,1)}, bf16[128,4096]{1,0:T(8,128)(2,1)S(1)}, u32[]{:S(2)}, u32[]{:S(2)}) collective-permute-start(bf16[128,4096]{1,0:T(8,128)(2,1)} %refs_0_.4), channel_id=1, source_target_pairs={{0,4},{1,5},{2,6},{3,7},{4,0},{5,1},{6,2},{7,3},{8,12},{9,13},{10,... | collective-permute-start | bytes 3145736 | tf_op jit(solution)/shard_map/ppermute | solution.py:260
  6.9 38.0 %collective-permute-start.3 = (bf16[128,4096]{1,0:T(8,128)(2,1)}, bf16[128,4096]{1,0:T(8,128)(2,1)S(1)}, u32[]{:S(2)}, u32[]{:S(2)}) collective-permute-start(bf16[128,4096]{1,0:T(8,128)(2,1)} %refs_0_.4), channel_id=1, source_target_pairs={{0,2},{1,3},{2,0},{3,1},{4,6},{5,7},{6,4},{7,5},{8,10},{9,11},{10,... | collective-permute-start | bytes 3145736 | tf_op jit(solution)/shard_map/ppermute | solution.py:260
  16.9 17.6 %collective-permute-start.9 = (bf16[640,256]{1,0:T(8,128)(2,1)S(1)}, bf16[640,256]{1,0:T(8,128)(2,1)S(1)}, u32[]{:S(2)}, u32[]{:S(2)}) collective-permute-start(bf16[640,256]{1,0:T(8,128)(2,1)S(1)} %get-tuple-element.62.refs_9_), channel_id=1, source_target_pairs={{0,16},{1,17},{2,18},{3,19},{4,20},{5,21},{6,22},{7,23},{8,24},{9,... | collective-permute-start | bytes 983048 | tf_op jit(solution)/shard_map/ppermute | solution.py:260
  19.5 15.8 %collective-permute-start.8 = (bf16[640,256]{1,0:T(8,128)(2,1)S(1)}, bf16[640,256]{1,0:T(8,128)(2,1)S(1)}, u32[]{:S(2)}, u32[]{:S(2)}) collective-permute-start(bf16[640,256]{1,0:T(8,128)(2,1)S(1)} %get-tuple-element.62.refs_9_), channel_id=1, source_target_pairs={{0,8},{1,9},{2,10},{3,11},{4,12},{5,13},{6,14},{7,15},{8,0},{9,1},... | collective-permute-start | bytes 983048 | tf_op jit(solution)/shard_map/ppermute | solution.py:260
  20.0 24.9 %collective-permute-start.5 = (bf16[640,256]{1,0:T(8,128)(2,1)S(1)}, bf16[640,256]{1,0:T(8,128)(2,1)S(1)}, u32[]{:S(2)}, u32[]{:S(2)}) collective-permute-start(bf16[640,256]{1,0:T(8,128)(2,1)S(1)} %get-tuple-element.62.refs_9_), channel_id=1, source_target_pairs={{0,24},{1,25},{2,26},{3,27},{4,28},{5,29},{6,30},{7,31},{8,16},{9,... | collective-permute-start | bytes 983048 | tf_op jit(solution)/shard_map/ppermute | solution.py:260
  34.5 12.6 %collective-permute-start.12 = (bf16[640,256]{1,0:T(8,128)(2,1)S(1)}, bf16[640,256]{1,0:T(8,128)(2,1)S(1)}, u32[]{:S(2)}, u32[]{:S(2)}) collective-permute-start(bf16[640,256]{1,0:T(8,128)(2,1)S(1)} %collective-permute-done.9.refs_11_), channel_id=1, source_target_pairs={{0,1},{1,0},{2,3},{3,2},{4,5},{5,4},{6,7},{7,6},{8,9},{9,8},{10,11... | collective-permute-start | bytes 983048 | tf_op jit(solution)/shard_map/ppermute | solution.py:260
  35.4 12.2 %collective-permute-start.11 = (bf16[640,256]{1,0:T(8,128)(2,1)S(1)}, bf16[640,256]{1,0:T(8,128)(2,1)S(1)}, u32[]{:S(2)}, u32[]{:S(2)}) collective-permute-start(bf16[640,256]{1,0:T(8,128)(2,1)S(1)} %collective-permute-done.8.refs_10_), channel_id=1, source_target_pairs={{0,1},{1,0},{2,3},{3,2},{4,5},{5,4},{6,7},{7,6},{8,9},{9,8},{10,11... | collective-permute-start | bytes 983048 | tf_op jit(solution)/shard_map/ppermute | solution.py:260
  44.9 13.7 %collective-permute-start.7 = (bf16[64,4096]{1,0:T(8,128)(2,1)S(1)}, bf16[64,4096]{1,0:T(8,128)(2,1)S(1)}, u32[]{:S(2)}, u32[]{:S(2)}) collective-permute-start(bf16[64,4096]{1,0:T(8,128)(2,1)S(1)} %slice.7), channel_id=1, source_target_pairs={{0,2},{1,3},{2,0},{3,1},{4,6},{5,7},{6,4},{7,5},{8,10},{9,11},{10,... | collective-permute-start | bytes 1572872 | tf_op jit(solution)/shard_map/ppermute | solution.py:260
  45.5 13.2 %collective-permute-start.6 = (bf16[64,4096]{1,0:T(8,128)(2,1)S(1)}, bf16[64,4096]{1,0:T(8,128)(2,1)S(1)}, u32[]{:S(2)}, u32[]{:S(2)}) collective-permute-start(bf16[64,4096]{1,0:T(8,128)(2,1)S(1)} %slice.6), channel_id=1, source_target_pairs={{0,4},{1,5},{2,6},{3,7},{4,0},{5,1},{6,2},{7,3},{8,12},{9,13},{10,... | collective-permute-start | bytes 1572872 | tf_op jit(solution)/shard_map/ppermute | solution.py:260
  47.1 2.5 %collective-permute-start.10 = (bf16[640,256]{1,0:T(8,128)(2,1)S(1)}, bf16[640,256]{1,0:T(8,128)(2,1)S(1)}, u32[]{:S(2)}, u32[]{:S(2)}) collective-permute-start(bf16[640,256]{1,0:T(8,128)(2,1)S(1)} %get-tuple-element.62.refs_9_), channel_id=1, source_target_pairs={{0,1},{1,0},{2,3},{3,2},{4,5},{5,4},{6,7},{7,6},{8,9},{9,8},{10,11... | collective-permute-start | bytes 983048 | tf_op jit(solution)/shard_map/ppermute | solution.py:260
  47.1 2.5 %collective-permute-start.13 = (bf16[640,256]{1,0:T(8,128)(2,1)S(1)}, bf16[640,256]{1,0:T(8,128)(2,1)S(1)}, u32[]{:S(2)}, u32[]{:S(2)}) collective-permute-start(bf16[640,256]{1,0:T(8,128)(2,1)S(1)} %collective-permute-done.5.refs_12_), channel_id=1, source_target_pairs={{0,1},{1,0},{2,3},{3,2},{4,5},{5,4},{6,7},{7,6},{8,9},{9,8},{10,11... | collective-permute-start | bytes 983048 | tf_op jit(solution)/shard_map/ppermute | solution.py:260
  47.6 2.0 %collective-permute-start.14 = (bf16[4,256,128]{2,1,0:T(8,128)(2,1)S(1)}, bf16[4,256,128]{2,1,0:T(8,128)(2,1)S(1)}, u32[]{:S(2)}, u32[]{:S(2)}) collective-permute-start(bf16[4,256,128]{2,1,0:T(8,128)(2,1)S(1)} %get-tuple-element.63.refs_17_), channel_id=1, source_target_pairs={{0,1},{1,0},{2,3},{3,2},{4,5},{5,4},{6,7},{7,6},{8,9},{9,8},{10,11... | collective-permute-start | bytes 786440 | tf_op jit(solution)/shard_map/ppermute | solution.py:260
  63.4 3.6 %collective-permute-start.15 = (bf16[4,256,128]{2,1,0:T(8,128)(2,1)S(1)}, bf16[4,256,128]{2,1,0:T(8,128)(2,1)S(1)}, u32[]{:S(2)}, u32[]{:S(2)}) collective-permute-start(bf16[4,256,128]{2,1,0:T(8,128)(2,1)S(1)} %get-tuple-element.71.own.refs_7_), channel_id=1, source_target_pairs={{0,1},{1,0},{2,3},{3,2},{4,5},{5,4},{6,7},{7,6},{8,9},{9,8},{10,11... | collective-permute-start | bytes 786440 | tf_op jit(solution)/shard_map/ppermute | solution.py:260
  64.0 3.8 %collective-permute-start.28 = (bf16[256,512]{1,0:T(8,128)(2,1)S(1)}, bf16[256,512]{1,0:T(8,128)(2,1)S(1)}, u32[]{:S(2)}, u32[]{:S(2)}) collective-permute-start(bf16[256,512]{1,0:T(8,128)(2,1)S(1)} %get-tuple-element.85), channel_id=1, source_target_pairs={{0,1},{1,0},{2,3},{3,2},{4,5},{5,4},{6,7},{7,6},{8,9},{9,8},{10,11... | collective-permute-start | bytes 786440 | tf_op jit(solution)/shard_map/ppermute | solution.py:260
  65.0 4.2 %collective-permute-start.26 = (bf16[256,512]{1,0:T(8,128)(2,1)S(1)}, bf16[256,512]{1,0:T(8,128)(2,1)S(1)}, u32[]{:S(2)}, u32[]{:S(2)}) collective-permute-start(bf16[256,512]{1,0:T(8,128)(2,1)S(1)} %get-tuple-element.83), channel_id=1, source_target_pairs={{0,1},{1,0},{2,3},{3,2},{4,5},{5,4},{6,7},{7,6},{8,9},{9,8},{10,11... | collective-permute-start | bytes 786440 | tf_op jit(solution)/shard_map/ppermute | solution.py:260
  65.5 5.6 %collective-permute-start.24 = (bf16[256,512]{1,0:T(8,128)(2,1)S(1)}, bf16[256,512]{1,0:T(8,128)(2,1)S(1)}, u32[]{:S(2)}, u32[]{:S(2)}) collective-permute-start(bf16[256,512]{1,0:T(8,128)(2,1)S(1)} %get-tuple-element.81), channel_id=1, source_target_pairs={{0,1},{1,0},{2,3},{3,2},{4,5},{5,4},{6,7},{7,6},{8,9},{9,8},{10,11... | collective-permute-start | bytes 786440 | tf_op jit(solution)/shard_map/ppermute | solution.py:260
  66.5 9.5 %collective-permute-start.23 = (bf16[256,512]{1,0:T(8,128)(2,1)S(1)}, bf16[256,512]{1,0:T(8,128)(2,1)S(1)}, u32[]{:S(2)}, u32[]{:S(2)}) collective-permute-start(bf16[256,512]{1,0:T(8,128)(2,1)S(1)} %get-tuple-element.79), channel_id=1, source_target_pairs={{0,1},{1,0},{2,3},{3,2},{4,5},{5,4},{6,7},{7,6},{8,9},{9,8},{10,11... | collective-permute-start | bytes 786440 | tf_op jit(solution)/shard_map/ppermute | solution.py:260
  67.1 4.2 %collective-permute-start.18 = (bf16[128,128]{1,0:T(8,128)(2,1)S(1)}, bf16[128,128]{1,0:T(8,128)(2,1)S(1)}, u32[]{:S(2)}, u32[]{:S(2)}) collective-permute-start(bf16[128,128]{1,0:T(8,128)(2,1)S(1)} %shard_map.88), channel_id=1, source_target_pairs={{24,0},{25,1},{26,2},{27,3},{28,4},{29,5},{30,6},{31,7}} | collective-permute-start | bytes 98312 | tf_op jit(solution)/shard_map/ppermute | solution.py:272
  67.8 7.6 %collective-permute-start.17 = (bf16[128,128]{1,0:T(8,128)(2,1)S(1)}, bf16[128,128]{1,0:T(8,128)(2,1)S(1)}, u32[]{:S(2)}, u32[]{:S(2)}) collective-permute-start(bf16[128,128]{1,0:T(8,128)(2,1)S(1)} %shard_map.88), channel_id=1, source_target_pairs={{16,0},{17,1},{18,2},{19,3},{20,4},{21,5},{22,6},{23,7},{24,8},{25... | collective-permute-start | bytes 98312 | tf_op jit(solution)/shard_map/ppermute | solution.py:272
  69.1 6.8 %collective-permute-start.16 = (bf16[128,128]{1,0:T(8,128)(2,1)S(1)}, bf16[128,128]{1,0:T(8,128)(2,1)S(1)}, u32[]{:S(2)}, u32[]{:S(2)}) collective-permute-start(bf16[128,128]{1,0:T(8,128)(2,1)S(1)} %shard_map.88), channel_id=1, source_target_pairs={{8,0},{9,1},{10,2},{11,3},{12,4},{13,5},{14,6},{15,7},{16,8},{17,9... | collective-permute-start | bytes 98312 | tf_op jit(solution)/shard_map/ppermute | solution.py:272
  71.2 13.0 %collective-permute-start.29 = (bf16[256,512]{1,0:T(8,128)(2,1)S(1)}, bf16[256,512]{1,0:T(8,128)(2,1)S(1)}, u32[]{:S(2)}, u32[]{:S(2)}) collective-permute-start(bf16[256,512]{1,0:T(8,128)(2,1)S(1)} %add_convert_fusion), channel_id=1, source_target_pairs={{0,8},{1,9},{2,10},{3,11},{4,12},{5,13},{6,14},{7,15},{8,0},{9,1},... | collective-permute-start | bytes 786440 | tf_op jit(solution)/shard_map/ppermute | solution.py:260
  71.3 21.9 %collective-permute-start.27 = (bf16[256,512]{1,0:T(8,128)(2,1)S(1)}, bf16[256,512]{1,0:T(8,128)(2,1)S(1)}, u32[]{:S(2)}, u32[]{:S(2)}) collective-permute-start(bf16[256,512]{1,0:T(8,128)(2,1)S(1)} %add_convert_fusion.1), channel_id=1, source_target_pairs={{0,16},{1,17},{2,18},{3,19},{4,20},{5,21},{6,22},{7,23},{8,24},{9,... | collective-permute-start | bytes 786440 | tf_op jit(solution)/shard_map/ppermute | solution.py:260
  75.3 23.8 %collective-permute-start.25 = (bf16[256,512]{1,0:T(8,128)(2,1)S(1)}, bf16[256,512]{1,0:T(8,128)(2,1)S(1)}, u32[]{:S(2)}, u32[]{:S(2)}) collective-permute-start(bf16[256,512]{1,0:T(8,128)(2,1)S(1)} %add_convert_fusion.2), channel_id=1, source_target_pairs={{0,24},{1,25},{2,26},{3,27},{4,28},{5,29},{6,30},{7,31},{8,16},{9,... | collective-permute-start | bytes 786440 | tf_op jit(solution)/shard_map/ppermute | solution.py:260
  77.9 24.9 %collective-permute-start.20 = (bf16[128,512]{1,0:T(8,128)(2,1)S(1)}, bf16[128,512]{1,0:T(8,128)(2,1)S(1)}, u32[]{:S(2)}, u32[]{:S(2)}) collective-permute-start(bf16[128,512]{1,0:T(8,128)(2,1)S(1)} %get-tuple-element.73), channel_id=1, source_target_pairs={{0,2},{1,3},{2,0},{3,1},{4,6},{5,7},{6,4},{7,5},{8,10},{9,11},{10,... | collective-permute-start | bytes 393224 | tf_op jit(solution)/shard_map/ppermute | solution.py:260
  79.7 23.3 %collective-permute-start.21 = (bf16[128,512]{1,0:T(8,128)(2,1)S(1)}, bf16[128,512]{1,0:T(8,128)(2,1)S(1)}, u32[]{:S(2)}, u32[]{:S(2)}) collective-permute-start(bf16[128,512]{1,0:T(8,128)(2,1)S(1)} %get-tuple-element.74), channel_id=1, source_target_pairs={{0,4},{1,5},{2,6},{3,7},{4,0},{5,1},{6,2},{7,3},{8,12},{9,13},{10,... | collective-permute-start | bytes 393224 | tf_op jit(solution)/shard_map/ppermute | solution.py:260
  84.2 18.8 %collective-permute-start.22 = (bf16[128,512]{1,0:T(8,128)(2,1)S(1)}, bf16[128,512]{1,0:T(8,128)(2,1)S(1)}, u32[]{:S(2)}, u32[]{:S(2)}) collective-permute-start(bf16[128,512]{1,0:T(8,128)(2,1)S(1)} %get-tuple-element.75), channel_id=1, source_target_pairs={{0,6},{1,7},{2,4},{3,5},{4,2},{5,3},{6,0},{7,1},{8,14},{9,15},{10,... | collective-permute-start | bytes 393224 | tf_op jit(solution)/shard_map/ppermute | solution.py:260
  99.4 4.4 %collective-permute-start.30 = (bf16[256,128]{1,0:T(8,128)(2,1)S(1)}, bf16[256,128]{1,0:T(8,128)(2,1)S(1)}, u32[]{:S(2)}, u32[]{:S(2)}) collective-permute-start(bf16[256,128]{1,0:T(8,128)(2,1)S(1)} %get-tuple-element.87), channel_id=1, source_target_pairs={{0,2},{1,3},{2,0},{3,1},{4,6},{5,7},{6,4},{7,5},{8,10},{9,11},{10,... | collective-permute-start | bytes 196616 | tf_op jit(solution)/shard_map/ppermute | solution.py:260
  101.1 5.0 %collective-permute-start.31 = (bf16[256,128]{1,0:T(8,128)(2,1)S(1)}, bf16[256,128]{1,0:T(8,128)(2,1)S(1)}, u32[]{:S(2)}, u32[]{:S(2)}) collective-permute-start(bf16[256,128]{1,0:T(8,128)(2,1)S(1)} %get-tuple-element.88), channel_id=1, source_target_pairs={{0,4},{1,5},{2,6},{3,7},{4,0},{5,1},{6,2},{7,3},{8,12},{9,13},{10,... | collective-permute-start | bytes 196616 | tf_op jit(solution)/shard_map/ppermute | solution.py:260
  102.9 5.2 %collective-permute-start.32 = (bf16[256,128]{1,0:T(8,128)(2,1)S(1)}, bf16[256,128]{1,0:T(8,128)(2,1)S(1)}, u32[]{:S(2)}, u32[]{:S(2)}) collective-permute-start(bf16[256,128]{1,0:T(8,128)(2,1)S(1)} %get-tuple-element.89), channel_id=1, source_target_pairs={{0,6},{1,7},{2,4},{3,5},{4,2},{5,3},{6,0},{7,1},{8,14},{9,15},{10,... | collective-permute-start | bytes 196616 | tf_op jit(solution)/shard_map/ppermute | solution.py:260
  (4 other events, 17.3 us)

commit v3 on v2

--- a/solution.py
+++ b/solution.py
@@ -34,7 +34,7 @@
     return me >> low & HEADS_GROUP - 1, me >> high, me & CORES - 1
 
 
-def call(kernel, outs, args, flops=0, scratch=(), mib=16, space=pltpu.VMEM, urgent=False):
+def call(kernel, outs, args, flops=0, scratch=(), mib=16, space=pltpu.VMEM, urgent=0):
     shapes = [jax.ShapeDtypeStruct(shape, dtype) for shape, dtype in outs]
     moved = sum(a.size * a.dtype.itemsize for a in args) + sum(s.size * s.dtype.itemsize for s in shapes)
     return pl.pallas_call(
@@ -45,7 +45,7 @@
         out_specs=[pl.BlockSpec(memory_space=pltpu.VMEM)] * len(shapes),
         scratch_shapes=list(scratch),
         compiler_params=pltpu.CompilerParams(vmem_limit_bytes=mib << 20),
-        cost_estimate=pl.CostEstimate(flops=URGENT if urgent else flops, bytes_accessed=moved, transcendentals=0),
+        cost_estimate=pl.CostEstimate(flops=urgent or flops, bytes_accessed=moved, transcendentals=0),
     )(*args)
 
 
@@ -74,12 +74,23 @@
         copy.wait()
 
 
-def state_kernel(rows, depth, place, p0, p1, p2, p3, pay, states):
-    total = jnp.zeros((FEAT, HEAD_DIM), F32)
-    for j, p in enumerate((p0, p1, p2, p3)):
+def state_of(p, rows, depth):
+    keys = jnp.maximum(p[depth : depth + rows, :], 0)
+    return dot(keys, p[depth + rows :, :HEAD_DIM], ((0,), (0,)))
+
+
+def own_kernel(rows, depth, place, p, shard, state):
+    shard[...] = p[:depth, :]
+    state[...] = state_of(p, rows, depth)
+
+
+def state_kernel(rows, depth, place, shard, own_state, p1, p2, p3, pay, states):
+    pay[:depth, :] = shard[...]
+    total = own_state[...]
+    states[0] = total.astype(BF16)
+    for j, p in ((1, p1), (2, p2), (3, p3)):
         pay[j * depth : (j + 1) * depth, :] = p[:depth, :]
-        keys = jnp.maximum(p[depth : depth + rows, :], 0)
-        state = dot(keys, p[depth + rows :, :HEAD_DIM], ((0,), (0,)))
+        state = state_of(p, rows, depth)
         states[j] = state.astype(BF16)
         total = total + state
     total = total.astype(BF16)
@@ -277,21 +288,26 @@
         [place, w_query, key_input, values, cotangent],
         scratch=[pltpu.SemaphoreType.DMA((16,))],
         space=pltpu.HBM,
-        mib=62,
+        mib=59,
     )
     hidden, packs = lax.optimization_barrier((hidden, packs))
     p = [packs[0]] + [chip_swap(packs[k], k) for k in (1, 2, 3)]
     h1, h2 = chip_swap(hidden, 1), chip_swap(hidden, 2)
+    start = call(
+        functools.partial(own_kernel, rows, depth),
+        [((depth, FEAT), BF16), ((FEAT, HEAD_DIM), F32)],
+        [place, p[0]],
+    )
     pay, states = call(
         functools.partial(state_kernel, rows, depth),
         [((4 * depth + HALF, FEAT), BF16), ((4, FEAT, HEAD_DIM), BF16)],
-        [place, *p],
-        urgent=True,
+        [place, *start, *p[1:]],
+        urgent=URGENT,
     )
     pays = [pay] + [None] * (outer - 1)
-    for k in reversed(range(1, outer)):
-        pays[k] = plane_swap(pay, k)
-    h1, h2, pays[-1], late_pay, late_states = lax.optimization_barrier((h1, h2, pays[-1], pay, states))
+    for k in sorted(range(1, outer), key=lambda k: (k.bit_count(), -k)):
+        pays[k] = plane_swap(pays[k & k - 1], k & -k)
+    h1, h2, late_pay, late_states = lax.optimization_barrier((h1, h2, pay, states))
     h3 = [chip_swap(h1[: rows // 2], 2), chip_swap(h2[rows // 2 :], 1)]
     h = [hidden, h1, h2, *h3]
     other_pays = [core_swap(late_pay)] + [core_swap(pays[k]) for k in range(1, outer)]
@@ -319,9 +335,15 @@
         [place, grown, other_grown],
         scratch=[pltpu.VMEM((FEAT, HEAD_DIM), F32)],
     )
-    later = [down(half, k) for k in range(1, outer)]
+    rest, window, step = jnp.zeros(half.shape, F32), half, 1
+    while step < outer:
+        came = down(window, step)
+        rest = rest + came.astype(F32)
+        window = (window.astype(F32) + came.astype(F32)).astype(BF16)
+        step *= 2
     sums = [None] * outer
-    for k in reversed(range(outer)):
+    order = sorted(range(outer), key=lambda k: (-k.bit_count(), k))
+    for k in order:
         keep, give = call(
             functools.partial(grad_kernel, depth, k),
             [((FEAT, 4 * depth), F32), ((FEAT, 4 * depth), BF16)],
@@ -329,15 +351,21 @@
             flops=2 * positions * width * FEAT // outer,
         )
         sums[k] = keep + core_swap(give).astype(F32)
+    arrived = []
+    for k in order[:-1]:
+        came, onward = plane_swap(sums[k].astype(BF16), k & -k), k & k - 1
+        if onward:
+            sums[onward] = sums[onward] + came.astype(F32)
+        else:
+            arrived.append(came)
     own = sums[0]
-    arrived = [plane_swap(sums[k].astype(BF16), k) for k in reversed(range(1, outer))]
     val_part, key_part = call(
         functools.partial(side_kernel, rows),
         [((positions, HEAD_DIM), F32), ((positions, FEAT), F32)],
         [place, *kept],
         flops=6 * positions * FEAT * HEAD_DIM,
     )
-    rest = sum((x.astype(F32) for x in later), jnp.zeros((HALF, HEAD_DIM), F32)).astype(BF16)
+    rest = rest.astype(BF16)
     other_rest = core_swap(rest)
     outs = call(
         functools.partial(finish_kernel, rows, depth, outer),
@@ -356,12 +384,13 @@
         ],
         [place, *placed],
     )
+    own, placed = lax.optimization_barrier((own, placed))
     blocks = call(
         functools.partial(sum_kernel, depth),
         [((FEAT, depth), F32)] + [((FEAT, depth), BF16)] * 3,
         [place, own, *arrived],
         scratch=[pltpu.VMEM((4, FEAT, depth), F32)],
-        urgent=True,
+        urgent=URGENT,
     )
     columns = [blocks[0]] + [chip_swap(blocks[k], k) for k in (1, 2, 3)]
     (query_grad,) = call(

time: 109 us -> 98.4 us (0.903)
  the two profiles are of different devices: /device:TPU:14 before, /device:TPU:0 now
where the time goes in v3:
time: 98.4 us; the launch traced here: 98.2 us
  waiting for transfers between devices  51.2 us (52%)
  starting transfers between devices  32.6 us (33%)
  Pallas kernels  12.2 us (12%)
  local copies, waits for them, and re-layouts  1.01 us (1%)
    ppermute x30, waiting for transfers between devices, swap(): return lax.ppermute(block, 'ctx', [(i, i ^ bits) for i in range(count)])  45.1 us
    ppermute x30, starting transfers between devices, swap(): return lax.ppermute(block, 'ctx', [(i, i ^ bits) for i in range(count)])  30.1 us
    pallas_call x14, Pallas kernels, call(): pl.pallas_call(kernel, out_shape=shapes, in_specs=[pl.BlockSpec(memory_sp...  12.2 us
    ppermute x2, waiting for transfers between devices, down(): lax.ppermute(block, 'ctx', [(i, i - inner * k) for i in range(inner * k,...  6.05 us
    ppermute x2, starting transfers between devices, down(): lax.ppermute(block, 'ctx', [(i, i - inner * k) for i in range(inner * k,...  2.58 us
  transfers between devices with their start and end apart: 32, of which 15 were waited for; matrix products, arithmetic and copies ran while one was open for 0% of the time, Pallas kernels for 4%

profile of v3, /device:TPU:0, one launch (start us, length us, event | category | flops | bytes accessed | tf_op | source)
XLA Modules:
  0.0 98.2 jit_solution(7445030269176271475)
XLA Ops:
  0.6 2.2 %shard_map.84 = (bf16[384,256]{1,0:T(8,128)(2,1)}, bf16[384,256]{1,0:T(8,128)(2,1)}, bf16[384,256]{1,0:T(8,128)(2,1)}, bf16[384,256]{1,0:T(8,128)(2,1)}) custom-call(s32[1]{0:T(128)} %bitcast.place, bf16[128,1024]{1,0:T(8,128)(2,1)} %w.1, bf16[128,1024]{1,0:T(8,128)(2,1)} %key.1, bf16[128,512]{1,0:T(8,128)(2,1)} %val.1, bf16[128,512]{1,0:T(8,128)(2,1)} %cot.1), custom_call_target="tpu_custom_call" | custom-call | bytes 1572868 | tf_op jit(solution)/shard_map/pallas_call | solution.py:40
  2.8 3.0 %collective-permute-start = (bf16[384,256]{1,0:T(8,128)(2,1)}, bf16[384,256]{1,0:T(8,128)(2,1)S(1)}, u32[]{:S(2)}, u32[]{:S(2)}) collective-permute-start(bf16[384,256]{1,0:T(8,128)(2,1)} %get-tuple-element.55), channel_id=1, source_target_pairs={{0,2},{1,3},{2,0},{3,1},{4,6},{5,7},{6,4},{7,5},{8,10},{9,11},{10,... | collective-permute-start | bytes 589832 | tf_op jit(solution)/shard_map/ppermute | solution.py:271
  5.8 1.5 %collective-permute-start.1 = (bf16[384,256]{1,0:T(8,128)(2,1)}, bf16[384,256]{1,0:T(8,128)(2,1)S(1)}, u32[]{:S(2)}, u32[]{:S(2)}) collective-permute-start(bf16[384,256]{1,0:T(8,128)(2,1)} %get-tuple-element.56), channel_id=1, source_target_pairs={{0,4},{1,5},{2,6},{3,7},{4,0},{5,1},{6,2},{7,3},{8,12},{9,13},{10,... | collective-permute-start | bytes 589832 | tf_op jit(solution)/shard_map/ppermute | solution.py:271
  7.4 2.0 %collective-permute-start.4 = (bf16[128,4096]{1,0:T(8,128)(2,1)}, bf16[128,4096]{1,0:T(8,128)(2,1)S(1)}, u32[]{:S(2)}, u32[]{:S(2)}) collective-permute-start(bf16[128,4096]{1,0:T(8,128)(2,1)} %refs_0_.4), channel_id=1, source_target_pairs={{0,4},{1,5},{2,6},{3,7},{4,0},{5,1},{6,2},{7,3},{8,12},{9,13},{10,... | collective-permute-start | bytes 3145736 | tf_op jit(solution)/shard_map/ppermute | solution.py:271
  9.3 1.5 %collective-permute-start.3 = (bf16[128,4096]{1,0:T(8,128)(2,1)}, bf16[128,4096]{1,0:T(8,128)(2,1)S(1)}, u32[]{:S(2)}, u32[]{:S(2)}) collective-permute-start(bf16[128,4096]{1,0:T(8,128)(2,1)} %refs_0_.4), channel_id=1, source_target_pairs={{0,2},{1,3},{2,0},{3,1},{4,6},{5,7},{6,4},{7,5},{8,10},{9,11},{10,... | collective-permute-start | bytes 3145736 | tf_op jit(solution)/shard_map/ppermute | solution.py:271
  10.8 0.9 copy-done.1
  12.0 6.1 %collective-permute-done.1.p2.refs_7_.refs_2_ = bf16[384,256]{1,0:T(8,128)(2,1)S(1)} collective-permute-done((bf16[384,256]{1,0:T(8,128)(2,1)}, bf16[384,256]{1,0:T(8,128)(2,1)S(1)}, u32[]{:S(2)}, u32[]{:S(2)}) %collective-permute-start.1) | collective-permute-done | bytes 196640 | tf_op jit(solution)/shard_map/ppermute | solution.py:271
  18.3 2.7 %collective-permute-start.8 = (bf16[640,256]{1,0:T(8,128)(2,1)S(1)}, bf16[640,256]{1,0:T(8,128)(2,1)S(1)}, u32[]{:S(2)}, u32[]{:S(2)}) collective-permute-start(bf16[640,256]{1,0:T(8,128)(2,1)S(1)} %get-tuple-element.65.refs_9_), channel_id=1, source_target_pairs={{0,16},{1,17},{2,18},{3,19},{4,20},{5,21},{6,22},{7,23},{8,24},{9,... | collective-permute-start | bytes 983048 | tf_op jit(solution)/shard_map/ppermute | solution.py:271
  21.0 1.6 %collective-permute-start.7 = (bf16[640,256]{1,0:T(8,128)(2,1)S(1)}, bf16[640,256]{1,0:T(8,128)(2,1)S(1)}, u32[]{:S(2)}, u32[]{:S(2)}) collective-permute-start(bf16[640,256]{1,0:T(8,128)(2,1)S(1)} %get-tuple-element.65.refs_9_), channel_id=1, source_target_pairs={{0,8},{1,9},{2,10},{3,11},{4,12},{5,13},{6,14},{7,15},{8,0},{9,1},... | collective-permute-start | bytes 983048 | tf_op jit(solution)/shard_map/ppermute | solution.py:271
  22.6 10.7 %collective-permute-done.8.refs_11_ = bf16[640,256]{1,0:T(8,128)(2,1)S(1)} collective-permute-done((bf16[640,256]{1,0:T(8,128)(2,1)S(1)}, bf16[640,256]{1,0:T(8,128)(2,1)S(1)}, u32[]{:S(2)}, u32[]{:S(2)}) %collective-permute-start.8) | collective-permute-done | bytes 327712 | tf_op jit(solution)/shard_map/ppermute | solution.py:271
  34.4 4.7 %collective-permute-done.4.refs_2_ = bf16[128,4096]{1,0:T(8,128)(2,1)S(1)} collective-permute-done((bf16[128,4096]{1,0:T(8,128)(2,1)}, bf16[128,4096]{1,0:T(8,128)(2,1)S(1)}, u32[]{:S(2)}, u32[]{:S(2)}) %collective-permute-start.4) | collective-permute-done | bytes 1048608 | tf_op jit(solution)/shard_map/ppermute | solution.py:271
  39.6 1.7 %collective-permute-start.5 = (bf16[64,4096]{1,0:T(8,128)(2,1)S(1)}, bf16[64,4096]{1,0:T(8,128)(2,1)S(1)}, u32[]{:S(2)}, u32[]{:S(2)}) collective-permute-start(bf16[64,4096]{1,0:T(8,128)(2,1)S(1)} %slice.6), channel_id=1, source_target_pairs={{0,4},{1,5},{2,6},{3,7},{4,0},{5,1},{6,2},{7,3},{8,12},{9,13},{10,... | collective-permute-start | bytes 1572872 | tf_op jit(solution)/shard_map/ppermute | solution.py:271
  42.4 1.0 %collective-permute-done.13.refs_16_ = bf16[640,256]{1,0:T(8,128)(2,1)S(1)} collective-permute-done((bf16[640,256]{1,0:T(8,128)(2,1)S(1)}, bf16[640,256]{1,0:T(8,128)(2,1)S(1)}, u32[]{:S(2)}, u32[]{:S(2)}) %collective-permute-start.13) | collective-permute-done | bytes 327712 | tf_op jit(solution)/shard_map/ppermute | solution.py:271
  44.2 7.5 %collective-permute-done.6.refs_4_ = bf16[64,4096]{1,0:T(8,128)(2,1)S(1)} collective-permute-done((bf16[64,4096]{1,0:T(8,128)(2,1)S(1)}, bf16[64,4096]{1,0:T(8,128)(2,1)S(1)}, u32[]{:S(2)}, u32[]{:S(2)}) %collective-permute-start.6) | collective-permute-done | bytes 524320 | tf_op jit(solution)/shard_map/ppermute | solution.py:271
  52.1 4.7 %shard_map.87 = (bf16[4,128,128]{2,1,0:T(8,128)(2,1)S(1)}, bf16[256,512]{1,0:T(8,128)(2,1)S(1)}, bf16[4,256,128]{2,1,0:T(8,128)(2,1)S(1)}, bf16[4,128,256]{2,1,0...) custom-call(s32[1]{0:T(128)} %bitcast.place, ...), custom_call_target="tpu_custom_call" | custom-call | flops 1476395008 | bytes 9437188 | tf_op jit(solution)/shard_map/pallas_call | solution.py:40
  60.5 1.3 %collective-permute-start.16 = (bf16[128,128]{1,0:T(8,128)(2,1)S(1)}, bf16[128,128]{1,0:T(8,128)(2,1)S(1)}, u32[]{:S(2)}, u32[]{:S(2)}) collective-permute-start(bf16[128,128]{1,0:T(8,128)(2,1)S(1)} %shard_map.89), channel_id=1, source_target_pairs={{8,0},{9,1},{10,2},{11,3},{12,4},{13,5},{14,6},{15,7},{16,8},{17,9... | collective-permute-start | bytes 98312 | tf_op jit(solution)/shard_map/ppermute | solution.py:283
  61.8 2.7 %collective-permute-start.27 = (bf16[256,512]{1,0:T(8,128)(2,1)S(1)}, bf16[256,512]{1,0:T(8,128)(2,1)S(1)}, u32[]{:S(2)}, u32[]{:S(2)}) collective-permute-start(bf16[256,512]{1,0:T(8,128)(2,1)S(1)} %add_convert_fusion.1), channel_id=1, source_target_pairs={{0,8},{1,9},{2,10},{3,11},{4,12},{5,13},{6,14},{7,15},{8,0},{9,1},... | collective-permute-start | bytes 786440 | tf_op jit(solution)/shard_map/ppermute | solution.py:271
  64.6 2.0 %collective-permute-done.16 = bf16[128,128]{1,0:T(8,128)(2,1)S(1)} collective-permute-done((bf16[128,128]{1,0:T(8,128)(2,1)S(1)}, bf16[128,128]{1,0:T(8,128)(2,1)S(1)}, u32[]{:S(2)}, u32[]{:S(2)}) %collective-permute-start.16) | collective-permute-done | bytes 32800 | tf_op jit(solution)/shard_map/ppermute | solution.py:283
  66.5 1.3 %collective-permute-start.17 = (bf16[128,128]{1,0:T(8,128)(2,1)S(1)}, bf16[128,128]{1,0:T(8,128)(2,1)S(1)}, u32[]{:S(2)}, u32[]{:S(2)}) collective-permute-start(bf16[128,128]{1,0:T(8,128)(2,1)S(1)} %fusion), channel_id=1, source_target_pairs={{16,0},{17,1},{18,2},{19,3},{20,4},{21,5},{22,6},{23,7},{24,8},{25... | collective-permute-start | bytes 98312 | tf_op jit(solution)/shard_map/ppermute | solution.py:283
  67.9 1.4 %collective-permute-start.24 = (bf16[256,512]{1,0:T(8,128)(2,1)S(1)}, bf16[256,512]{1,0:T(8,128)(2,1)S(1)}, u32[]{:S(2)}, u32[]{:S(2)}) collective-permute-start(bf16[256,512]{1,0:T(8,128)(2,1)S(1)} %add_convert_fusion.2), channel_id=1, source_target_pairs={{0,8},{1,9},{2,10},{3,11},{4,12},{5,13},{6,14},{7,15},{8,0},{9,1},... | collective-permute-start | bytes 786440 | tf_op jit(solution)/shard_map/ppermute | solution.py:271
  69.3 4.1 %collective-permute-done.17 = bf16[128,128]{1,0:T(8,128)(2,1)S(1)} collective-permute-done((bf16[128,128]{1,0:T(8,128)(2,1)S(1)}, bf16[128,128]{1,0:T(8,128)(2,1)S(1)}, u32[]{:S(2)}, u32[]{:S(2)}) %collective-permute-start.17) | collective-permute-done | bytes 32800 | tf_op jit(solution)/shard_map/ppermute | solution.py:283
  73.6 1.4 %collective-permute-start.28 = (bf16[256,512]{1,0:T(8,128)(2,1)S(1)}, bf16[256,512]{1,0:T(8,128)(2,1)S(1)}, u32[]{:S(2)}, u32[]{:S(2)}) collective-permute-start(bf16[256,512]{1,0:T(8,128)(2,1)S(1)} %add_convert_fusion), channel_id=1, source_target_pairs={{0,16},{1,17},{2,18},{3,19},{4,20},{5,21},{6,22},{7,23},{8,24},{9,... | collective-permute-start | bytes 786440 | tf_op jit(solution)/shard_map/ppermute | solution.py:271
  75.7 1.5 %collective-permute-start.19 = (bf16[128,512]{1,0:T(8,128)(2,1)S(1)}, bf16[128,512]{1,0:T(8,128)(2,1)S(1)}, u32[]{:S(2)}, u32[]{:S(2)}) collective-permute-start(bf16[128,512]{1,0:T(8,128)(2,1)S(1)} %get-tuple-element.76), channel_id=1, source_target_pairs={{0,2},{1,3},{2,0},{3,1},{4,6},{5,7},{6,4},{7,5},{8,10},{9,11},{10,... | collective-permute-start | bytes 393224 | tf_op jit(solution)/shard_map/ppermute | solution.py:271
  77.1 1.4 %collective-permute-start.20 = (bf16[128,512]{1,0:T(8,128)(2,1)S(1)}, bf16[128,512]{1,0:T(8,128)(2,1)S(1)}, u32[]{:S(2)}, u32[]{:S(2)}) collective-permute-start(bf16[128,512]{1,0:T(8,128)(2,1)S(1)} %get-tuple-element.77), channel_id=1, source_target_pairs={{0,4},{1,5},{2,6},{3,7},{4,0},{5,1},{6,2},{7,3},{8,12},{9,13},{10,... | collective-permute-start | bytes 393224 | tf_op jit(solution)/shard_map/ppermute | solution.py:271
  79.3 2.2 %collective-permute-done.19.refs_1_ = bf16[128,512]{1,0:T(8,128)(2,1)S(1)} collective-permute-done((bf16[128,512]{1,0:T(8,128)(2,1)S(1)}, bf16[128,512]{1,0:T(8,128)(2,1)S(1)}, u32[]{:S(2)}, u32[]{:S(2)}) %collective-permute-start.19) | collective-permute-done | bytes 131104 | tf_op jit(solution)/shard_map/ppermute | solution.py:271
  81.5 3.4 %collective-permute-done.20.refs_2_ = bf16[128,512]{1,0:T(8,128)(2,1)S(1)} collective-permute-done((bf16[128,512]{1,0:T(8,128)(2,1)S(1)}, bf16[128,512]{1,0:T(8,128)(2,1)S(1)}, u32[]{:S(2)}, u32[]{:S(2)}) %collective-permute-start.20) | collective-permute-done | bytes 131104 | tf_op jit(solution)/shard_map/ppermute | solution.py:271
  84.9 4.0 %collective-permute-done.28.refs_1_ = bf16[256,512]{1,0:T(8,128)(2,1)S(1)} collective-permute-done((bf16[256,512]{1,0:T(8,128)(2,1)S(1)}, bf16[256,512]{1,0:T(8,128)(2,1)S(1)}, u32[]{:S(2)}, u32[]{:S(2)}) %collective-permute-start.28) | collective-permute-done | bytes 262176 | tf_op jit(solution)/shard_map/ppermute | solution.py:271
  89.1 1.4 %collective-permute-start.29 = (bf16[256,128]{1,0:T(8,128)(2,1)S(1)}, bf16[256,128]{1,0:T(8,128)(2,1)S(1)}, u32[]{:S(2)}, u32[]{:S(2)}) collective-permute-start(bf16[256,128]{1,0:T(8,128)(2,1)S(1)} %get-tuple-element.91), channel_id=1, source_target_pairs={{0,2},{1,3},{2,0},{3,1},{4,6},{5,7},{6,4},{7,5},{8,10},{9,11},{10,... | collective-permute-start | bytes 196616 | tf_op jit(solution)/shard_map/ppermute | solution.py:271
  90.5 1.5 %collective-permute-start.30 = (bf16[256,128]{1,0:T(8,128)(2,1)S(1)}, bf16[256,128]{1,0:T(8,128)(2,1)S(1)}, u32[]{:S(2)}, u32[]{:S(2)}) collective-permute-start(bf16[256,128]{1,0:T(8,128)(2,1)S(1)} %get-tuple-element.92), channel_id=1, source_target_pairs={{0,4},{1,5},{2,6},{3,7},{4,0},{5,1},{6,2},{7,3},{8,12},{9,13},{10,... | collective-permute-start | bytes 196616 | tf_op jit(solution)/shard_map/ppermute | solution.py:271
  93.5 2.0 %collective-permute-done.30.refs_2_ = bf16[256,128]{1,0:T(8,128)(2,1)S(1)} collective-permute-done((bf16[256,128]{1,0:T(8,128)(2,1)S(1)}, bf16[256,128]{1,0:T(8,128)(2,1)S(1)}, u32[]{:S(2)}, u32[]{:S(2)}) %collective-permute-start.30) | collective-permute-done | bytes 65568 | tf_op jit(solution)/shard_map/ppermute | solution.py:271
  95.5 1.7 %collective-permute-done.31.refs_3_ = bf16[256,128]{1,0:T(8,128)(2,1)S(1)} collective-permute-done((bf16[256,128]{1,0:T(8,128)(2,1)S(1)}, bf16[256,128]{1,0:T(8,128)(2,1)S(1)}, u32[]{:S(2)}, u32[]{:S(2)}) %collective-permute-start.31) | collective-permute-done | bytes 65568 | tf_op jit(solution)/shard_map/ppermute | solution.py:271
  97.2 1.0 shard_map.97
  (60 shorter events, 11.4 us)
Async XLA Ops:
  2.8 9.1 %collective-permute-start = (bf16[384,256]{1,0:T(8,128)(2,1)}, bf16[384,256]{1,0:T(8,128)(2,1)S(1)}, u32[]{:S(2)}, u32[]{:S(2)}) collective-permute-start(bf16[384,256]{1,0:T(8,128)(2,1)} %get-tuple-element.55), channel_id=1, source_target_pairs={{0,2},{1,3},{2,0},{3,1},{4,6},{5,7},{6,4},{7,5},{8,10},{9,11},{10,... | collective-permute-start | bytes 589832 | tf_op jit(solution)/shard_map/ppermute | solution.py:271
  5.8 12.2 %collective-permute-start.1 = (bf16[384,256]{1,0:T(8,128)(2,1)}, bf16[384,256]{1,0:T(8,128)(2,1)S(1)}, u32[]{:S(2)}, u32[]{:S(2)}) collective-permute-start(bf16[384,256]{1,0:T(8,128)(2,1)} %get-tuple-element.56), channel_id=1, source_target_pairs={{0,4},{1,5},{2,6},{3,7},{4,0},{5,1},{6,2},{7,3},{8,12},{9,13},{10,... | collective-permute-start | bytes 589832 | tf_op jit(solution)/shard_map/ppermute | solution.py:271
  7.3 10.7 %collective-permute-start.2 = (bf16[384,256]{1,0:T(8,128)(2,1)}, bf16[384,256]{1,0:T(8,128)(2,1)S(1)}, u32[]{:S(2)}, u32[]{:S(2)}) collective-permute-start(bf16[384,256]{1,0:T(8,128)(2,1)} %get-tuple-element.57), channel_id=1, source_target_pairs={{0,6},{1,7},{2,4},{3,5},{4,2},{5,3},{6,0},{7,1},{8,14},{9,15},{10,... | collective-permute-start | bytes 589832 | tf_op jit(solution)/shard_map/ppermute | solution.py:271
  7.4 31.7 %collective-permute-start.4 = (bf16[128,4096]{1,0:T(8,128)(2,1)}, bf16[128,4096]{1,0:T(8,128)(2,1)S(1)}, u32[]{:S(2)}, u32[]{:S(2)}) collective-permute-start(bf16[128,4096]{1,0:T(8,128)(2,1)} %refs_0_.4), channel_id=1, source_target_pairs={{0,4},{1,5},{2,6},{3,7},{4,0},{5,1},{6,2},{7,3},{8,12},{9,13},{10,... | collective-permute-start | bytes 3145736 | tf_op jit(solution)/shard_map/ppermute | solution.py:271
  9.3 29.7 %collective-permute-start.3 = (bf16[128,4096]{1,0:T(8,128)(2,1)}, bf16[128,4096]{1,0:T(8,128)(2,1)S(1)}, u32[]{:S(2)}, u32[]{:S(2)}) collective-permute-start(bf16[128,4096]{1,0:T(8,128)(2,1)} %refs_0_.4), channel_id=1, source_target_pairs={{0,2},{1,3},{2,0},{3,1},{4,6},{5,7},{6,4},{7,5},{8,10},{9,11},{10,... | collective-permute-start | bytes 3145736 | tf_op jit(solution)/shard_map/ppermute | solution.py:271
  18.3 14.9 %collective-permute-start.8 = (bf16[640,256]{1,0:T(8,128)(2,1)S(1)}, bf16[640,256]{1,0:T(8,128)(2,1)S(1)}, u32[]{:S(2)}, u32[]{:S(2)}) collective-permute-start(bf16[640,256]{1,0:T(8,128)(2,1)S(1)} %get-tuple-element.65.refs_9_), channel_id=1, source_target_pairs={{0,16},{1,17},{2,18},{3,19},{4,20},{5,21},{6,22},{7,23},{8,24},{9,... | collective-permute-start | bytes 983048 | tf_op jit(solution)/shard_map/ppermute | solution.py:271
  21.0 12.9 %collective-permute-start.7 = (bf16[640,256]{1,0:T(8,128)(2,1)S(1)}, bf16[640,256]{1,0:T(8,128)(2,1)S(1)}, u32[]{:S(2)}, u32[]{:S(2)}) collective-permute-start(bf16[640,256]{1,0:T(8,128)(2,1)S(1)} %get-tuple-element.65.refs_9_), channel_id=1, source_target_pairs={{0,8},{1,9},{2,10},{3,11},{4,12},{5,13},{6,14},{7,15},{8,0},{9,1},... | collective-permute-start | bytes 983048 | tf_op jit(solution)/shard_map/ppermute | solution.py:271
  33.3 8.5 %collective-permute-start.9 = (bf16[640,256]{1,0:T(8,128)(2,1)S(1)}, bf16[640,256]{1,0:T(8,128)(2,1)S(1)}, u32[]{:S(2)}, u32[]{:S(2)}) collective-permute-start(bf16[640,256]{1,0:T(8,128)(2,1)S(1)} %collective-permute-done.8.refs_11_), channel_id=1, source_target_pairs={{0,8},{1,9},{2,10},{3,11},{4,12},{5,13},{6,14},{7,15},{8,0},{9,1},... | collective-permute-start | bytes 983048 | tf_op jit(solution)/shard_map/ppermute | solution.py:271
  33.9 7.9 %collective-permute-start.12 = (bf16[640,256]{1,0:T(8,128)(2,1)S(1)}, bf16[640,256]{1,0:T(8,128)(2,1)S(1)}, u32[]{:S(2)}, u32[]{:S(2)}) collective-permute-start(bf16[640,256]{1,0:T(8,128)(2,1)S(1)} %collective-permute-done.8.refs_11_), channel_id=1, source_target_pairs={{0,1},{1,0},{2,3},{3,2},{4,5},{5,4},{6,7},{7,6},{8,9},{9,8},{10,11... | collective-permute-start | bytes 983048 | tf_op jit(solution)/shard_map/ppermute | solution.py:271
  33.9 8.4 %collective-permute-start.11 = (bf16[640,256]{1,0:T(8,128)(2,1)S(1)}, bf16[640,256]{1,0:T(8,128)(2,1)S(1)}, u32[]{:S(2)}, u32[]{:S(2)}) collective-permute-start(bf16[640,256]{1,0:T(8,128)(2,1)S(1)} %collective-permute-done.7.refs_10_), channel_id=1, source_target_pairs={{0,1},{1,0},{2,3},{3,2},{4,5},{5,4},{6,7},{7,6},{8,9},{9,8},{10,11... | collective-permute-start | bytes 983048 | tf_op jit(solution)/shard_map/ppermute | solution.py:271
  39.2 12.5 %collective-permute-start.6 = (bf16[64,4096]{1,0:T(8,128)(2,1)S(1)}, bf16[64,4096]{1,0:T(8,128)(2,1)S(1)}, u32[]{:S(2)}, u32[]{:S(2)}) collective-permute-start(bf16[64,4096]{1,0:T(8,128)(2,1)S(1)} %slice.7), channel_id=1, source_target_pairs={{0,2},{1,3},{2,0},{3,1},{4,6},{5,7},{6,4},{7,5},{8,10},{9,11},{10,... | collective-permute-start | bytes 1572872 | tf_op jit(solution)/shard_map/ppermute | solution.py:271
  39.6 12.5 %collective-permute-start.5 = (bf16[64,4096]{1,0:T(8,128)(2,1)S(1)}, bf16[64,4096]{1,0:T(8,128)(2,1)S(1)}, u32[]{:S(2)}, u32[]{:S(2)}) collective-permute-start(bf16[64,4096]{1,0:T(8,128)(2,1)S(1)} %slice.6), channel_id=1, source_target_pairs={{0,4},{1,5},{2,6},{3,7},{4,0},{5,1},{6,2},{7,3},{8,12},{9,13},{10,... | collective-permute-start | bytes 1572872 | tf_op jit(solution)/shard_map/ppermute | solution.py:271
  41.8 1.6 %collective-permute-start.13 = (bf16[640,256]{1,0:T(8,128)(2,1)S(1)}, bf16[640,256]{1,0:T(8,128)(2,1)S(1)}, u32[]{:S(2)}, u32[]{:S(2)}) collective-permute-start(bf16[640,256]{1,0:T(8,128)(2,1)S(1)} %collective-permute-done.9.refs_12_), channel_id=1, source_target_pairs={{0,1},{1,0},{2,3},{3,2},{4,5},{5,4},{6,7},{7,6},{8,9},{9,8},{10,11... | collective-permute-start | bytes 983048 | tf_op jit(solution)/shard_map/ppermute | solution.py:271
  41.8 2.5 %collective-permute-start.10 = (bf16[640,256]{1,0:T(8,128)(2,1)S(1)}, bf16[640,256]{1,0:T(8,128)(2,1)S(1)}, u32[]{:S(2)}, u32[]{:S(2)}) collective-permute-start(bf16[640,256]{1,0:T(8,128)(2,1)S(1)} %get-tuple-element.65.refs_9_), channel_id=1, source_target_pairs={{0,1},{1,0},{2,3},{3,2},{4,5},{5,4},{6,7},{7,6},{8,9},{9,8},{10,11... | collective-permute-start | bytes 983048 | tf_op jit(solution)/shard_map/ppermute | solution.py:271
  42.3 2.0 %collective-permute-start.14 = (bf16[4,256,128]{2,1,0:T(8,128)(2,1)S(1)}, bf16[4,256,128]{2,1,0:T(8,128)(2,1)S(1)}, u32[]{:S(2)}, u32[]{:S(2)}) collective-permute-start(bf16[4,256,128]{2,1,0:T(8,128)(2,1)S(1)} %get-tuple-element.66.refs_17_), channel_id=1, source_target_pairs={{0,1},{1,0},{2,3},{3,2},{4,5},{5,4},{6,7},{7,6},{8,9},{9,8},{10,11... | collective-permute-start | bytes 786440 | tf_op jit(solution)/shard_map/ppermute | solution.py:271
  56.8 3.6 %collective-permute-start.15 = (bf16[4,256,128]{2,1,0:T(8,128)(2,1)S(1)}, bf16[4,256,128]{2,1,0:T(8,128)(2,1)S(1)}, u32[]{:S(2)}, u32[]{:S(2)}) collective-permute-start(bf16[4,256,128]{2,1,0:T(8,128)(2,1)S(1)} %get-tuple-element.74.own.refs_7_), channel_id=1, source_target_pairs={{0,1},{1,0},{2,3},{3,2},{4,5},{5,4},{6,7},{7,6},{8,9},{9,8},{10,11... | collective-permute-start | bytes 786440 | tf_op jit(solution)/shard_map/ppermute | solution.py:271
  57.3 4.4 %collective-permute-start.26 = (bf16[256,512]{1,0:T(8,128)(2,1)S(1)}, bf16[256,512]{1,0:T(8,128)(2,1)S(1)}, u32[]{:S(2)}, u32[]{:S(2)}) collective-permute-start(bf16[256,512]{1,0:T(8,128)(2,1)S(1)} %get-tuple-element.89), channel_id=1, source_target_pairs={{0,1},{1,0},{2,3},{3,2},{4,5},{5,4},{6,7},{7,6},{8,9},{9,8},{10,11... | collective-permute-start | bytes 786440 | tf_op jit(solution)/shard_map/ppermute | solution.py:271
  58.4 15.1 %collective-permute-start.25 = (bf16[256,512]{1,0:T(8,128)(2,1)S(1)}, bf16[256,512]{1,0:T(8,128)(2,1)S(1)}, u32[]{:S(2)}, u32[]{:S(2)}) collective-permute-start(bf16[256,512]{1,0:T(8,128)(2,1)S(1)} %get-tuple-element.87), channel_id=1, source_target_pairs={{0,1},{1,0},{2,3},{3,2},{4,5},{5,4},{6,7},{7,6},{8,9},{9,8},{10,11... | collective-permute-start | bytes 786440 | tf_op jit(solution)/shard_map/ppermute | solution.py:271
  58.9 8.9 %collective-permute-start.23 = (bf16[256,512]{1,0:T(8,128)(2,1)S(1)}, bf16[256,512]{1,0:T(8,128)(2,1)S(1)}, u32[]{:S(2)}, u32[]{:S(2)}) collective-permute-start(bf16[256,512]{1,0:T(8,128)(2,1)S(1)} %get-tuple-element.85), channel_id=1, source_target_pairs={{0,1},{1,0},{2,3},{3,2},{4,5},{5,4},{6,7},{7,6},{8,9},{9,8},{10,11... | collective-permute-start | bytes 786440 | tf_op jit(solution)/shard_map/ppermute | solution.py:271
  60.0 18.6 %collective-permute-start.22 = (bf16[256,512]{1,0:T(8,128)(2,1)S(1)}, bf16[256,512]{1,0:T(8,128)(2,1)S(1)}, u32[]{:S(2)}, u32[]{:S(2)}) collective-permute-start(bf16[256,512]{1,0:T(8,128)(2,1)S(1)} %get-tuple-element.82), channel_id=1, source_target_pairs={{0,1},{1,0},{2,3},{3,2},{4,5},{5,4},{6,7},{7,6},{8,9},{9,8},{10,11... | collective-permute-start | bytes 786440 | tf_op jit(solution)/shard_map/ppermute | solution.py:271
  60.5 6.1 %collective-permute-start.16 = (bf16[128,128]{1,0:T(8,128)(2,1)S(1)}, bf16[128,128]{1,0:T(8,128)(2,1)S(1)}, u32[]{:S(2)}, u32[]{:S(2)}) collective-permute-start(bf16[128,128]{1,0:T(8,128)(2,1)S(1)} %shard_map.89), channel_id=1, source_target_pairs={{8,0},{9,1},{10,2},{11,3},{12,4},{13,5},{14,6},{15,7},{16,8},{17,9... | collective-permute-start | bytes 98312 | tf_op jit(solution)/shard_map/ppermute | solution.py:283
  61.8 11.6 %collective-permute-start.27 = (bf16[256,512]{1,0:T(8,128)(2,1)S(1)}, bf16[256,512]{1,0:T(8,128)(2,1)S(1)}, u32[]{:S(2)}, u32[]{:S(2)}) collective-permute-start(bf16[256,512]{1,0:T(8,128)(2,1)S(1)} %add_convert_fusion.1), channel_id=1, source_target_pairs={{0,8},{1,9},{2,10},{3,11},{4,12},{5,13},{6,14},{7,15},{8,0},{9,1},... | collective-permute-start | bytes 786440 | tf_op jit(solution)/shard_map/ppermute | solution.py:271
  66.5 6.8 %collective-permute-start.17 = (bf16[128,128]{1,0:T(8,128)(2,1)S(1)}, bf16[128,128]{1,0:T(8,128)(2,1)S(1)}, u32[]{:S(2)}, u32[]{:S(2)}) collective-permute-start(bf16[128,128]{1,0:T(8,128)(2,1)S(1)} %fusion), channel_id=1, source_target_pairs={{16,0},{17,1},{18,2},{19,3},{20,4},{21,5},{22,6},{23,7},{24,8},{25... | collective-permute-start | bytes 98312 | tf_op jit(solution)/shard_map/ppermute | solution.py:283
  67.9 17.0 %collective-permute-start.24 = (bf16[256,512]{1,0:T(8,128)(2,1)S(1)}, bf16[256,512]{1,0:T(8,128)(2,1)S(1)}, u32[]{:S(2)}, u32[]{:S(2)}) collective-permute-start(bf16[256,512]{1,0:T(8,128)(2,1)S(1)} %add_convert_fusion.2), channel_id=1, source_target_pairs={{0,8},{1,9},{2,10},{3,11},{4,12},{5,13},{6,14},{7,15},{8,0},{9,1},... | collective-permute-start | bytes 786440 | tf_op jit(solution)/shard_map/ppermute | solution.py:271
  73.4 1.6 %collective-permute-start.18 = (bf16[128,128]{1,0:T(8,128)(2,1)S(1)}, bf16[128,128]{1,0:T(8,128)(2,1)S(1)}, u32[]{:S(2)}, u32[]{:S(2)}) collective-permute-start(bf16[128,128]{1,0:T(8,128)(2,1)S(1)} %fusion.1.refs_9_), channel_id=1, source_target_pairs={{0,1},{1,0},{2,3},{3,2},{4,5},{5,4},{6,7},{7,6},{8,9},{9,8},{10,11... | collective-permute-start | bytes 98312 | tf_op jit(solution)/shard_map/ppermute | solution.py:271
  73.6 15.3 %collective-permute-start.28 = (bf16[256,512]{1,0:T(8,128)(2,1)S(1)}, bf16[256,512]{1,0:T(8,128)(2,1)S(1)}, u32[]{:S(2)}, u32[]{:S(2)}) collective-permute-start(bf16[256,512]{1,0:T(8,128)(2,1)S(1)} %add_convert_fusion), channel_id=1, source_target_pairs={{0,16},{1,17},{2,18},{3,19},{4,20},{5,21},{6,22},{7,23},{8,24},{9,... | collective-permute-start | bytes 786440 | tf_op jit(solution)/shard_map/ppermute | solution.py:271
  75.7 5.8 %collective-permute-start.19 = (bf16[128,512]{1,0:T(8,128)(2,1)S(1)}, bf16[128,512]{1,0:T(8,128)(2,1)S(1)}, u32[]{:S(2)}, u32[]{:S(2)}) collective-permute-start(bf16[128,512]{1,0:T(8,128)(2,1)S(1)} %get-tuple-element.76), channel_id=1, source_target_pairs={{0,2},{1,3},{2,0},{3,1},{4,6},{5,7},{6,4},{7,5},{8,10},{9,11},{10,... | collective-permute-start | bytes 393224 | tf_op jit(solution)/shard_map/ppermute | solution.py:271
  77.1 7.8 %collective-permute-start.20 = (bf16[128,512]{1,0:T(8,128)(2,1)S(1)}, bf16[128,512]{1,0:T(8,128)(2,1)S(1)}, u32[]{:S(2)}, u32[]{:S(2)}) collective-permute-start(bf16[128,512]{1,0:T(8,128)(2,1)S(1)} %get-tuple-element.77), channel_id=1, source_target_pairs={{0,4},{1,5},{2,6},{3,7},{4,0},{5,1},{6,2},{7,3},{8,12},{9,13},{10,... | collective-permute-start | bytes 393224 | tf_op jit(solution)/shard_map/ppermute | solution.py:271
  78.6 6.3 %collective-permute-start.21 = (bf16[128,512]{1,0:T(8,128)(2,1)S(1)}, bf16[128,512]{1,0:T(8,128)(2,1)S(1)}, u32[]{:S(2)}, u32[]{:S(2)}) collective-permute-start(bf16[128,512]{1,0:T(8,128)(2,1)S(1)} %get-tuple-element.78), channel_id=1, source_target_pairs={{0,6},{1,7},{2,4},{3,5},{4,2},{5,3},{6,0},{7,1},{8,14},{9,15},{10,... | collective-permute-start | bytes 393224 | tf_op jit(solution)/shard_map/ppermute | solution.py:271
  89.1 4.4 %collective-permute-start.29 = (bf16[256,128]{1,0:T(8,128)(2,1)S(1)}, bf16[256,128]{1,0:T(8,128)(2,1)S(1)}, u32[]{:S(2)}, u32[]{:S(2)}) collective-permute-start(bf16[256,128]{1,0:T(8,128)(2,1)S(1)} %get-tuple-element.91), channel_id=1, source_target_pairs={{0,2},{1,3},{2,0},{3,1},{4,6},{5,7},{6,4},{7,5},{8,10},{9,11},{10,... | collective-permute-start | bytes 196616 | tf_op jit(solution)/shard_map/ppermute | solution.py:271
  90.5 5.0 %collective-permute-start.30 = (bf16[256,128]{1,0:T(8,128)(2,1)S(1)}, bf16[256,128]{1,0:T(8,128)(2,1)S(1)}, u32[]{:S(2)}, u32[]{:S(2)}) collective-permute-start(bf16[256,128]{1,0:T(8,128)(2,1)S(1)} %get-tuple-element.92), channel_id=1, source_target_pairs={{0,4},{1,5},{2,6},{3,7},{4,0},{5,1},{6,2},{7,3},{8,12},{9,13},{10,... | collective-permute-start | bytes 196616 | tf_op jit(solution)/shard_map/ppermute | solution.py:271
  92.1 5.2 %collective-permute-start.31 = (bf16[256,128]{1,0:T(8,128)(2,1)S(1)}, bf16[256,128]{1,0:T(8,128)(2,1)S(1)}, u32[]{:S(2)}, u32[]{:S(2)}) collective-permute-start(bf16[256,128]{1,0:T(8,128)(2,1)S(1)} %get-tuple-element.93), channel_id=1, source_target_pairs={{0,6},{1,7},{2,4},{3,5},{4,2},{5,3},{6,0},{7,1},{8,14},{9,15},{10,... | collective-permute-start | bytes 196616 | tf_op jit(solution)/shard_map/ppermute | solution.py:271
  (3 other events, 27.0 us)

commit v4 on v3

--- a/solution.py
+++ b/solution.py
@@ -107,12 +107,42 @@
     return (there < here).astype(jnp.int32).astype(F32)
 
 
+def causal_mask(rows):
+    return lax.broadcasted_iota(jnp.int32, (rows, rows), 0) >= lax.broadcasted_iota(
+        jnp.int32, (rows, rows), 1
+    )
+
+
+def attend_block(j, rows, depth, query, p, prior_high, prior_low, outs):
+    att, dq_t, grown, feats_out, d_num_out, scores_out, mixed_out = outs
+    causal = causal_mask(rows)
+    feats = jnp.maximum(query, 0.0).astype(BF16)
+    keys = jnp.maximum(p[depth : depth + rows, :], 0)
+    vals = p[depth + rows :, :HEAD_DIM]
+    grad = p[depth + rows :, HEAD_DIM:].astype(F32)
+    scores = jnp.where(causal, dot(feats, keys, ((1,), (1,))), 0.0).astype(BF16)
+    numer = dot(scores, vals) + dot(feats, prior_high) + dot(feats, prior_low)
+    inv = lax.rsqrt(jnp.mean(numer * numer, axis=-1, keepdims=True) + EPSILON)
+    normed = numer * inv
+    att[j] = normed.astype(BF16)
+    d_num = (inv * (grad - normed * jnp.mean(grad * normed, axis=-1, keepdims=True))).astype(BF16)
+    mixed = jnp.where(causal, dot(d_num, vals, ((1,), (1,))), 0.0).astype(BF16)
+    d_feat = dot(mixed, keys) + dot(d_num, prior_high, ((1,), (1,))) + dot(d_num, prior_low, ((1,), (1,)))
+    d_query = jnp.where(query > 0, d_feat, 0.0)
+    dq_t[:, j * rows : (j + 1) * rows] = d_query.T.astype(BF16)
+    grown[j] = dot(feats, d_num, ((0,), (0,))).astype(BF16)
+    feats_out[j] = feats
+    d_num_out[j] = d_num
+    scores_out[j] = scores
+    mixed_out[j] = mixed
+
+
 def attend_kernel(rows, depth, outer, place, *refs):
-    h, refs = refs[:5], refs[5:]
-    p, refs = refs[:4], refs[4:]
+    h, refs = refs[:3], refs[3:]
+    p, refs = refs[:3], refs[3:]
     own_pay, refs = refs[:outer], refs[outer:]
     other_pay, refs = refs[:outer], refs[outer:]
-    own_states, other_states, att, dq_t, grown, feats_out, d_num_out, scores_out, mixed_out, weights, proj = refs
+    own_states, other_states, *outs, weights, last_high, last_low, proj = refs
     q, z, core = seat(place)
     base = jnp.zeros((FEAT, HEAD_DIM), F32)
     for k in range(outer):
@@ -135,9 +165,6 @@
             proj[...] = part
     own = [own_states[j].astype(F32) for j in range(4)]
     other = [other_states[j].astype(F32) for j in range(4)]
-    causal = lax.broadcasted_iota(jnp.int32, (rows, rows), 0) >= lax.broadcasted_iota(
-        jnp.int32, (rows, rows), 1
-    )
     for j in range(4):
         here = (q ^ j) * CORES + core
         prior = base
@@ -146,48 +173,37 @@
                 if flip == 0 and i == j:
                     continue
                 prior = prior + before((q ^ i) * CORES + (core ^ flip), here) * group[i]
-        prior_high, prior_low = split(prior)
-        block = slice(j * rows, (j + 1) * rows)
-        query = proj[block, :]
-        feats = jnp.maximum(query, 0.0).astype(BF16)
-        keys = jnp.maximum(p[j][depth : depth + rows, :], 0)
-        vals = p[j][depth + rows :, :HEAD_DIM]
-        grad = p[j][depth + rows :, HEAD_DIM:].astype(F32)
-        scores = jnp.where(causal, dot(feats, keys, ((1,), (1,))), 0.0).astype(BF16)
-        numer = dot(scores, vals) + dot(feats, prior_high) + dot(feats, prior_low)
-        inv = lax.rsqrt(jnp.mean(numer * numer, axis=-1, keepdims=True) + EPSILON)
-        normed = numer * inv
-        att[j] = normed.astype(BF16)
-        d_num = (inv * (grad - normed * jnp.mean(grad * normed, axis=-1, keepdims=True))).astype(BF16)
-        mixed = jnp.where(causal, dot(d_num, vals, ((1,), (1,))), 0.0).astype(BF16)
-        d_feat = dot(mixed, keys) + dot(d_num, prior_high, ((1,), (1,))) + dot(d_num, prior_low, ((1,), (1,)))
-        d_query = jnp.where(query > 0, d_feat, 0.0)
-        dq_t[:, block] = d_query.T.astype(BF16)
-        grown[j] = dot(feats, d_num, ((0,), (0,))).astype(BF16)
-        feats_out[j] = feats
-        d_num_out[j] = d_num
-        scores_out[j] = scores
-        mixed_out[j] = mixed
-
-
-def half_kernel(place, own, other, half, total):
+        high, low = split(prior)
+        if j < 3:
+            attend_block(j, rows, depth, proj[j * rows : (j + 1) * rows, :], p[j], high, low, outs)
+        else:
+            last_high[...] = high
+            last_low[...] = low
+
+
+def last_kernel(rows, depth, place, top, bottom, weights, p, high, low, *outs):
+    query = dot(jnp.concatenate([top[...], bottom[...]], axis=0), weights[...])
+    attend_block(0, rows, depth, query, p, high[...], low[...], outs)
+
+
+def half_kernel(place, *refs):
+    *parts, half, total = refs
     _, _, core = seat(place)
-    total[...] = sum(ref[j].astype(F32) for ref in (own, other) for j in range(4))
+    total[...] = sum(ref[j].astype(F32) for ref in parts for j in range(ref.shape[0]))
     half[...] = total[pl.ds(pl.multiple_of(core * HALF, HALF), HALF), :].astype(BF16)
 
 
-def side_kernel(rows, place, feats, d_num, scores, mixed, val_part, key_part):
-    for j in range(4):
-        block = slice(j * rows, (j + 1) * rows)
-        val_part[block, :] = dot(scores[j], d_num[j], ((0,), (0,)))
-        key_part[block, :] = dot(mixed[j], feats[j], ((0,), (0,)))
+def side_kernel(place, feats, d_num, scores, mixed, val_part, key_part):
+    for j in range(feats.shape[0]):
+        val_part[j] = dot(scores[j], d_num[j], ((0,), (0,)))
+        key_part[j] = dot(mixed[j], feats[j], ((0,), (0,)))
 
 
 def grad_kernel(depth, k, place, *refs):
-    *h, dq_t, keep, give = refs
+    *h, dq_first, dq_last, keep, give = refs
     _, z, core = seat(place)
     pair = CORES * depth
-    lhs = dq_t[...]
+    lhs = jnp.concatenate([dq_first[...], dq_last[...]], axis=1)
     for i in range(4):
         start = pl.multiple_of(((z ^ k) * 4 + i) * pair, pair)
         out = dot(lhs, hidden_columns(h, start, pair))
@@ -219,13 +235,16 @@
 
 def finish_kernel(rows, depth, outer, place, *refs):
     p, refs = refs[:4], refs[4:]
-    att, val_part, key_part, own_grown, other_grown, own_rest, other_rest, *outs, rest = refs
+    pairs, (own_rest, other_rest, *outs, rest) = refs[:10], refs[10:]
+    att, val_part, key_part, own_grown, other_grown = (
+        [*(first.at[j] for j in range(3)), last.at[0]] for first, last in zip(pairs[:5], pairs[5:])
+    )
     q, _, core = seat(place)
     for flip, ref in ((0, own_rest), (1, other_rest)):
         rest[pl.ds(pl.multiple_of((core ^ flip) * HALF, HALF), HALF), :] = ref[...].astype(F32)
     base = rest[...]
-    own = [own_grown[j].astype(F32) for j in range(4)]
-    other = [other_grown[j].astype(F32) for j in range(4)]
+    own = [ref[...].astype(F32) for ref in own_grown]
+    other = [ref[...].astype(F32) for ref in other_grown]
     for j, out in enumerate(outs):
         here = (q ^ j) * CORES + core
         later = base
@@ -235,13 +254,12 @@
                     continue
                 later = later + before(here, (q ^ i) * CORES + (core ^ flip)) * group[i]
         high, low = split(later)
-        block = slice(j * rows, (j + 1) * rows)
         raw = p[j][depth : depth + rows, :]
         keys = jnp.maximum(raw, 0)
         vals = p[j][depth + rows :, :HEAD_DIM]
-        d_val = val_part[block, :] + dot(keys, high) + dot(keys, low)
-        d_key = key_part[block, :] + dot(vals, high, ((1,), (1,))) + dot(vals, low, ((1,), (1,)))
-        out[:, :HEAD_DIM] = att[j]
+        d_val = val_part[j][...] + dot(keys, high) + dot(keys, low)
+        d_key = key_part[j][...] + dot(vals, high, ((1,), (1,))) + dot(vals, low, ((1,), (1,)))
+        out[:, :HEAD_DIM] = att[j][...]
         out[:, HEAD_DIM : 2 * HEAD_DIM] = d_val.astype(BF16)
         out[:, 2 * HEAD_DIM :] = jnp.where(raw.astype(F32) > 0, d_key, 0.0).astype(BF16)
 
@@ -313,44 +331,66 @@
     other_pays = [core_swap(late_pay)] + [core_swap(pays[k]) for k in range(1, outer)]
     other_states = core_swap(late_states)
     positions = 4 * rows
-    att, dq_t, grown, *kept = call(
+
+    def kept(blocks):
+        return [
+            ((blocks, rows, HEAD_DIM), BF16),
+            ((FEAT, blocks * rows), BF16),
+            ((blocks, FEAT, HEAD_DIM), BF16),
+            ((blocks, rows, FEAT), BF16),
+            ((blocks, rows, HEAD_DIM), BF16),
+            ((blocks, rows, rows), BF16),
+            ((blocks, rows, rows), BF16),
+        ]
+
+    def side(parts):
+        blocks = parts[0].shape[0]
+        return call(
+            side_kernel,
+            [((blocks, rows, HEAD_DIM), F32), ((blocks, rows, FEAT), F32)],
+            [place, *parts],
+            flops=6 * blocks * rows * FEAT * HEAD_DIM,
+        )
+
+    *first, weights, high, low = call(
         functools.partial(attend_kernel, rows, depth, outer),
-        [
-            ((4, rows, HEAD_DIM), BF16),
-            ((FEAT, positions), BF16),
-            ((4, FEAT, HEAD_DIM), BF16),
-            ((4, rows, FEAT), BF16),
-            ((4, rows, HEAD_DIM), BF16),
-            ((4, rows, rows), BF16),
-            ((4, rows, rows), BF16),
-        ],
-        [place, *h, *p, *pays, *other_pays, states, other_states],
-        flops=2 * positions * width * FEAT + 24 * positions * FEAT * HEAD_DIM,
-        scratch=[pltpu.VMEM((width, FEAT), BF16), pltpu.VMEM((positions, FEAT), F32)],
-    )
-    other_grown = core_swap(grown)
+        kept(3) + [((width, FEAT), BF16), ((FEAT, HEAD_DIM), BF16), ((FEAT, HEAD_DIM), BF16)],
+        [place, hidden, h1, h2, *p[:3], *pays, *other_pays, states, other_states],
+        flops=2 * 3 * rows * width * FEAT,
+        scratch=[pltpu.VMEM((3 * rows, FEAT), F32)],
+    )
+    last = call(
+        functools.partial(last_kernel, rows, depth),
+        kept(1),
+        [place, *h3, weights, p[3], high, low],
+        flops=2 * rows * width * FEAT,
+    )
+    others = [core_swap(first[2]), core_swap(last[2])]
     (half,) = call(
         half_kernel,
         [((HALF, HEAD_DIM), BF16)],
-        [place, grown, other_grown],
+        [place, first[2], last[2], *others],
         scratch=[pltpu.VMEM((FEAT, HEAD_DIM), F32)],
     )
+    sums = [None] * outer
+    order = sorted(range(outer), key=lambda k: (-k.bit_count(), k))
+    dq_first, dq_last = first[1], last[1]
+    for k in order:
+        keep, give = call(
+            functools.partial(grad_kernel, depth, k),
+            [((FEAT, 4 * depth), F32), ((FEAT, 4 * depth), BF16)],
+            [place, *h, dq_first, dq_last],
+            flops=2 * positions * width * FEAT // outer,
+        )
+        sums[k] = keep + core_swap(give).astype(F32)
+        if k == order[0]:
+            sums[k], half = lax.optimization_barrier((sums[k].astype(BF16), half))
     rest, window, step = jnp.zeros(half.shape, F32), half, 1
     while step < outer:
         came = down(window, step)
         rest = rest + came.astype(F32)
         window = (window.astype(F32) + came.astype(F32)).astype(BF16)
         step *= 2
-    sums = [None] * outer
-    order = sorted(range(outer), key=lambda k: (-k.bit_count(), k))
-    for k in order:
-        keep, give = call(
-            functools.partial(grad_kernel, depth, k),
-            [((FEAT, 4 * depth), F32), ((FEAT, 4 * depth), BF16)],
-            [place, *h, dq_t],
-            flops=2 * positions * width * FEAT // outer,
-        )
-        sums[k] = keep + core_swap(give).astype(F32)
     arrived = []
     for k in order[:-1]:
         came, onward = plane_swap(sums[k].astype(BF16), k & -k), k & k - 1
@@ -359,18 +399,19 @@
         else:
             arrived.append(came)
     own = sums[0]
-    val_part, key_part = call(
-        functools.partial(side_kernel, rows),
-        [((positions, HEAD_DIM), F32), ((positions, FEAT), F32)],
-        [place, *kept],
-        flops=6 * positions * FEAT * HEAD_DIM,
-    )
     rest = rest.astype(BF16)
     other_rest = core_swap(rest)
     outs = call(
         functools.partial(finish_kernel, rows, depth, outer),
         [((rows, 2 * HEAD_DIM + FEAT), BF16)] * 4,
-        [place, *p, att, val_part, key_part, grown, other_grown, rest, other_rest],
+        [
+            place,
+            *p,
+            *(first[0], *side(first[3:]), first[2], others[0]),
+            *(last[0], *side(last[3:]), last[2], others[1]),
+            rest,
+            other_rest,
+        ],
         flops=16 * positions * FEAT * HEAD_DIM,
         scratch=[pltpu.VMEM((FEAT, HEAD_DIM), F32)],
     )

time: 98.4 us -> 93.7 us (0.952)
  waiting for transfers between devices: 51.2 us -> 44.2 us
  starting transfers between devices: 32.6 us -> 34.3 us
    ppermute x30 -> x31, waiting for transfers between devices: 45.1 us -> 40.3 us  [swap(): return lax.ppermute(block, 'ctx', [(i, i ^ bits) for i in range(count)])]
    ppermute x2, waiting for transfers between devices: 6.05 us -> 3.84 us  [down(): lax.ppermute(block, 'ctx', [(i, i - inner * k) for i in range(inner * k,...]
    ppermute x30 -> x31, starting transfers between devices: 30.1 us -> 31.7 us  [swap(): return lax.ppermute(block, 'ctx', [(i, i ^ bits) for i in range(count)])]
    pallas_call x14 -> x16, Pallas kernels: 12.2 us -> 12.8 us  [call(): pl.pallas_call(kernel, out_shape=shapes, in_specs=[pl.BlockSpec(memory_sp...]
  transfers between devices with their start and end apart: 32 -> 33, of which waited for: 15 -> 18; matrix products, arithmetic and copies ran while one was open for 0% -> 0% of each run, Pallas kernels for 4% -> 8%
where the time goes in v4:
time: 93.7 us; the launch traced here: 93.5 us
  waiting for transfers between devices  44.2 us (47%)
  starting transfers between devices  34.3 us (37%)
  Pallas kernels  12.8 us (14%)
  local copies, waits for them, and re-layouts  1.01 us (1%)
    ppermute x31, waiting for transfers between devices, swap(): return lax.ppermute(block, 'ctx', [(i, i ^ bits) for i in range(count)])  40.3 us
    ppermute x31, starting transfers between devices, swap(): return lax.ppermute(block, 'ctx', [(i, i ^ bits) for i in range(count)])  31.7 us
    pallas_call x16, Pallas kernels, call(): pl.pallas_call(kernel, out_shape=shapes, in_specs=[pl.BlockSpec(memory_sp...  12.8 us
    ppermute x2, waiting for transfers between devices, down(): lax.ppermute(block, 'ctx', [(i, i - inner * k) for i in range(inner * k,...  3.84 us
    ppermute x2, starting transfers between devices, down(): lax.ppermute(block, 'ctx', [(i, i - inner * k) for i in range(inner * k,...  2.58 us
  transfers between devices with their start and end apart: 33, of which 18 were waited for; matrix products, arithmetic and copies ran while one was open for 0% of the time, Pallas kernels for 8%

profile of v4, /device:TPU:0, one launch (start us, length us, event | category | flops | bytes accessed | tf_op | source)
XLA Modules:
  0.0 93.5 jit_solution(9863417405735447255)
XLA Ops:
  0.6 2.2 %shard_map.84 = (bf16[384,256]{1,0:T(8,128)(2,1)}, bf16[384,256]{1,0:T(8,128)(2,1)}, bf16[384,256]{1,0:T(8,128)(2,1)}, bf16[384,256]{1,0:T(8,128)(2,1)}) custom-call(s32[1]{0:T(128)} %bitcast.place, bf16[128,1024]{1,0:T(8,128)(2,1)} %w.1, bf16[128,1024]{1,0:T(8,128)(2,1)} %key.1, bf16[128,512]{1,0:T(8,128)(2,1)} %val.1, bf16[128,512]{1,0:T(8,128)(2,1)} %cot.1), custom_call_target="tpu_custom_call" | custom-call | bytes 1572868 | tf_op jit(solution)/shard_map/pallas_call | solution.py:40
  2.8 3.0 %collective-permute-start = (bf16[384,256]{1,0:T(8,128)(2,1)}, bf16[384,256]{1,0:T(8,128)(2,1)S(1)}, u32[]{:S(2)}, u32[]{:S(2)}) collective-permute-start(bf16[384,256]{1,0:T(8,128)(2,1)} %get-tuple-element.69), channel_id=1, source_target_pairs={{0,2},{1,3},{2,0},{3,1},{4,6},{5,7},{6,4},{7,5},{8,10},{9,11},{10,... | collective-permute-start | bytes 589832 | tf_op jit(solution)/shard_map/ppermute | solution.py:289
  5.8 1.5 %collective-permute-start.1 = (bf16[384,256]{1,0:T(8,128)(2,1)}, bf16[384,256]{1,0:T(8,128)(2,1)S(1)}, u32[]{:S(2)}, u32[]{:S(2)}) collective-permute-start(bf16[384,256]{1,0:T(8,128)(2,1)} %get-tuple-element.70), channel_id=1, source_target_pairs={{0,4},{1,5},{2,6},{3,7},{4,0},{5,1},{6,2},{7,3},{8,12},{9,13},{10,... | collective-permute-start | bytes 589832 | tf_op jit(solution)/shard_map/ppermute | solution.py:289
  7.4 2.0 %collective-permute-start.4 = (bf16[128,4096]{1,0:T(8,128)(2,1)}, bf16[128,4096]{1,0:T(8,128)(2,1)S(1)}, u32[]{:S(2)}, u32[]{:S(2)}) collective-permute-start(bf16[128,4096]{1,0:T(8,128)(2,1)} %refs_0_.4), channel_id=1, source_target_pairs={{0,4},{1,5},{2,6},{3,7},{4,0},{5,1},{6,2},{7,3},{8,12},{9,13},{10,... | collective-permute-start | bytes 3145736 | tf_op jit(solution)/shard_map/ppermute | solution.py:289
  9.3 1.5 %collective-permute-start.3 = (bf16[128,4096]{1,0:T(8,128)(2,1)}, bf16[128,4096]{1,0:T(8,128)(2,1)S(1)}, u32[]{:S(2)}, u32[]{:S(2)}) collective-permute-start(bf16[128,4096]{1,0:T(8,128)(2,1)} %refs_0_.4), channel_id=1, source_target_pairs={{0,2},{1,3},{2,0},{3,1},{4,6},{5,7},{6,4},{7,5},{8,10},{9,11},{10,... | collective-permute-start | bytes 3145736 | tf_op jit(solution)/shard_map/ppermute | solution.py:289
  12.0 6.1 %collective-permute-done.1.p2.refs_5_.refs_2_ = bf16[384,256]{1,0:T(8,128)(2,1)S(1)} collective-permute-done((bf16[384,256]{1,0:T(8,128)(2,1)}, bf16[384,256]{1,0:T(8,128)(2,1)S(1)}, u32[]{:S(2)}, u32[]{:S(2)}) %collective-permute-start.1) | collective-permute-done | bytes 196640 | tf_op jit(solution)/shard_map/ppermute | solution.py:289
  18.3 2.7 %collective-permute-start.6 = (bf16[640,256]{1,0:T(8,128)(2,1)S(1)}, bf16[640,256]{1,0:T(8,128)(2,1)S(1)}, u32[]{:S(2)}, u32[]{:S(2)}) collective-permute-start(bf16[640,256]{1,0:T(8,128)(2,1)S(1)} %get-tuple-element.79.refs_6_), channel_id=1, source_target_pairs={{0,16},{1,17},{2,18},{3,19},{4,20},{5,21},{6,22},{7,23},{8,24},{9,... | collective-permute-start | bytes 983048 | tf_op jit(solution)/shard_map/ppermute | solution.py:289
  21.0 1.6 %collective-permute-start.5 = (bf16[640,256]{1,0:T(8,128)(2,1)S(1)}, bf16[640,256]{1,0:T(8,128)(2,1)S(1)}, u32[]{:S(2)}, u32[]{:S(2)}) collective-permute-start(bf16[640,256]{1,0:T(8,128)(2,1)S(1)} %get-tuple-element.79.refs_6_), channel_id=1, source_target_pairs={{0,8},{1,9},{2,10},{3,11},{4,12},{5,13},{6,14},{7,15},{8,0},{9,1},... | collective-permute-start | bytes 983048 | tf_op jit(solution)/shard_map/ppermute | solution.py:289
  22.6 10.7 %collective-permute-done.6.refs_8_ = bf16[640,256]{1,0:T(8,128)(2,1)S(1)} collective-permute-done((bf16[640,256]{1,0:T(8,128)(2,1)S(1)}, bf16[640,256]{1,0:T(8,128)(2,1)S(1)}, u32[]{:S(2)}, u32[]{:S(2)}) %collective-permute-start.6) | collective-permute-done | bytes 327712 | tf_op jit(solution)/shard_map/ppermute | solution.py:289
  34.4 4.7 %collective-permute-done.4.refs_2_ = bf16[128,4096]{1,0:T(8,128)(2,1)S(1)} collective-permute-done((bf16[128,4096]{1,0:T(8,128)(2,1)}, bf16[128,4096]{1,0:T(8,128)(2,1)S(1)}, u32[]{:S(2)}, u32[]{:S(2)}) %collective-permute-start.4) | collective-permute-done | bytes 1048608 | tf_op jit(solution)/shard_map/ppermute | solution.py:289
  39.6 1.7 %collective-permute-start.14 = (bf16[64,4096]{1,0:T(8,128)(2,1)S(1)}, bf16[64,4096]{1,0:T(8,128)(2,1)S(1)}, u32[]{:S(2)}, u32[]{:S(2)}) collective-permute-start(bf16[64,4096]{1,0:T(8,128)(2,1)S(1)} %slice.6), channel_id=1, source_target_pairs={{0,4},{1,5},{2,6},{3,7},{4,0},{5,1},{6,2},{7,3},{8,12},{9,13},{10,... | collective-permute-start | bytes 1572872 | tf_op jit(solution)/shard_map/ppermute | solution.py:289
  42.4 1.0 %collective-permute-done.11.refs_13_ = bf16[640,256]{1,0:T(8,128)(2,1)S(1)} collective-permute-done((bf16[640,256]{1,0:T(8,128)(2,1)S(1)}, bf16[640,256]{1,0:T(8,128)(2,1)S(1)}, u32[]{:S(2)}, u32[]{:S(2)}) %collective-permute-start.11) | collective-permute-done | bytes 327712 | tf_op jit(solution)/shard_map/ppermute | solution.py:289
  44.3 3.8 %shard_map.87 = (bf16[3,128,128]{2,1,0:T(8,128)(2,1)S(1)}, bf16[256,384]{1,0:T(8,128)(2,1)S(1)}, bf16[3,256,128]{2,1,0:T(8,128)(2,1)S(1)}, bf16[3,128,256]{2,1,0...) custom-call(s32[1]{0:T(128)} %bitcast.place, ...), custom_call_target="tpu_custom_call" | custom-call | flops 805306368 | bytes 10092548 | tf_op jit(solution)/shard_map/pallas_call | solution.py:40
  48.0 3.7 %collective-permute-done.15.bottom.refs_4_ = bf16[64,4096]{1,0:T(8,128)(2,1)S(1)} collective-permute-done((bf16[64,4096]{1,0:T(8,128)(2,1)S(1)}, bf16[64,4096]{1,0:T(8,128)(2,1)S(1)}, u32[]{:S(2)}, u32[]{:S(2)}) %collective-permute-start.15) | collective-permute-done | bytes 524320 | tf_op jit(solution)/shard_map/ppermute | solution.py:289
  52.1 1.3 %shard_map.89 = (bf16[1,128,128]{2,1,0:T(8,128)(2,1)S(1)}, bf16[256,128]{1,0:T(8,128)(2,1)S(1)}, bf16[1,256,128]{2,1,0:T(8,128)(2,1)S(1)}, bf16[1,128,256]{2,1,0...) custom-call(s32[1]{0:T(128)} %bitcast.place, ...), custom_call_target="tpu_custom_call" | custom-call | flops 268435456 | bytes 3801092 | tf_op jit(solution)/shard_map/pallas_call | solution.py:40
  56.1 1.3 %collective-permute-start.18 = (bf16[128,128]{1,0:T(8,128)(2,1)S(1)}, bf16[128,128]{1,0:T(8,128)(2,1)S(1)}, u32[]{:S(2)}, u32[]{:S(2)}) collective-permute-start(bf16[128,128]{1,0:T(8,128)(2,1)S(1)} %shard_map.92), channel_id=1, source_target_pairs={{8,0},{9,1},{10,2},{11,3},{12,4},{13,5},{14,6},{15,7},{16,8},{17,9... | collective-permute-start | bytes 98312 | tf_op jit(solution)/shard_map/ppermute | solution.py:301
  59.2 2.7 %collective-permute-start.28 = (bf16[256,512]{1,0:T(8,128)(2,1)S(1)}, bf16[256,512]{1,0:T(8,128)(2,1)S(1)}, u32[]{:S(2)}, u32[]{:S(2)}) collective-permute-start(bf16[256,512]{1,0:T(8,128)(2,1)S(1)} %add_convert_fusion.2), channel_id=1, source_target_pairs={{0,8},{1,9},{2,10},{3,11},{4,12},{5,13},{6,14},{7,15},{8,0},{9,1},... | collective-permute-start | bytes 786440 | tf_op jit(solution)/shard_map/ppermute | solution.py:289
  61.9 1.3 %collective-permute-start.19 = (bf16[128,128]{1,0:T(8,128)(2,1)S(1)}, bf16[128,128]{1,0:T(8,128)(2,1)S(1)}, u32[]{:S(2)}, u32[]{:S(2)}) collective-permute-start(bf16[128,128]{1,0:T(8,128)(2,1)S(1)} %fusion), channel_id=1, source_target_pairs={{16,0},{17,1},{18,2},{19,3},{20,4},{21,5},{22,6},{23,7},{24,8},{25... | collective-permute-start | bytes 98312 | tf_op jit(solution)/shard_map/ppermute | solution.py:301
  63.3 1.6 %collective-permute-start.26 = (bf16[256,512]{1,0:T(8,128)(2,1)S(1)}, bf16[256,512]{1,0:T(8,128)(2,1)S(1)}, u32[]{:S(2)}, u32[]{:S(2)}) collective-permute-start(bf16[256,512]{1,0:T(8,128)(2,1)S(1)} %add_convert_fusion.1), channel_id=1, source_target_pairs={{0,8},{1,9},{2,10},{3,11},{4,12},{5,13},{6,14},{7,15},{8,0},{9,1},... | collective-permute-start | bytes 786440 | tf_op jit(solution)/shard_map/ppermute | solution.py:289
  64.9 3.8 %collective-permute-done.19 = bf16[128,128]{1,0:T(8,128)(2,1)S(1)} collective-permute-done((bf16[128,128]{1,0:T(8,128)(2,1)S(1)}, bf16[128,128]{1,0:T(8,128)(2,1)S(1)}, u32[]{:S(2)}, u32[]{:S(2)}) %collective-permute-start.19) | collective-permute-done | bytes 32800 | tf_op jit(solution)/shard_map/ppermute | solution.py:301
  69.8 2.4 %collective-permute-start.29 = (bf16[256,512]{1,0:T(8,128)(2,1)S(1)}, bf16[256,512]{1,0:T(8,128)(2,1)S(1)}, u32[]{:S(2)}, u32[]{:S(2)}) collective-permute-start(bf16[256,512]{1,0:T(8,128)(2,1)S(1)} %add_convert_fusion), channel_id=1, source_target_pairs={{0,16},{1,17},{2,18},{3,19},{4,20},{5,21},{6,22},{7,23},{8,24},{9,... | collective-permute-start | bytes 786440 | tf_op jit(solution)/shard_map/ppermute | solution.py:289
  72.9 1.5 %collective-permute-start.21 = (bf16[128,512]{1,0:T(8,128)(2,1)S(1)}, bf16[128,512]{1,0:T(8,128)(2,1)S(1)}, u32[]{:S(2)}, u32[]{:S(2)}) collective-permute-start(bf16[128,512]{1,0:T(8,128)(2,1)S(1)} %get-tuple-element.106), channel_id=1, source_target_pairs={{0,2},{1,3},{2,0},{3,1},{4,6},{5,7},{6,4},{7,5},{8,10},{9,11},{10,... | collective-permute-start | bytes 393224 | tf_op jit(solution)/shard_map/ppermute | solution.py:289
  74.3 1.5 %collective-permute-start.22 = (bf16[128,512]{1,0:T(8,128)(2,1)S(1)}, bf16[128,512]{1,0:T(8,128)(2,1)S(1)}, u32[]{:S(2)}, u32[]{:S(2)}) collective-permute-start(bf16[128,512]{1,0:T(8,128)(2,1)S(1)} %get-tuple-element.107), channel_id=1, source_target_pairs={{0,4},{1,5},{2,6},{3,7},{4,0},{5,1},{6,2},{7,3},{8,12},{9,13},{10,... | collective-permute-start | bytes 393224 | tf_op jit(solution)/shard_map/ppermute | solution.py:289
  76.5 2.1 %collective-permute-done.21.refs_1_ = bf16[128,512]{1,0:T(8,128)(2,1)S(1)} collective-permute-done((bf16[128,512]{1,0:T(8,128)(2,1)S(1)}, bf16[128,512]{1,0:T(8,128)(2,1)S(1)}, u32[]{:S(2)}, u32[]{:S(2)}) %collective-permute-start.21) | collective-permute-done | bytes 131104 | tf_op jit(solution)/shard_map/ppermute | solution.py:289
  78.6 1.2 %collective-permute-done.22.refs_2_ = bf16[128,512]{1,0:T(8,128)(2,1)S(1)} collective-permute-done((bf16[128,512]{1,0:T(8,128)(2,1)S(1)}, bf16[128,512]{1,0:T(8,128)(2,1)S(1)}, u32[]{:S(2)}, u32[]{:S(2)}) %collective-permute-start.22) | collective-permute-done | bytes 131104 | tf_op jit(solution)/shard_map/ppermute | solution.py:289
  79.8 1.9 %collective-permute-done.23.refs_3_ = bf16[128,512]{1,0:T(8,128)(2,1)S(1)} collective-permute-done((bf16[128,512]{1,0:T(8,128)(2,1)S(1)}, bf16[128,512]{1,0:T(8,128)(2,1)S(1)}, u32[]{:S(2)}, u32[]{:S(2)}) %collective-permute-start.23) | collective-permute-done | bytes 131104 | tf_op jit(solution)/shard_map/ppermute | solution.py:289
  81.7 2.6 %collective-permute-done.29.refs_1_ = bf16[256,512]{1,0:T(8,128)(2,1)S(1)} collective-permute-done((bf16[256,512]{1,0:T(8,128)(2,1)S(1)}, bf16[256,512]{1,0:T(8,128)(2,1)S(1)}, u32[]{:S(2)}, u32[]{:S(2)}) %collective-permute-start.29) | collective-permute-done | bytes 262176 | tf_op jit(solution)/shard_map/ppermute | solution.py:289
  84.5 1.4 %collective-permute-start.30 = (bf16[256,128]{1,0:T(8,128)(2,1)S(1)}, bf16[256,128]{1,0:T(8,128)(2,1)S(1)}, u32[]{:S(2)}, u32[]{:S(2)}) collective-permute-start(bf16[256,128]{1,0:T(8,128)(2,1)S(1)} %get-tuple-element.119), channel_id=1, source_target_pairs={{0,2},{1,3},{2,0},{3,1},{4,6},{5,7},{6,4},{7,5},{8,10},{9,11},{10,... | collective-permute-start | bytes 196616 | tf_op jit(solution)/shard_map/ppermute | solution.py:289
  85.9 1.5 %collective-permute-start.31 = (bf16[256,128]{1,0:T(8,128)(2,1)S(1)}, bf16[256,128]{1,0:T(8,128)(2,1)S(1)}, u32[]{:S(2)}, u32[]{:S(2)}) collective-permute-start(bf16[256,128]{1,0:T(8,128)(2,1)S(1)} %get-tuple-element.120), channel_id=1, source_target_pairs={{0,4},{1,5},{2,6},{3,7},{4,0},{5,1},{6,2},{7,3},{8,12},{9,13},{10,... | collective-permute-start | bytes 196616 | tf_op jit(solution)/shard_map/ppermute | solution.py:289
  89.4 1.2 %collective-permute-done.31.refs_2_ = bf16[256,128]{1,0:T(8,128)(2,1)S(1)} collective-permute-done((bf16[256,128]{1,0:T(8,128)(2,1)S(1)}, bf16[256,128]{1,0:T(8,128)(2,1)S(1)}, u32[]{:S(2)}, u32[]{:S(2)}) %collective-permute-start.31) | collective-permute-done | bytes 65568 | tf_op jit(solution)/shard_map/ppermute | solution.py:289
  90.6 1.9 %collective-permute-done.32.refs_3_ = bf16[256,128]{1,0:T(8,128)(2,1)S(1)} collective-permute-done((bf16[256,128]{1,0:T(8,128)(2,1)S(1)}, bf16[256,128]{1,0:T(8,128)(2,1)S(1)}, u32[]{:S(2)}, u32[]{:S(2)}) %collective-permute-start.32) | collective-permute-done | bytes 65568 | tf_op jit(solution)/shard_map/ppermute | solution.py:289
  92.5 1.0 %shard_map.99 = f32[128,1024]{1,0:T(8,128)} custom-call(s32[1]{0:T(128)} %bitcast.place, f32[256,128]{1,0:T(8,128)S(1)} %get-tuple-element.118.refs_0_, bf16[256,128]{1,0:T(8,128)(2,1)S(1)} %collective-permute-done.30.refs_1_, bf16[256,128]{1,0:T(8,128)(2,1)S(1)} %collective-permute-done.31.refs_2_, bf16[256,128]{1,0:T(8,128)(2,1)S(1)} %collective-permute-done.32.refs_3_), custom_call_target="tpu_custom_call" | custom-call | bytes 851972 | tf_op jit(solution)/shard_map/pallas_call | solution.py:40
  (64 shorter events, 14.5 us)
Async XLA Ops:
  2.8 9.1 %collective-permute-start = (bf16[384,256]{1,0:T(8,128)(2,1)}, bf16[384,256]{1,0:T(8,128)(2,1)S(1)}, u32[]{:S(2)}, u32[]{:S(2)}) collective-permute-start(bf16[384,256]{1,0:T(8,128)(2,1)} %get-tuple-element.69), channel_id=1, source_target_pairs={{0,2},{1,3},{2,0},{3,1},{4,6},{5,7},{6,4},{7,5},{8,10},{9,11},{10,... | collective-permute-start | bytes 589832 | tf_op jit(solution)/shard_map/ppermute | solution.py:289
  5.8 12.2 %collective-permute-start.1 = (bf16[384,256]{1,0:T(8,128)(2,1)}, bf16[384,256]{1,0:T(8,128)(2,1)S(1)}, u32[]{:S(2)}, u32[]{:S(2)}) collective-permute-start(bf16[384,256]{1,0:T(8,128)(2,1)} %get-tuple-element.70), channel_id=1, source_target_pairs={{0,4},{1,5},{2,6},{3,7},{4,0},{5,1},{6,2},{7,3},{8,12},{9,13},{10,... | collective-permute-start | bytes 589832 | tf_op jit(solution)/shard_map/ppermute | solution.py:289
  7.3 10.7 %collective-permute-start.2 = (bf16[384,256]{1,0:T(8,128)(2,1)}, bf16[384,256]{1,0:T(8,128)(2,1)S(1)}, u32[]{:S(2)}, u32[]{:S(2)}) collective-permute-start(bf16[384,256]{1,0:T(8,128)(2,1)} %get-tuple-element.71), channel_id=1, source_target_pairs={{0,6},{1,7},{2,4},{3,5},{4,2},{5,3},{6,0},{7,1},{8,14},{9,15},{10,... | collective-permute-start | bytes 589832 | tf_op jit(solution)/shard_map/ppermute | solution.py:289
  7.4 31.7 %collective-permute-start.4 = (bf16[128,4096]{1,0:T(8,128)(2,1)}, bf16[128,4096]{1,0:T(8,128)(2,1)S(1)}, u32[]{:S(2)}, u32[]{:S(2)}) collective-permute-start(bf16[128,4096]{1,0:T(8,128)(2,1)} %refs_0_.4), channel_id=1, source_target_pairs={{0,4},{1,5},{2,6},{3,7},{4,0},{5,1},{6,2},{7,3},{8,12},{9,13},{10,... | collective-permute-start | bytes 3145736 | tf_op jit(solution)/shard_map/ppermute | solution.py:289
  9.3 29.7 %collective-permute-start.3 = (bf16[128,4096]{1,0:T(8,128)(2,1)}, bf16[128,4096]{1,0:T(8,128)(2,1)S(1)}, u32[]{:S(2)}, u32[]{:S(2)}) collective-permute-start(bf16[128,4096]{1,0:T(8,128)(2,1)} %refs_0_.4), channel_id=1, source_target_pairs={{0,2},{1,3},{2,0},{3,1},{4,6},{5,7},{6,4},{7,5},{8,10},{9,11},{10,... | collective-permute-start | bytes 3145736 | tf_op jit(solution)/shard_map/ppermute | solution.py:289
  18.3 14.9 %collective-permute-start.6 = (bf16[640,256]{1,0:T(8,128)(2,1)S(1)}, bf16[640,256]{1,0:T(8,128)(2,1)S(1)}, u32[]{:S(2)}, u32[]{:S(2)}) collective-permute-start(bf16[640,256]{1,0:T(8,128)(2,1)S(1)} %get-tuple-element.79.refs_6_), channel_id=1, source_target_pairs={{0,16},{1,17},{2,18},{3,19},{4,20},{5,21},{6,22},{7,23},{8,24},{9,... | collective-permute-start | bytes 983048 | tf_op jit(solution)/shard_map/ppermute | solution.py:289
  21.0 12.9 %collective-permute-start.5 = (bf16[640,256]{1,0:T(8,128)(2,1)S(1)}, bf16[640,256]{1,0:T(8,128)(2,1)S(1)}, u32[]{:S(2)}, u32[]{:S(2)}) collective-permute-start(bf16[640,256]{1,0:T(8,128)(2,1)S(1)} %get-tuple-element.79.refs_6_), channel_id=1, source_target_pairs={{0,8},{1,9},{2,10},{3,11},{4,12},{5,13},{6,14},{7,15},{8,0},{9,1},... | collective-permute-start | bytes 983048 | tf_op jit(solution)/shard_map/ppermute | solution.py:289
  33.3 8.5 %collective-permute-start.7 = (bf16[640,256]{1,0:T(8,128)(2,1)S(1)}, bf16[640,256]{1,0:T(8,128)(2,1)S(1)}, u32[]{:S(2)}, u32[]{:S(2)}) collective-permute-start(bf16[640,256]{1,0:T(8,128)(2,1)S(1)} %collective-permute-done.6.refs_8_), channel_id=1, source_target_pairs={{0,8},{1,9},{2,10},{3,11},{4,12},{5,13},{6,14},{7,15},{8,0},{9,1},... | collective-permute-start | bytes 983048 | tf_op jit(solution)/shard_map/ppermute | solution.py:289
  33.9 7.9 %collective-permute-start.10 = (bf16[640,256]{1,0:T(8,128)(2,1)S(1)}, bf16[640,256]{1,0:T(8,128)(2,1)S(1)}, u32[]{:S(2)}, u32[]{:S(2)}) collective-permute-start(bf16[640,256]{1,0:T(8,128)(2,1)S(1)} %collective-permute-done.6.refs_8_), channel_id=1, source_target_pairs={{0,1},{1,0},{2,3},{3,2},{4,5},{5,4},{6,7},{7,6},{8,9},{9,8},{10,11... | collective-permute-start | bytes 983048 | tf_op jit(solution)/shard_map/ppermute | solution.py:289
  33.9 8.4 %collective-permute-start.9 = (bf16[640,256]{1,0:T(8,128)(2,1)S(1)}, bf16[640,256]{1,0:T(8,128)(2,1)S(1)}, u32[]{:S(2)}, u32[]{:S(2)}) collective-permute-start(bf16[640,256]{1,0:T(8,128)(2,1)S(1)} %collective-permute-done.5.refs_7_), channel_id=1, source_target_pairs={{0,1},{1,0},{2,3},{3,2},{4,5},{5,4},{6,7},{7,6},{8,9},{9,8},{10,11... | collective-permute-start | bytes 983048 | tf_op jit(solution)/shard_map/ppermute | solution.py:289
  39.2 12.5 %collective-permute-start.15 = (bf16[64,4096]{1,0:T(8,128)(2,1)S(1)}, bf16[64,4096]{1,0:T(8,128)(2,1)S(1)}, u32[]{:S(2)}, u32[]{:S(2)}) collective-permute-start(bf16[64,4096]{1,0:T(8,128)(2,1)S(1)} %slice.7), channel_id=1, source_target_pairs={{0,2},{1,3},{2,0},{3,1},{4,6},{5,7},{6,4},{7,5},{8,10},{9,11},{10,... | collective-permute-start | bytes 1572872 | tf_op jit(solution)/shard_map/ppermute | solution.py:289
  39.6 12.5 %collective-permute-start.14 = (bf16[64,4096]{1,0:T(8,128)(2,1)S(1)}, bf16[64,4096]{1,0:T(8,128)(2,1)S(1)}, u32[]{:S(2)}, u32[]{:S(2)}) collective-permute-start(bf16[64,4096]{1,0:T(8,128)(2,1)S(1)} %slice.6), channel_id=1, source_target_pairs={{0,4},{1,5},{2,6},{3,7},{4,0},{5,1},{6,2},{7,3},{8,12},{9,13},{10,... | collective-permute-start | bytes 1572872 | tf_op jit(solution)/shard_map/ppermute | solution.py:289
  41.8 1.6 %collective-permute-start.11 = (bf16[640,256]{1,0:T(8,128)(2,1)S(1)}, bf16[640,256]{1,0:T(8,128)(2,1)S(1)}, u32[]{:S(2)}, u32[]{:S(2)}) collective-permute-start(bf16[640,256]{1,0:T(8,128)(2,1)S(1)} %collective-permute-done.7.refs_9_), channel_id=1, source_target_pairs={{0,1},{1,0},{2,3},{3,2},{4,5},{5,4},{6,7},{7,6},{8,9},{9,8},{10,11... | collective-permute-start | bytes 983048 | tf_op jit(solution)/shard_map/ppermute | solution.py:289
  41.8 2.5 %collective-permute-start.8 = (bf16[640,256]{1,0:T(8,128)(2,1)S(1)}, bf16[640,256]{1,0:T(8,128)(2,1)S(1)}, u32[]{:S(2)}, u32[]{:S(2)}) collective-permute-start(bf16[640,256]{1,0:T(8,128)(2,1)S(1)} %get-tuple-element.79.refs_6_), channel_id=1, source_target_pairs={{0,1},{1,0},{2,3},{3,2},{4,5},{5,4},{6,7},{7,6},{8,9},{9,8},{10,11... | collective-permute-start | bytes 983048 | tf_op jit(solution)/shard_map/ppermute | solution.py:289
  42.3 2.0 %collective-permute-start.12 = (bf16[4,256,128]{2,1,0:T(8,128)(2,1)S(1)}, bf16[4,256,128]{2,1,0:T(8,128)(2,1)S(1)}, u32[]{:S(2)}, u32[]{:S(2)}) collective-permute-start(bf16[4,256,128]{2,1,0:T(8,128)(2,1)S(1)} %get-tuple-element.80.refs_14_), channel_id=1, source_target_pairs={{0,1},{1,0},{2,3},{3,2},{4,5},{5,4},{6,7},{7,6},{8,9},{9,8},{10,11... | collective-permute-start | bytes 786440 | tf_op jit(solution)/shard_map/ppermute | solution.py:289
  53.9 2.1 %collective-permute-start.17 = (bf16[256,512]{1,0:T(8,128)(2,1)S(1)}, bf16[256,512]{1,0:T(8,128)(2,1)S(1)}, u32[]{:S(2)}, u32[]{:S(2)}) collective-permute-start(bf16[256,512]{1,0:T(8,128)(2,1)S(1)} %get-tuple-element.103), channel_id=1, source_target_pairs={{0,1},{1,0},{2,3},{3,2},{4,5},{5,4},{6,7},{7,6},{8,9},{9,8},{10,11... | collective-permute-start | bytes 786440 | tf_op jit(solution)/shard_map/ppermute | solution.py:289
  54.0 1.8 %collective-permute-start.13 = (bf16[3,256,128]{2,1,0:T(8,128)(2,1)S(1)}, bf16[3,256,128]{2,1,0:T(8,128)(2,1)S(1)}, u32[]{:S(2)}, u32[]{:S(2)}) collective-permute-start(bf16[3,256,128]{2,1,0:T(8,128)(2,1)S(1)} %get-tuple-element.88.refs_0_.refs_7_), channel_id=1, source_target_pairs={{0,1},{1,0},{2,3},{3,2},{4,5},{5,4},{6,7},{7,6},{8,9},{9,8},{10,11... | collective-permute-start | bytes 589832 | tf_op jit(solution)/shard_map/ppermute | solution.py:289
  55.3 7.9 %collective-permute-start.25 = (bf16[256,512]{1,0:T(8,128)(2,1)S(1)}, bf16[256,512]{1,0:T(8,128)(2,1)S(1)}, u32[]{:S(2)}, u32[]{:S(2)}) collective-permute-start(bf16[256,512]{1,0:T(8,128)(2,1)S(1)} %get-tuple-element.114), channel_id=1, source_target_pairs={{0,1},{1,0},{2,3},{3,2},{4,5},{5,4},{6,7},{7,6},{8,9},{9,8},{10,11... | collective-permute-start | bytes 786440 | tf_op jit(solution)/shard_map/ppermute | solution.py:289
  56.1 5.8 %collective-permute-start.18 = (bf16[128,128]{1,0:T(8,128)(2,1)S(1)}, bf16[128,128]{1,0:T(8,128)(2,1)S(1)}, u32[]{:S(2)}, u32[]{:S(2)}) collective-permute-start(bf16[128,128]{1,0:T(8,128)(2,1)S(1)} %shard_map.92), channel_id=1, source_target_pairs={{8,0},{9,1},{10,2},{11,3},{12,4},{13,5},{14,6},{15,7},{16,8},{17,9... | collective-permute-start | bytes 98312 | tf_op jit(solution)/shard_map/ppermute | solution.py:301
  57.9 10.9 %collective-permute-start.27 = (bf16[256,512]{1,0:T(8,128)(2,1)S(1)}, bf16[256,512]{1,0:T(8,128)(2,1)S(1)}, u32[]{:S(2)}, u32[]{:S(2)}) collective-permute-start(bf16[256,512]{1,0:T(8,128)(2,1)S(1)} %get-tuple-element.116), channel_id=1, source_target_pairs={{0,1},{1,0},{2,3},{3,2},{4,5},{5,4},{6,7},{7,6},{8,9},{9,8},{10,11... | collective-permute-start | bytes 786440 | tf_op jit(solution)/shard_map/ppermute | solution.py:289
  58.5 17.3 %collective-permute-start.24 = (bf16[256,512]{1,0:T(8,128)(2,1)S(1)}, bf16[256,512]{1,0:T(8,128)(2,1)S(1)}, u32[]{:S(2)}, u32[]{:S(2)}) collective-permute-start(bf16[256,512]{1,0:T(8,128)(2,1)S(1)} %get-tuple-element.111), channel_id=1, source_target_pairs={{0,1},{1,0},{2,3},{3,2},{4,5},{5,4},{6,7},{7,6},{8,9},{9,8},{10,11... | collective-permute-start | bytes 786440 | tf_op jit(solution)/shard_map/ppermute | solution.py:289
  59.2 10.5 %collective-permute-start.28 = (bf16[256,512]{1,0:T(8,128)(2,1)S(1)}, bf16[256,512]{1,0:T(8,128)(2,1)S(1)}, u32[]{:S(2)}, u32[]{:S(2)}) collective-permute-start(bf16[256,512]{1,0:T(8,128)(2,1)S(1)} %add_convert_fusion.2), channel_id=1, source_target_pairs={{0,8},{1,9},{2,10},{3,11},{4,12},{5,13},{6,14},{7,15},{8,0},{9,1},... | collective-permute-start | bytes 786440 | tf_op jit(solution)/shard_map/ppermute | solution.py:289
  61.9 6.8 %collective-permute-start.19 = (bf16[128,128]{1,0:T(8,128)(2,1)S(1)}, bf16[128,128]{1,0:T(8,128)(2,1)S(1)}, u32[]{:S(2)}, u32[]{:S(2)}) collective-permute-start(bf16[128,128]{1,0:T(8,128)(2,1)S(1)} %fusion), channel_id=1, source_target_pairs={{16,0},{17,1},{18,2},{19,3},{20,4},{21,5},{22,6},{23,7},{24,8},{25... | collective-permute-start | bytes 98312 | tf_op jit(solution)/shard_map/ppermute | solution.py:301
  63.3 18.4 %collective-permute-start.26 = (bf16[256,512]{1,0:T(8,128)(2,1)S(1)}, bf16[256,512]{1,0:T(8,128)(2,1)S(1)}, u32[]{:S(2)}, u32[]{:S(2)}) collective-permute-start(bf16[256,512]{1,0:T(8,128)(2,1)S(1)} %add_convert_fusion.1), channel_id=1, source_target_pairs={{0,8},{1,9},{2,10},{3,11},{4,12},{5,13},{6,14},{7,15},{8,0},{9,1},... | collective-permute-start | bytes 786440 | tf_op jit(solution)/shard_map/ppermute | solution.py:289
  68.7 3.5 %collective-permute-start.20 = (bf16[128,128]{1,0:T(8,128)(2,1)S(1)}, bf16[128,128]{1,0:T(8,128)(2,1)S(1)}, u32[]{:S(2)}, u32[]{:S(2)}) collective-permute-start(bf16[128,128]{1,0:T(8,128)(2,1)S(1)} %fusion.1.refs_14_), channel_id=1, source_target_pairs={{0,1},{1,0},{2,3},{3,2},{4,5},{5,4},{6,7},{7,6},{8,9},{9,8},{10,11... | collective-permute-start | bytes 98312 | tf_op jit(solution)/shard_map/ppermute | solution.py:289
  69.8 14.5 %collective-permute-start.29 = (bf16[256,512]{1,0:T(8,128)(2,1)S(1)}, bf16[256,512]{1,0:T(8,128)(2,1)S(1)}, u32[]{:S(2)}, u32[]{:S(2)}) collective-permute-start(bf16[256,512]{1,0:T(8,128)(2,1)S(1)} %add_convert_fusion), channel_id=1, source_target_pairs={{0,16},{1,17},{2,18},{3,19},{4,20},{5,21},{6,22},{7,23},{8,24},{9,... | collective-permute-start | bytes 786440 | tf_op jit(solution)/shard_map/ppermute | solution.py:289
  72.9 5.8 %collective-permute-start.21 = (bf16[128,512]{1,0:T(8,128)(2,1)S(1)}, bf16[128,512]{1,0:T(8,128)(2,1)S(1)}, u32[]{:S(2)}, u32[]{:S(2)}) collective-permute-start(bf16[128,512]{1,0:T(8,128)(2,1)S(1)} %get-tuple-element.106), channel_id=1, source_target_pairs={{0,2},{1,3},{2,0},{3,1},{4,6},{5,7},{6,4},{7,5},{8,10},{9,11},{10,... | collective-permute-start | bytes 393224 | tf_op jit(solution)/shard_map/ppermute | solution.py:289
  74.3 5.5 %collective-permute-start.22 = (bf16[128,512]{1,0:T(8,128)(2,1)S(1)}, bf16[128,512]{1,0:T(8,128)(2,1)S(1)}, u32[]{:S(2)}, u32[]{:S(2)}) collective-permute-start(bf16[128,512]{1,0:T(8,128)(2,1)S(1)} %get-tuple-element.107), channel_id=1, source_target_pairs={{0,4},{1,5},{2,6},{3,7},{4,0},{5,1},{6,2},{7,3},{8,12},{9,13},{10,... | collective-permute-start | bytes 393224 | tf_op jit(solution)/shard_map/ppermute | solution.py:289
  75.9 5.9 %collective-permute-start.23 = (bf16[128,512]{1,0:T(8,128)(2,1)S(1)}, bf16[128,512]{1,0:T(8,128)(2,1)S(1)}, u32[]{:S(2)}, u32[]{:S(2)}) collective-permute-start(bf16[128,512]{1,0:T(8,128)(2,1)S(1)} %get-tuple-element.108), channel_id=1, source_target_pairs={{0,6},{1,7},{2,4},{3,5},{4,2},{5,3},{6,0},{7,1},{8,14},{9,15},{10,... | collective-permute-start | bytes 393224 | tf_op jit(solution)/shard_map/ppermute | solution.py:289
  84.5 5.0 %collective-permute-start.30 = (bf16[256,128]{1,0:T(8,128)(2,1)S(1)}, bf16[256,128]{1,0:T(8,128)(2,1)S(1)}, u32[]{:S(2)}, u32[]{:S(2)}) collective-permute-start(bf16[256,128]{1,0:T(8,128)(2,1)S(1)} %get-tuple-element.119), channel_id=1, source_target_pairs={{0,2},{1,3},{2,0},{3,1},{4,6},{5,7},{6,4},{7,5},{8,10},{9,11},{10,... | collective-permute-start | bytes 196616 | tf_op jit(solution)/shard_map/ppermute | solution.py:289
  85.9 4.8 %collective-permute-start.31 = (bf16[256,128]{1,0:T(8,128)(2,1)S(1)}, bf16[256,128]{1,0:T(8,128)(2,1)S(1)}, u32[]{:S(2)}, u32[]{:S(2)}) collective-permute-start(bf16[256,128]{1,0:T(8,128)(2,1)S(1)} %get-tuple-element.120), channel_id=1, source_target_pairs={{0,4},{1,5},{2,6},{3,7},{4,0},{5,1},{6,2},{7,3},{8,12},{9,13},{10,... | collective-permute-start | bytes 196616 | tf_op jit(solution)/shard_map/ppermute | solution.py:289
  87.4 5.2 %collective-permute-start.32 = (bf16[256,128]{1,0:T(8,128)(2,1)S(1)}, bf16[256,128]{1,0:T(8,128)(2,1)S(1)}, u32[]{:S(2)}, u32[]{:S(2)}) collective-permute-start(bf16[256,128]{1,0:T(8,128)(2,1)S(1)} %get-tuple-element.121), channel_id=1, source_target_pairs={{0,6},{1,7},{2,4},{3,5},{4,2},{5,3},{6,0},{7,1},{8,14},{9,15},{10,... | collective-permute-start | bytes 196616 | tf_op jit(solution)/shard_map/ppermute | solution.py:289
  (4 other events, 54.2 us)

commit v5 on v4

--- a/solution.py
+++ b/solution.py
@@ -181,16 +181,42 @@
             last_low[...] = low
 
 
-def last_kernel(rows, depth, place, top, bottom, weights, p, high, low, *outs):
+def last_kernel(rows, depth, place, top, bottom, weights, p, high, low, grown, *outs):
+    *outs, every = outs
     query = dot(jnp.concatenate([top[...], bottom[...]], axis=0), weights[...])
     attend_block(0, rows, depth, query, p, high[...], low[...], outs)
-
-
-def half_kernel(place, *refs):
-    *parts, half, total = refs
+    every[:3] = grown[...]
+    every[3] = outs[2][0]
+
+
+def load_kernel(depth, place, keep, gift, *refs):
+    *parts, load, half, total = refs
     _, _, core = seat(place)
+    load[:FEAT, :] = (keep[...] + gift[...].astype(F32)).astype(BF16)
     total[...] = sum(ref[j].astype(F32) for ref in parts for j in range(ref.shape[0]))
-    half[...] = total[pl.ds(pl.multiple_of(core * HALF, HALF), HALF), :].astype(BF16)
+    mine = total[pl.ds(pl.multiple_of(core * HALF, HALF), HALF), :].astype(BF16)
+    half[...] = mine
+    wide = load.shape[1] // HEAD_DIM
+    tall = HALF // wide
+    for i in range(wide):
+        load[FEAT:, i * HEAD_DIM : (i + 1) * HEAD_DIM] = mine[i * tall : (i + 1) * tall, :]
+
+
+def unload_kernel(place, load, half, came, window):
+    wide = load.shape[1] // HEAD_DIM
+    tall = HALF // wide
+    for i in range(wide):
+        came[i * tall : (i + 1) * tall, :] = load[FEAT:, i * HEAD_DIM : (i + 1) * HEAD_DIM]
+    window[...] = (half[...].astype(F32) + came[...].astype(F32)).astype(BF16)
+
+
+def rest_kernel(place, *refs):
+    *steps, rest = refs
+    _, z, _ = seat(place)
+    total = jnp.zeros(rest.shape, F32)
+    for i, ref in enumerate(steps):
+        total = total + before(z, z ^ 1 << i) * ref[...].astype(F32)
+    rest[...] = total.astype(BF16)
 
 
 def side_kernel(place, feats, d_num, scores, mixed, val_part, key_part):
@@ -235,16 +261,16 @@
 
 def finish_kernel(rows, depth, outer, place, *refs):
     p, refs = refs[:4], refs[4:]
-    pairs, (own_rest, other_rest, *outs, rest) = refs[:10], refs[10:]
-    att, val_part, key_part, own_grown, other_grown = (
-        [*(first.at[j] for j in range(3)), last.at[0]] for first, last in zip(pairs[:5], pairs[5:])
+    pairs, (own_grown, other_grown, own_rest, other_rest, *outs, rest) = refs[:6], refs[6:]
+    att, val_part, key_part = (
+        [*(first.at[j] for j in range(3)), last.at[0]] for first, last in zip(pairs[:3], pairs[3:])
     )
     q, _, core = seat(place)
     for flip, ref in ((0, own_rest), (1, other_rest)):
         rest[pl.ds(pl.multiple_of((core ^ flip) * HALF, HALF), HALF), :] = ref[...].astype(F32)
     base = rest[...]
-    own = [ref[...].astype(F32) for ref in own_grown]
-    other = [ref[...].astype(F32) for ref in other_grown]
+    own = [own_grown[j].astype(F32) for j in range(4)]
+    other = [other_grown[j].astype(F32) for j in range(4)]
     for j, out in enumerate(outs):
         here = (q ^ j) * CORES + core
         later = base
@@ -297,9 +323,6 @@
     def plane_swap(block, k):
         return swap(block, inner * k)
 
-    def down(block, k):
-        return lax.ppermute(block, "ctx", [(i, i - inner * k) for i in range(inner * k, count)])
-
     packs = call(
         pack_kernel,
         [((depth + 2 * rows, FEAT), BF16)] * 4,
@@ -359,47 +382,53 @@
         flops=2 * 3 * rows * width * FEAT,
         scratch=[pltpu.VMEM((3 * rows, FEAT), F32)],
     )
-    last = call(
+    *last, grown = call(
         functools.partial(last_kernel, rows, depth),
-        kept(1),
-        [place, *h3, weights, p[3], high, low],
+        kept(1) + [((4, FEAT, HEAD_DIM), BF16)],
+        [place, *h3, weights, p[3], high, low, first[2]],
         flops=2 * rows * width * FEAT,
     )
-    others = [core_swap(first[2]), core_swap(last[2])]
-    (half,) = call(
-        half_kernel,
-        [((HALF, HEAD_DIM), BF16)],
-        [place, first[2], last[2], *others],
-        scratch=[pltpu.VMEM((FEAT, HEAD_DIM), F32)],
-    )
+    other_grown = core_swap(grown)
     sums = [None] * outer
     order = sorted(range(outer), key=lambda k: (-k.bit_count(), k))
-    dq_first, dq_last = first[1], last[1]
     for k in order:
         keep, give = call(
             functools.partial(grad_kernel, depth, k),
             [((FEAT, 4 * depth), F32), ((FEAT, 4 * depth), BF16)],
-            [place, *h, dq_first, dq_last],
+            [place, *h, first[1], last[1]],
             flops=2 * positions * width * FEAT // outer,
         )
-        sums[k] = keep + core_swap(give).astype(F32)
+        gift = core_swap(give)
         if k == order[0]:
-            sums[k], half = lax.optimization_barrier((sums[k].astype(BF16), half))
-    rest, window, step = jnp.zeros(half.shape, F32), half, 1
-    while step < outer:
-        came = down(window, step)
-        rest = rest + came.astype(F32)
-        window = (window.astype(F32) + came.astype(F32)).astype(BF16)
-        step *= 2
-    arrived = []
+            extra = HALF * HEAD_DIM // (4 * depth)
+            sums[k], half = call(
+                functools.partial(load_kernel, depth),
+                [((FEAT + extra, 4 * depth), BF16), ((HALF, HEAD_DIM), BF16)],
+                [place, keep, gift, grown, other_grown],
+                scratch=[pltpu.VMEM((FEAT, HEAD_DIM), F32)],
+            )
+        else:
+            sums[k] = keep + gift.astype(F32)
+    arrived, steps = [], []
     for k in order[:-1]:
         came, onward = plane_swap(sums[k].astype(BF16), k & -k), k & k - 1
+        if k == order[0]:
+            came, _ = lax.optimization_barrier((came, sums[order[1]].astype(BF16)))
+            near, window = call(
+                unload_kernel, [((HALF, HEAD_DIM), BF16)] * 2, [place, came, half]
+            )
+            steps.append(near)
+            came = came[:FEAT]
         if onward:
             sums[onward] = sums[onward] + came.astype(F32)
         else:
             arrived.append(came)
+    while 1 << len(steps) < outer:
+        came = plane_swap(window, 1 << len(steps))
+        steps.append(came)
+        window = (window.astype(F32) + came.astype(F32)).astype(BF16)
+    (rest,) = call(rest_kernel, [((HALF, HEAD_DIM), BF16)], [place, *steps])
     own = sums[0]
-    rest = rest.astype(BF16)
     other_rest = core_swap(rest)
     outs = call(
         functools.partial(finish_kernel, rows, depth, outer),
@@ -407,8 +436,10 @@
         [
             place,
             *p,
-            *(first[0], *side(first[3:]), first[2], others[0]),
-            *(last[0], *side(last[3:]), last[2], others[1]),
+            *(first[0], *side(first[3:])),
+            *(last[0], *side(last[3:])),
+            grown,
+            other_grown,
             rest,
             other_rest,
         ],
@@ -425,7 +456,6 @@
         ],
         [place, *placed],
     )
-    own, placed = lax.optimization_barrier((own, placed))
     blocks = call(
         functools.partial(sum_kernel, depth),
         [((FEAT, depth), F32)] + [((FEAT, depth), BF16)] * 3,

time: 93.7 us -> 92.8 us (level)
  starting transfers between devices: 34.3 us -> 29.8 us
  waiting for transfers between devices: 44.2 us -> 47.2 us
    ppermute x31, waiting for transfers between devices: 40.3 us -> 47.2 us  [swap(): return lax.ppermute(block, 'ctx', [(i, i ^ bits) for i in range(count)])]
    ppermute x2 -> x0, waiting for transfers between devices: 3.84 us -> none  [down(): lax.ppermute(block, 'ctx', [(i, i - inner * k) for i in range(inner * k,...]
    ppermute x2 -> x0, starting transfers between devices: 2.58 us -> none  [down(): lax.ppermute(block, 'ctx', [(i, i - inner * k) for i in range(inner * k,...]
    ppermute x31, starting transfers between devices: 31.7 us -> 29.8 us  [swap(): return lax.ppermute(block, 'ctx', [(i, i ^ bits) for i in range(count)])]
    pallas_call x16 -> x18, Pallas kernels: 12.8 us -> 13.5 us  [call(): pl.pallas_call(kernel, out_shape=shapes, in_specs=[pl.BlockSpec(memory_sp...]
  transfers between devices with their start and end apart: 33 -> 31, of which waited for: 18 -> 16; matrix products, arithmetic and copies ran while one was open for 0% -> 0% of each run, Pallas kernels for 8% -> 9%
where the time goes in v5:
time: 92.8 us; the launch traced here: 92.6 us
  waiting for transfers between devices  47.2 us (51%)
  starting transfers between devices  29.8 us (32%)
  Pallas kernels  13.5 us (15%)
  local copies, waits for them, and re-layouts  1.01 us (1%)
    ppermute x31, waiting for transfers between devices, swap(): return lax.ppermute(block, 'ctx', [(i, i ^ bits) for i in range(count)])  47.2 us
    ppermute x31, starting transfers between devices, swap(): return lax.ppermute(block, 'ctx', [(i, i ^ bits) for i in range(count)])  29.8 us
    pallas_call x18, Pallas kernels, call(): pl.pallas_call(kernel, out_shape=shapes, in_specs=[pl.BlockSpec(memory_sp...  13.5 us
  transfers between devices with their start and end apart: 31, of which 16 were waited for; matrix products, arithmetic and copies ran while one was open for 0% of the time, Pallas kernels for 9%

profile of v5, /device:TPU:0, one launch (start us, length us, event | category | flops | bytes accessed | tf_op | source)
XLA Modules:
  0.0 92.6 jit_solution(1252557250746705279)
XLA Ops:
  0.6 2.2 %shard_map.84 = (bf16[384,256]{1,0:T(8,128)(2,1)}, bf16[384,256]{1,0:T(8,128)(2,1)}, bf16[384,256]{1,0:T(8,128)(2,1)}, bf16[384,256]{1,0:T(8,128)(2,1)}) custom-call(s32[1]{0:T(128)} %bitcast.place, bf16[128,1024]{1,0:T(8,128)(2,1)} %w.1, bf16[128,1024]{1,0:T(8,128)(2,1)} %key.1, bf16[128,512]{1,0:T(8,128)(2,1)} %val.1, bf16[128,512]{1,0:T(8,128)(2,1)} %cot.1), custom_call_target="tpu_custom_call" | custom-call | bytes 1572868 | tf_op jit(solution)/shard_map/pallas_call | solution.py:40
  2.8 3.0 %collective-permute-start = (bf16[384,256]{1,0:T(8,128)(2,1)}, bf16[384,256]{1,0:T(8,128)(2,1)S(1)}, u32[]{:S(2)}, u32[]{:S(2)}) collective-permute-start(bf16[384,256]{1,0:T(8,128)(2,1)} %get-tuple-element.71), channel_id=1, source_target_pairs={{0,2},{1,3},{2,0},{3,1},{4,6},{5,7},{6,4},{7,5},{8,10},{9,11},{10,... | collective-permute-start | bytes 589832 | tf_op jit(solution)/shard_map/ppermute | solution.py:315
  5.8 1.5 %collective-permute-start.1 = (bf16[384,256]{1,0:T(8,128)(2,1)}, bf16[384,256]{1,0:T(8,128)(2,1)S(1)}, u32[]{:S(2)}, u32[]{:S(2)}) collective-permute-start(bf16[384,256]{1,0:T(8,128)(2,1)} %get-tuple-element.72), channel_id=1, source_target_pairs={{0,4},{1,5},{2,6},{3,7},{4,0},{5,1},{6,2},{7,3},{8,12},{9,13},{10,... | collective-permute-start | bytes 589832 | tf_op jit(solution)/shard_map/ppermute | solution.py:315
  7.4 2.0 %collective-permute-start.4 = (bf16[128,4096]{1,0:T(8,128)(2,1)}, bf16[128,4096]{1,0:T(8,128)(2,1)S(1)}, u32[]{:S(2)}, u32[]{:S(2)}) collective-permute-start(bf16[128,4096]{1,0:T(8,128)(2,1)} %refs_0_.4), channel_id=1, source_target_pairs={{0,4},{1,5},{2,6},{3,7},{4,0},{5,1},{6,2},{7,3},{8,12},{9,13},{10,... | collective-permute-start | bytes 3145736 | tf_op jit(solution)/shard_map/ppermute | solution.py:315
  9.3 1.5 %collective-permute-start.3 = (bf16[128,4096]{1,0:T(8,128)(2,1)}, bf16[128,4096]{1,0:T(8,128)(2,1)S(1)}, u32[]{:S(2)}, u32[]{:S(2)}) collective-permute-start(bf16[128,4096]{1,0:T(8,128)(2,1)} %refs_0_.4), channel_id=1, source_target_pairs={{0,2},{1,3},{2,0},{3,1},{4,6},{5,7},{6,4},{7,5},{8,10},{9,11},{10,... | collective-permute-start | bytes 3145736 | tf_op jit(solution)/shard_map/ppermute | solution.py:315
  10.8 0.9 copy-done.1
  12.0 6.1 %collective-permute-done.1.p2.refs_5_.refs_2_ = bf16[384,256]{1,0:T(8,128)(2,1)S(1)} collective-permute-done((bf16[384,256]{1,0:T(8,128)(2,1)}, bf16[384,256]{1,0:T(8,128)(2,1)S(1)}, u32[]{:S(2)}, u32[]{:S(2)}) %collective-permute-start.1) | collective-permute-done | bytes 196640 | tf_op jit(solution)/shard_map/ppermute | solution.py:315
  18.3 2.7 %collective-permute-start.6 = (bf16[640,256]{1,0:T(8,128)(2,1)S(1)}, bf16[640,256]{1,0:T(8,128)(2,1)S(1)}, u32[]{:S(2)}, u32[]{:S(2)}) collective-permute-start(bf16[640,256]{1,0:T(8,128)(2,1)S(1)} %get-tuple-element.81.refs_6_), channel_id=1, source_target_pairs={{0,16},{1,17},{2,18},{3,19},{4,20},{5,21},{6,22},{7,23},{8,24},{9,... | collective-permute-start | bytes 983048 | tf_op jit(solution)/shard_map/ppermute | solution.py:315
  21.0 1.6 %collective-permute-start.5 = (bf16[640,256]{1,0:T(8,128)(2,1)S(1)}, bf16[640,256]{1,0:T(8,128)(2,1)S(1)}, u32[]{:S(2)}, u32[]{:S(2)}) collective-permute-start(bf16[640,256]{1,0:T(8,128)(2,1)S(1)} %get-tuple-element.81.refs_6_), channel_id=1, source_target_pairs={{0,8},{1,9},{2,10},{3,11},{4,12},{5,13},{6,14},{7,15},{8,0},{9,1},... | collective-permute-start | bytes 983048 | tf_op jit(solution)/shard_map/ppermute | solution.py:315
  22.6 10.7 %collective-permute-done.6.refs_8_ = bf16[640,256]{1,0:T(8,128)(2,1)S(1)} collective-permute-done((bf16[640,256]{1,0:T(8,128)(2,1)S(1)}, bf16[640,256]{1,0:T(8,128)(2,1)S(1)}, u32[]{:S(2)}, u32[]{:S(2)}) %collective-permute-start.6) | collective-permute-done | bytes 327712 | tf_op jit(solution)/shard_map/ppermute | solution.py:315
  34.4 4.7 %collective-permute-done.4.refs_2_ = bf16[128,4096]{1,0:T(8,128)(2,1)S(1)} collective-permute-done((bf16[128,4096]{1,0:T(8,128)(2,1)}, bf16[128,4096]{1,0:T(8,128)(2,1)S(1)}, u32[]{:S(2)}, u32[]{:S(2)}) %collective-permute-start.4) | collective-permute-done | bytes 1048608 | tf_op jit(solution)/shard_map/ppermute | solution.py:315
  39.6 1.7 %collective-permute-start.13 = (bf16[64,4096]{1,0:T(8,128)(2,1)S(1)}, bf16[64,4096]{1,0:T(8,128)(2,1)S(1)}, u32[]{:S(2)}, u32[]{:S(2)}) collective-permute-start(bf16[64,4096]{1,0:T(8,128)(2,1)S(1)} %slice.9), channel_id=1, source_target_pairs={{0,4},{1,5},{2,6},{3,7},{4,0},{5,1},{6,2},{7,3},{8,12},{9,13},{10,... | collective-permute-start | bytes 1572872 | tf_op jit(solution)/shard_map/ppermute | solution.py:315
  42.4 1.0 %collective-permute-done.11.refs_13_ = bf16[640,256]{1,0:T(8,128)(2,1)S(1)} collective-permute-done((bf16[640,256]{1,0:T(8,128)(2,1)S(1)}, bf16[640,256]{1,0:T(8,128)(2,1)S(1)}, u32[]{:S(2)}, u32[]{:S(2)}) %collective-permute-start.11) | collective-permute-done | bytes 327712 | tf_op jit(solution)/shard_map/ppermute | solution.py:315
  43.4 0.8 collective-permute-done.12.refs_15_
  44.3 3.8 %shard_map.87 = (bf16[3,128,128]{2,1,0:T(8,128)(2,1)S(1)}, bf16[256,384]{1,0:T(8,128)(2,1)S(1)}, bf16[3,256,128]{2,1,0:T(8,128)(2,1)S(1)}, bf16[3,128,256]{2,1,0...) custom-call(s32[1]{0:T(128)} %bitcast.place, ...), custom_call_target="tpu_custom_call" | custom-call | flops 805306368 | bytes 10092548 | tf_op jit(solution)/shard_map/pallas_call | solution.py:40
  48.0 3.7 %collective-permute-done.14.bottom.refs_4_ = bf16[64,4096]{1,0:T(8,128)(2,1)S(1)} collective-permute-done((bf16[64,4096]{1,0:T(8,128)(2,1)S(1)}, bf16[64,4096]{1,0:T(8,128)(2,1)S(1)}, u32[]{:S(2)}, u32[]{:S(2)}) %collective-permute-start.14) | collective-permute-done | bytes 524320 | tf_op jit(solution)/shard_map/ppermute | solution.py:315
  52.1 1.9 %shard_map.89 = (bf16[1,128,128]{2,1,0:T(8,128)(2,1)S(1)}, bf16[256,128]{1,0:T(8,128)(2,1)S(1)}, bf16[1,256,128]{2,1,0:T(8,128)(2,1)}, bf16[1,128,256]{2,1,0:T(8...) custom-call(s32[1]{0:T(128)} %bitcast.place, ...), custom_call_target="tpu_custom_call" | custom-call | flops 268435456 | bytes 4259844 | tf_op jit(solution)/shard_map/pallas_call | solution.py:40
  56.4 1.6 %collective-permute-start.17 = (bf16[288,512]{1,0:T(8,128)(2,1)S(1)}, bf16[288,512]{1,0:T(8,128)(2,1)S(1)}, u32[]{:S(2)}, u32[]{:S(2)}) collective-permute-start(bf16[288,512]{1,0:T(8,128)(2,1)S(1)} %get-tuple-element.106), channel_id=1, source_target_pairs={{0,8},{1,9},{2,10},{3,11},{4,12},{5,13},{6,14},{7,15},{8,0},{9,1},... | collective-permute-start | bytes 884744 | tf_op jit(solution)/shard_map/ppermute | solution.py:315
  60.5 5.9 %collective-permute-done.17.load = bf16[288,512]{1,0:T(8,128)(2,1)S(1)} collective-permute-done((bf16[288,512]{1,0:T(8,128)(2,1)S(1)}, bf16[288,512]{1,0:T(8,128)(2,1)S(1)}, u32[]{:S(2)}, u32[]{:S(2)}) %collective-permute-start.17) | collective-permute-done | bytes 294944 | tf_op jit(solution)/shard_map/ppermute | solution.py:315
  66.3 2.6 %collective-permute-start.19 = (bf16[128,128]{1,0:T(8,128)(2,1)S(1)}, bf16[128,128]{1,0:T(8,128)(2,1)S(1)}, u32[]{:S(2)}, u32[]{:S(2)}) collective-permute-start(bf16[128,128]{1,0:T(8,128)(2,1)S(1)} %get-tuple-element.112), channel_id=1, source_target_pairs={{0,16},{1,17},{2,18},{3,19},{4,20},{5,21},{6,22},{7,23},{8,24},{9,... | collective-permute-start | bytes 98312 | tf_op jit(solution)/shard_map/ppermute | solution.py:315
  69.5 2.2 %collective-permute-done.19.refs_1_ = bf16[128,128]{1,0:T(8,128)(2,1)S(1)} collective-permute-done((bf16[128,128]{1,0:T(8,128)(2,1)S(1)}, bf16[128,128]{1,0:T(8,128)(2,1)S(1)}, u32[]{:S(2)}, u32[]{:S(2)}) %collective-permute-start.19) | collective-permute-done | bytes 32800 | tf_op jit(solution)/shard_map/ppermute | solution.py:315
  71.9 1.1 %collective-permute-done.20.refs_13_ = bf16[128,128]{1,0:T(8,128)(2,1)S(1)} collective-permute-done((bf16[128,128]{1,0:T(8,128)(2,1)S(1)}, bf16[128,128]{1,0:T(8,128)(2,1)S(1)}, u32[]{:S(2)}, u32[]{:S(2)}) %collective-permute-start.20) | collective-permute-done | bytes 32800 | tf_op jit(solution)/shard_map/ppermute | solution.py:315
  73.0 0.7 shard_map.96
  73.7 1.4 %collective-permute-start.21 = (bf16[128,512]{1,0:T(8,128)(2,1)S(1)}, bf16[128,512]{1,0:T(8,128)(2,1)S(1)}, u32[]{:S(2)}, u32[]{:S(2)}) collective-permute-start(bf16[128,512]{1,0:T(8,128)(2,1)S(1)} %get-tuple-element.114), channel_id=1, source_target_pairs={{0,2},{1,3},{2,0},{3,1},{4,6},{5,7},{6,4},{7,5},{8,10},{9,11},{10,... | collective-permute-start | bytes 393224 | tf_op jit(solution)/shard_map/ppermute | solution.py:315
  75.1 1.5 %collective-permute-start.22 = (bf16[128,512]{1,0:T(8,128)(2,1)S(1)}, bf16[128,512]{1,0:T(8,128)(2,1)S(1)}, u32[]{:S(2)}, u32[]{:S(2)}) collective-permute-start(bf16[128,512]{1,0:T(8,128)(2,1)S(1)} %get-tuple-element.115), channel_id=1, source_target_pairs={{0,4},{1,5},{2,6},{3,7},{4,0},{5,1},{6,2},{7,3},{8,12},{9,13},{10,... | collective-permute-start | bytes 393224 | tf_op jit(solution)/shard_map/ppermute | solution.py:315
  77.3 6.1 %collective-permute-done.27.refs_1_ = bf16[256,512]{1,0:T(8,128)(2,1)S(1)} collective-permute-done((bf16[256,512]{1,0:T(8,128)(2,1)S(1)}, bf16[256,512]{1,0:T(8,128)(2,1)S(1)}, u32[]{:S(2)}, u32[]{:S(2)}) %collective-permute-start.27) | collective-permute-done | bytes 262176 | tf_op jit(solution)/shard_map/ppermute | solution.py:315
  83.5 1.4 %collective-permute-start.28 = (bf16[256,128]{1,0:T(8,128)(2,1)S(1)}, bf16[256,128]{1,0:T(8,128)(2,1)S(1)}, u32[]{:S(2)}, u32[]{:S(2)}) collective-permute-start(bf16[256,128]{1,0:T(8,128)(2,1)S(1)} %get-tuple-element.123), channel_id=1, source_target_pairs={{0,2},{1,3},{2,0},{3,1},{4,6},{5,7},{6,4},{7,5},{8,10},{9,11},{10,... | collective-permute-start | bytes 196616 | tf_op jit(solution)/shard_map/ppermute | solution.py:315
  84.9 1.5 %collective-permute-start.29 = (bf16[256,128]{1,0:T(8,128)(2,1)S(1)}, bf16[256,128]{1,0:T(8,128)(2,1)S(1)}, u32[]{:S(2)}, u32[]{:S(2)}) collective-permute-start(bf16[256,128]{1,0:T(8,128)(2,1)S(1)} %get-tuple-element.124), channel_id=1, source_target_pairs={{0,4},{1,5},{2,6},{3,7},{4,0},{5,1},{6,2},{7,3},{8,12},{9,13},{10,... | collective-permute-start | bytes 196616 | tf_op jit(solution)/shard_map/ppermute | solution.py:315
  87.1 0.9 shard_map.97
  88.0 1.2 %collective-permute-done.29.refs_2_ = bf16[256,128]{1,0:T(8,128)(2,1)S(1)} collective-permute-done((bf16[256,128]{1,0:T(8,128)(2,1)S(1)}, bf16[256,128]{1,0:T(8,128)(2,1)S(1)}, u32[]{:S(2)}, u32[]{:S(2)}) %collective-permute-start.29) | collective-permute-done | bytes 65568 | tf_op jit(solution)/shard_map/ppermute | solution.py:315
  89.2 2.4 %collective-permute-done.30.refs_3_ = bf16[256,128]{1,0:T(8,128)(2,1)S(1)} collective-permute-done((bf16[256,128]{1,0:T(8,128)(2,1)S(1)}, bf16[256,128]{1,0:T(8,128)(2,1)S(1)}, u32[]{:S(2)}, u32[]{:S(2)}) %collective-permute-start.30) | collective-permute-done | bytes 65568 | tf_op jit(solution)/shard_map/ppermute | solution.py:315
  91.6 1.0 %shard_map.101 = f32[128,1024]{1,0:T(8,128)} custom-call(s32[1]{0:T(128)} %bitcast.place, f32[256,128]{1,0:T(8,128)S(1)} %get-tuple-element.122.refs_0_, bf16[256,128]{1,0:T(8,128)(2,1)S(1)} %collective-permute-done.28.refs_1_, bf16[256,128]{1,0:T(8,128)(2,1)S(1)} %collective-permute-done.29.refs_2_, bf16[256,128]{1,0:T(8,128)(2,1)S(1)} %collective-permute-done.30.refs_3_), custom_call_target="tpu_custom_call" | custom-call | bytes 851972 | tf_op jit(solution)/shard_map/pallas_call | solution.py:40
  (59 shorter events, 10.5 us)
Async XLA Ops:
  2.8 9.1 %collective-permute-start = (bf16[384,256]{1,0:T(8,128)(2,1)}, bf16[384,256]{1,0:T(8,128)(2,1)S(1)}, u32[]{:S(2)}, u32[]{:S(2)}) collective-permute-start(bf16[384,256]{1,0:T(8,128)(2,1)} %get-tuple-element.71), channel_id=1, source_target_pairs={{0,2},{1,3},{2,0},{3,1},{4,6},{5,7},{6,4},{7,5},{8,10},{9,11},{10,... | collective-permute-start | bytes 589832 | tf_op jit(solution)/shard_map/ppermute | solution.py:315
  5.8 12.2 %collective-permute-start.1 = (bf16[384,256]{1,0:T(8,128)(2,1)}, bf16[384,256]{1,0:T(8,128)(2,1)S(1)}, u32[]{:S(2)}, u32[]{:S(2)}) collective-permute-start(bf16[384,256]{1,0:T(8,128)(2,1)} %get-tuple-element.72), channel_id=1, source_target_pairs={{0,4},{1,5},{2,6},{3,7},{4,0},{5,1},{6,2},{7,3},{8,12},{9,13},{10,... | collective-permute-start | bytes 589832 | tf_op jit(solution)/shard_map/ppermute | solution.py:315
  7.3 10.7 %collective-permute-start.2 = (bf16[384,256]{1,0:T(8,128)(2,1)}, bf16[384,256]{1,0:T(8,128)(2,1)S(1)}, u32[]{:S(2)}, u32[]{:S(2)}) collective-permute-start(bf16[384,256]{1,0:T(8,128)(2,1)} %get-tuple-element.73), channel_id=1, source_target_pairs={{0,6},{1,7},{2,4},{3,5},{4,2},{5,3},{6,0},{7,1},{8,14},{9,15},{10,... | collective-permute-start | bytes 589832 | tf_op jit(solution)/shard_map/ppermute | solution.py:315
  7.4 31.7 %collective-permute-start.4 = (bf16[128,4096]{1,0:T(8,128)(2,1)}, bf16[128,4096]{1,0:T(8,128)(2,1)S(1)}, u32[]{:S(2)}, u32[]{:S(2)}) collective-permute-start(bf16[128,4096]{1,0:T(8,128)(2,1)} %refs_0_.4), channel_id=1, source_target_pairs={{0,4},{1,5},{2,6},{3,7},{4,0},{5,1},{6,2},{7,3},{8,12},{9,13},{10,... | collective-permute-start | bytes 3145736 | tf_op jit(solution)/shard_map/ppermute | solution.py:315
  9.3 29.7 %collective-permute-start.3 = (bf16[128,4096]{1,0:T(8,128)(2,1)}, bf16[128,4096]{1,0:T(8,128)(2,1)S(1)}, u32[]{:S(2)}, u32[]{:S(2)}) collective-permute-start(bf16[128,4096]{1,0:T(8,128)(2,1)} %refs_0_.4), channel_id=1, source_target_pairs={{0,2},{1,3},{2,0},{3,1},{4,6},{5,7},{6,4},{7,5},{8,10},{9,11},{10,... | collective-permute-start | bytes 3145736 | tf_op jit(solution)/shard_map/ppermute | solution.py:315
  18.3 25.9 %copy-start = (bf16[128,4096]{1,0:T(8,128)(2,1)S(1)}, bf16[128,4096]{1,0:T(8,128)(2,1)}, u32[]{:S(2)}) copy-start(bf16[128,4096]{1,0:T(8,128)(2,1)} %refs_0_.4) | copy-start | bytes 3145732
  18.3 14.9 %collective-permute-start.6 = (bf16[640,256]{1,0:T(8,128)(2,1)S(1)}, bf16[640,256]{1,0:T(8,128)(2,1)S(1)}, u32[]{:S(2)}, u32[]{:S(2)}) collective-permute-start(bf16[640,256]{1,0:T(8,128)(2,1)S(1)} %get-tuple-element.81.refs_6_), channel_id=1, source_target_pairs={{0,16},{1,17},{2,18},{3,19},{4,20},{5,21},{6,22},{7,23},{8,24},{9,... | collective-permute-start | bytes 983048 | tf_op jit(solution)/shard_map/ppermute | solution.py:315
  21.0 12.9 %collective-permute-start.5 = (bf16[640,256]{1,0:T(8,128)(2,1)S(1)}, bf16[640,256]{1,0:T(8,128)(2,1)S(1)}, u32[]{:S(2)}, u32[]{:S(2)}) collective-permute-start(bf16[640,256]{1,0:T(8,128)(2,1)S(1)} %get-tuple-element.81.refs_6_), channel_id=1, source_target_pairs={{0,8},{1,9},{2,10},{3,11},{4,12},{5,13},{6,14},{7,15},{8,0},{9,1},... | collective-permute-start | bytes 983048 | tf_op jit(solution)/shard_map/ppermute | solution.py:315
  33.3 8.5 %collective-permute-start.7 = (bf16[640,256]{1,0:T(8,128)(2,1)S(1)}, bf16[640,256]{1,0:T(8,128)(2,1)S(1)}, u32[]{:S(2)}, u32[]{:S(2)}) collective-permute-start(bf16[640,256]{1,0:T(8,128)(2,1)S(1)} %collective-permute-done.6.refs_8_), channel_id=1, source_target_pairs={{0,8},{1,9},{2,10},{3,11},{4,12},{5,13},{6,14},{7,15},{8,0},{9,1},... | collective-permute-start | bytes 983048 | tf_op jit(solution)/shard_map/ppermute | solution.py:315
  33.9 7.9 %collective-permute-start.10 = (bf16[640,256]{1,0:T(8,128)(2,1)S(1)}, bf16[640,256]{1,0:T(8,128)(2,1)S(1)}, u32[]{:S(2)}, u32[]{:S(2)}) collective-permute-start(bf16[640,256]{1,0:T(8,128)(2,1)S(1)} %collective-permute-done.6.refs_8_), channel_id=1, source_target_pairs={{0,1},{1,0},{2,3},{3,2},{4,5},{5,4},{6,7},{7,6},{8,9},{9,8},{10,11... | collective-permute-start | bytes 983048 | tf_op jit(solution)/shard_map/ppermute | solution.py:315
  33.9 8.4 %collective-permute-start.9 = (bf16[640,256]{1,0:T(8,128)(2,1)S(1)}, bf16[640,256]{1,0:T(8,128)(2,1)S(1)}, u32[]{:S(2)}, u32[]{:S(2)}) collective-permute-start(bf16[640,256]{1,0:T(8,128)(2,1)S(1)} %collective-permute-done.5.refs_7_), channel_id=1, source_target_pairs={{0,1},{1,0},{2,3},{3,2},{4,5},{5,4},{6,7},{7,6},{8,9},{9,8},{10,11... | collective-permute-start | bytes 983048 | tf_op jit(solution)/shard_map/ppermute | solution.py:315
  39.2 12.5 %collective-permute-start.14 = (bf16[64,4096]{1,0:T(8,128)(2,1)S(1)}, bf16[64,4096]{1,0:T(8,128)(2,1)S(1)}, u32[]{:S(2)}, u32[]{:S(2)}) collective-permute-start(bf16[64,4096]{1,0:T(8,128)(2,1)S(1)} %slice.10), channel_id=1, source_target_pairs={{0,2},{1,3},{2,0},{3,1},{4,6},{5,7},{6,4},{7,5},{8,10},{9,11},{10,... | collective-permute-start | bytes 1572872 | tf_op jit(solution)/shard_map/ppermute | solution.py:315
  39.6 12.5 %collective-permute-start.13 = (bf16[64,4096]{1,0:T(8,128)(2,1)S(1)}, bf16[64,4096]{1,0:T(8,128)(2,1)S(1)}, u32[]{:S(2)}, u32[]{:S(2)}) collective-permute-start(bf16[64,4096]{1,0:T(8,128)(2,1)S(1)} %slice.9), channel_id=1, source_target_pairs={{0,4},{1,5},{2,6},{3,7},{4,0},{5,1},{6,2},{7,3},{8,12},{9,13},{10,... | collective-permute-start | bytes 1572872 | tf_op jit(solution)/shard_map/ppermute | solution.py:315
  41.8 1.6 %collective-permute-start.11 = (bf16[640,256]{1,0:T(8,128)(2,1)S(1)}, bf16[640,256]{1,0:T(8,128)(2,1)S(1)}, u32[]{:S(2)}, u32[]{:S(2)}) collective-permute-start(bf16[640,256]{1,0:T(8,128)(2,1)S(1)} %collective-permute-done.7.refs_9_), channel_id=1, source_target_pairs={{0,1},{1,0},{2,3},{3,2},{4,5},{5,4},{6,7},{7,6},{8,9},{9,8},{10,11... | collective-permute-start | bytes 983048 | tf_op jit(solution)/shard_map/ppermute | solution.py:315
  41.8 2.5 %collective-permute-start.8 = (bf16[640,256]{1,0:T(8,128)(2,1)S(1)}, bf16[640,256]{1,0:T(8,128)(2,1)S(1)}, u32[]{:S(2)}, u32[]{:S(2)}) collective-permute-start(bf16[640,256]{1,0:T(8,128)(2,1)S(1)} %get-tuple-element.81.refs_6_), channel_id=1, source_target_pairs={{0,1},{1,0},{2,3},{3,2},{4,5},{5,4},{6,7},{7,6},{8,9},{9,8},{10,11... | collective-permute-start | bytes 983048 | tf_op jit(solution)/shard_map/ppermute | solution.py:315
  42.3 2.0 %collective-permute-start.12 = (bf16[4,256,128]{2,1,0:T(8,128)(2,1)S(1)}, bf16[4,256,128]{2,1,0:T(8,128)(2,1)S(1)}, u32[]{:S(2)}, u32[]{:S(2)}) collective-permute-start(bf16[4,256,128]{2,1,0:T(8,128)(2,1)S(1)} %get-tuple-element.82.refs_14_), channel_id=1, source_target_pairs={{0,1},{1,0},{2,3},{3,2},{4,5},{5,4},{6,7},{7,6},{8,9},{9,8},{10,11... | collective-permute-start | bytes 786440 | tf_op jit(solution)/shard_map/ppermute | solution.py:315
  54.0 1.9 %collective-permute-start.15 = (bf16[4,256,128]{2,1,0:T(8,128)(2,1)S(1)}, bf16[4,256,128]{2,1,0:T(8,128)(2,1)S(1)}, u32[]{:S(2)}, u32[]{:S(2)}) collective-permute-start(bf16[4,256,128]{2,1,0:T(8,128)(2,1)S(1)} %get-tuple-element.101.refs_0_.refs_10_), channel_id=1, source_target_pairs={{0,1},{1,0},{2,3},{3,2},{4,5},{5,4},{6,7},{7,6},{8,9},{9,8},{10,11... | collective-permute-start | bytes 786440 | tf_op jit(solution)/shard_map/ppermute | solution.py:315
  54.5 1.7 %collective-permute-start.16 = (bf16[256,512]{1,0:T(8,128)(2,1)S(1)}, bf16[256,512]{1,0:T(8,128)(2,1)S(1)}, u32[]{:S(2)}, u32[]{:S(2)}) collective-permute-start(bf16[256,512]{1,0:T(8,128)(2,1)S(1)} %get-tuple-element.105), channel_id=1, source_target_pairs={{0,1},{1,0},{2,3},{3,2},{4,5},{5,4},{6,7},{7,6},{8,9},{9,8},{10,11... | collective-permute-start | bytes 786440 | tf_op jit(solution)/shard_map/ppermute | solution.py:315
  55.6 4.3 %collective-permute-start.18 = (bf16[256,512]{1,0:T(8,128)(2,1)S(1)}, bf16[256,512]{1,0:T(8,128)(2,1)S(1)}, u32[]{:S(2)}, u32[]{:S(2)}) collective-permute-start(bf16[256,512]{1,0:T(8,128)(2,1)S(1)} %get-tuple-element.108), channel_id=1, source_target_pairs={{0,1},{1,0},{2,3},{3,2},{4,5},{5,4},{6,7},{7,6},{8,9},{9,8},{10,11... | collective-permute-start | bytes 786440 | tf_op jit(solution)/shard_map/ppermute | solution.py:315
  56.4 9.9 %collective-permute-start.17 = (bf16[288,512]{1,0:T(8,128)(2,1)S(1)}, bf16[288,512]{1,0:T(8,128)(2,1)S(1)}, u32[]{:S(2)}, u32[]{:S(2)}) collective-permute-start(bf16[288,512]{1,0:T(8,128)(2,1)S(1)} %get-tuple-element.106), channel_id=1, source_target_pairs={{0,8},{1,9},{2,10},{3,11},{4,12},{5,13},{6,14},{7,15},{8,0},{9,1},... | collective-permute-start | bytes 884744 | tf_op jit(solution)/shard_map/ppermute | solution.py:315
  58.5 10.4 %collective-permute-start.26 = (bf16[256,512]{1,0:T(8,128)(2,1)S(1)}, bf16[256,512]{1,0:T(8,128)(2,1)S(1)}, u32[]{:S(2)}, u32[]{:S(2)}) collective-permute-start(bf16[256,512]{1,0:T(8,128)(2,1)S(1)} %get-tuple-element.121), channel_id=1, source_target_pairs={{0,1},{1,0},{2,3},{3,2},{4,5},{5,4},{6,7},{7,6},{8,9},{9,8},{10,11... | collective-permute-start | bytes 786440 | tf_op jit(solution)/shard_map/ppermute | solution.py:315
  59.1 12.7 %collective-permute-start.24 = (bf16[256,512]{1,0:T(8,128)(2,1)S(1)}, bf16[256,512]{1,0:T(8,128)(2,1)S(1)}, u32[]{:S(2)}, u32[]{:S(2)}) collective-permute-start(bf16[256,512]{1,0:T(8,128)(2,1)S(1)} %get-tuple-element.119), channel_id=1, source_target_pairs={{0,1},{1,0},{2,3},{3,2},{4,5},{5,4},{6,7},{7,6},{8,9},{9,8},{10,11... | collective-permute-start | bytes 786440 | tf_op jit(solution)/shard_map/ppermute | solution.py:315
  60.0 17.3 %collective-permute-start.25 = (bf16[256,512]{1,0:T(8,128)(2,1)S(1)}, bf16[256,512]{1,0:T(8,128)(2,1)S(1)}, u32[]{:S(2)}, u32[]{:S(2)}) collective-permute-start(bf16[256,512]{1,0:T(8,128)(2,1)S(1)} %add_convert_fusion.1), channel_id=1, source_target_pairs={{0,8},{1,9},{2,10},{3,11},{4,12},{5,13},{6,14},{7,15},{8,0},{9,1},... | collective-permute-start | bytes 786440 | tf_op jit(solution)/shard_map/ppermute | solution.py:315
  66.3 5.4 %collective-permute-start.19 = (bf16[128,128]{1,0:T(8,128)(2,1)S(1)}, bf16[128,128]{1,0:T(8,128)(2,1)S(1)}, u32[]{:S(2)}, u32[]{:S(2)}) collective-permute-start(bf16[128,128]{1,0:T(8,128)(2,1)S(1)} %get-tuple-element.112), channel_id=1, source_target_pairs={{0,16},{1,17},{2,18},{3,19},{4,20},{5,21},{6,22},{7,23},{8,24},{9,... | collective-permute-start | bytes 98312 | tf_op jit(solution)/shard_map/ppermute | solution.py:315
  69.1 14.2 %collective-permute-start.27 = (bf16[256,512]{1,0:T(8,128)(2,1)S(1)}, bf16[256,512]{1,0:T(8,128)(2,1)S(1)}, u32[]{:S(2)}, u32[]{:S(2)}) collective-permute-start(bf16[256,512]{1,0:T(8,128)(2,1)S(1)} %add_convert_fusion), channel_id=1, source_target_pairs={{0,16},{1,17},{2,18},{3,19},{4,20},{5,21},{6,22},{7,23},{8,24},{9,... | collective-permute-start | bytes 786440 | tf_op jit(solution)/shard_map/ppermute | solution.py:315
  71.7 1.3 %collective-permute-start.20 = (bf16[128,128]{1,0:T(8,128)(2,1)S(1)}, bf16[128,128]{1,0:T(8,128)(2,1)S(1)}, u32[]{:S(2)}, u32[]{:S(2)}) collective-permute-start(bf16[128,128]{1,0:T(8,128)(2,1)S(1)} %shard_map.95.refs_12_), channel_id=1, source_target_pairs={{0,1},{1,0},{2,3},{3,2},{4,5},{5,4},{6,7},{7,6},{8,9},{9,8},{10,11... | collective-permute-start | bytes 98312 | tf_op jit(solution)/shard_map/ppermute | solution.py:315
  73.7 12.7 %collective-permute-start.21 = (bf16[128,512]{1,0:T(8,128)(2,1)S(1)}, bf16[128,512]{1,0:T(8,128)(2,1)S(1)}, u32[]{:S(2)}, u32[]{:S(2)}) collective-permute-start(bf16[128,512]{1,0:T(8,128)(2,1)S(1)} %get-tuple-element.114), channel_id=1, source_target_pairs={{0,2},{1,3},{2,0},{3,1},{4,6},{5,7},{6,4},{7,5},{8,10},{9,11},{10,... | collective-permute-start | bytes 393224 | tf_op jit(solution)/shard_map/ppermute | solution.py:315
  75.1 11.9 %collective-permute-start.22 = (bf16[128,512]{1,0:T(8,128)(2,1)S(1)}, bf16[128,512]{1,0:T(8,128)(2,1)S(1)}, u32[]{:S(2)}, u32[]{:S(2)}) collective-permute-start(bf16[128,512]{1,0:T(8,128)(2,1)S(1)} %get-tuple-element.115), channel_id=1, source_target_pairs={{0,4},{1,5},{2,6},{3,7},{4,0},{5,1},{6,2},{7,3},{8,12},{9,13},{10,... | collective-permute-start | bytes 393224 | tf_op jit(solution)/shard_map/ppermute | solution.py:315
  76.6 10.4 %collective-permute-start.23 = (bf16[128,512]{1,0:T(8,128)(2,1)S(1)}, bf16[128,512]{1,0:T(8,128)(2,1)S(1)}, u32[]{:S(2)}, u32[]{:S(2)}) collective-permute-start(bf16[128,512]{1,0:T(8,128)(2,1)S(1)} %get-tuple-element.116), channel_id=1, source_target_pairs={{0,6},{1,7},{2,4},{3,5},{4,2},{5,3},{6,0},{7,1},{8,14},{9,15},{10,... | collective-permute-start | bytes 393224 | tf_op jit(solution)/shard_map/ppermute | solution.py:315
  83.5 4.5 %collective-permute-start.28 = (bf16[256,128]{1,0:T(8,128)(2,1)S(1)}, bf16[256,128]{1,0:T(8,128)(2,1)S(1)}, u32[]{:S(2)}, u32[]{:S(2)}) collective-permute-start(bf16[256,128]{1,0:T(8,128)(2,1)S(1)} %get-tuple-element.123), channel_id=1, source_target_pairs={{0,2},{1,3},{2,0},{3,1},{4,6},{5,7},{6,4},{7,5},{8,10},{9,11},{10,... | collective-permute-start | bytes 196616 | tf_op jit(solution)/shard_map/ppermute | solution.py:315
  84.9 4.3 %collective-permute-start.29 = (bf16[256,128]{1,0:T(8,128)(2,1)S(1)}, bf16[256,128]{1,0:T(8,128)(2,1)S(1)}, u32[]{:S(2)}, u32[]{:S(2)}) collective-permute-start(bf16[256,128]{1,0:T(8,128)(2,1)S(1)} %get-tuple-element.124), channel_id=1, source_target_pairs={{0,4},{1,5},{2,6},{3,7},{4,0},{5,1},{6,2},{7,3},{8,12},{9,13},{10,... | collective-permute-start | bytes 196616 | tf_op jit(solution)/shard_map/ppermute | solution.py:315
  86.4 5.2 %collective-permute-start.30 = (bf16[256,128]{1,0:T(8,128)(2,1)S(1)}, bf16[256,128]{1,0:T(8,128)(2,1)S(1)}, u32[]{:S(2)}, u32[]{:S(2)}) collective-permute-start(bf16[256,128]{1,0:T(8,128)(2,1)S(1)} %get-tuple-element.125), channel_id=1, source_target_pairs={{0,6},{1,7},{2,4},{3,5},{4,2},{5,3},{6,0},{7,1},{8,14},{9,15},{10,... | collective-permute-start | bytes 196616 | tf_op jit(solution)/shard_map/ppermute | solution.py:315
  (2 other events, 26.9 us)

commit v6 on v5

--- a/solution.py
+++ b/solution.py
@@ -17,6 +17,7 @@
 BF16 = jnp.bfloat16
 HALF = FEAT // 2
 URGENT = 1 << 35
+HOPS = (3, 2, 1, 0)
 
 
 def dot(a, b, dims=((1,), (0,))):
@@ -84,7 +85,7 @@
     state[...] = state_of(p, rows, depth)
 
 
-def state_kernel(rows, depth, place, shard, own_state, p1, p2, p3, pay, states):
+def state_kernel(rows, depth, place, shard, own_state, p3, p2, p1, pay, states):
     pay[:depth, :] = shard[...]
     total = own_state[...]
     states[0] = total.astype(BF16)
@@ -255,7 +256,7 @@
 def query_grad_kernel(place, *refs):
     out = refs[-1]
     q, _, _ = seat(place)
-    for k, ref in enumerate(refs[:-1]):
+    for k, ref in zip(HOPS, refs[:-1]):
         out[:, lanes(q ^ k, FEAT)] = ref[...].astype(F32).T
 
 
@@ -293,7 +294,7 @@
 def place_kernel(place, *refs):
     att, key_grad, val_grad = refs[-3:]
     q, _, _ = seat(place)
-    for k, ref in enumerate(refs[:-3]):
+    for k, ref in zip(HOPS, refs[:-3]):
         head = q ^ k
         att[:, lanes(head, HEAD_DIM)] = ref[:, :HEAD_DIM]
         val_grad[:, lanes(head, HEAD_DIM)] = ref[:, HEAD_DIM : 2 * HEAD_DIM]
@@ -342,7 +343,7 @@
     pay, states = call(
         functools.partial(state_kernel, rows, depth),
         [((4 * depth + HALF, FEAT), BF16), ((4, FEAT, HEAD_DIM), BF16)],
-        [place, *start, *p[1:]],
+        [place, *start, *(p[k] for k in HOPS[:3])],
         urgent=URGENT,
     )
     pays = [pay] + [None] * (outer - 1)
@@ -454,7 +455,7 @@
             ((rows, HEADS_GROUP * FEAT), BF16),
             ((rows, HEADS_GROUP * HEAD_DIM), BF16),
         ],
-        [place, *placed],
+        [place, *(placed[k] for k in HOPS)],
     )
     blocks = call(
         functools.partial(sum_kernel, depth),
@@ -465,7 +466,7 @@
     )
     columns = [blocks[0]] + [chip_swap(blocks[k], k) for k in (1, 2, 3)]
     (query_grad,) = call(
-        query_grad_kernel, [((depth, HEADS_GROUP * FEAT), F32)], [place, *columns]
+        query_grad_kernel, [((depth, HEADS_GROUP * FEAT), F32)], [place, *(columns[k] for k in HOPS)]
     )
     return (attended, query_grad, key_grad, value_grad)
 

time: 92.8 us -> 91.8 us (0.989)
  waiting for transfers between devices: 47.2 us -> 46.2 us
    ppermute x31, waiting for transfers between devices: 47.2 us -> 46.2 us  [swap(): return lax.ppermute(block, 'ctx', [(i, i ^ bits) for i in range(count)])]
where the time goes in v6:
time: 91.8 us; the launch traced here: 91.6 us
  waiting for transfers between devices  46.2 us (50%)
  starting transfers between devices  29.8 us (32%)
  Pallas kernels  13.5 us (15%)
  local copies, waits for them, and re-layouts  1.01 us (1%)
    ppermute x31, waiting for transfers between devices, swap(): return lax.ppermute(block, 'ctx', [(i, i ^ bits) for i in range(count)])  46.2 us
    ppermute x31, starting transfers between devices, swap(): return lax.ppermute(block, 'ctx', [(i, i ^ bits) for i in range(count)])  29.8 us
    pallas_call x18, Pallas kernels, call(): pl.pallas_call(kernel, out_shape=shapes, in_specs=[pl.BlockSpec(memory_sp...  13.5 us
  transfers between devices with their start and end apart: 31, of which 16 were waited for; matrix products, arithmetic and copies ran while one was open for 0% of the time, Pallas kernels for 9%

profile of v6, /device:TPU:0, one launch (start us, length us, event | category | flops | bytes accessed | tf_op | source)
XLA Modules:
  0.0 91.6 jit_solution(9081760815240272134)
XLA Ops:
  0.6 2.2 %shard_map.84 = (bf16[384,256]{1,0:T(8,128)(2,1)}, bf16[384,256]{1,0:T(8,128)(2,1)}, bf16[384,256]{1,0:T(8,128)(2,1)}, bf16[384,256]{1,0:T(8,128)(2,1)}) custom-call(s32[1]{0:T(128)} %bitcast.place, bf16[128,1024]{1,0:T(8,128)(2,1)} %w.1, bf16[128,1024]{1,0:T(8,128)(2,1)} %key.1, bf16[128,512]{1,0:T(8,128)(2,1)} %val.1, bf16[128,512]{1,0:T(8,128)(2,1)} %cot.1), custom_call_target="tpu_custom_call" | custom-call | bytes 1572868 | tf_op jit(solution)/shard_map/pallas_call | solution.py:41
  2.8 3.0 %collective-permute-start = (bf16[384,256]{1,0:T(8,128)(2,1)}, bf16[384,256]{1,0:T(8,128)(2,1)S(1)}, u32[]{:S(2)}, u32[]{:S(2)}) collective-permute-start(bf16[384,256]{1,0:T(8,128)(2,1)} %get-tuple-element.71), channel_id=1, source_target_pairs={{0,2},{1,3},{2,0},{3,1},{4,6},{5,7},{6,4},{7,5},{8,10},{9,11},{10,... | collective-permute-start | bytes 589832 | tf_op jit(solution)/shard_map/ppermute | solution.py:316
  5.8 1.5 %collective-permute-start.1 = (bf16[384,256]{1,0:T(8,128)(2,1)}, bf16[384,256]{1,0:T(8,128)(2,1)S(1)}, u32[]{:S(2)}, u32[]{:S(2)}) collective-permute-start(bf16[384,256]{1,0:T(8,128)(2,1)} %get-tuple-element.72), channel_id=1, source_target_pairs={{0,4},{1,5},{2,6},{3,7},{4,0},{5,1},{6,2},{7,3},{8,12},{9,13},{10,... | collective-permute-start | bytes 589832 | tf_op jit(solution)/shard_map/ppermute | solution.py:316
  7.4 2.0 %collective-permute-start.4 = (bf16[128,4096]{1,0:T(8,128)(2,1)}, bf16[128,4096]{1,0:T(8,128)(2,1)S(1)}, u32[]{:S(2)}, u32[]{:S(2)}) collective-permute-start(bf16[128,4096]{1,0:T(8,128)(2,1)} %refs_0_.4), channel_id=1, source_target_pairs={{0,4},{1,5},{2,6},{3,7},{4,0},{5,1},{6,2},{7,3},{8,12},{9,13},{10,... | collective-permute-start | bytes 3145736 | tf_op jit(solution)/shard_map/ppermute | solution.py:316
  9.3 1.5 %collective-permute-start.3 = (bf16[128,4096]{1,0:T(8,128)(2,1)}, bf16[128,4096]{1,0:T(8,128)(2,1)S(1)}, u32[]{:S(2)}, u32[]{:S(2)}) collective-permute-start(bf16[128,4096]{1,0:T(8,128)(2,1)} %refs_0_.4), channel_id=1, source_target_pairs={{0,2},{1,3},{2,0},{3,1},{4,6},{5,7},{6,4},{7,5},{8,10},{9,11},{10,... | collective-permute-start | bytes 3145736 | tf_op jit(solution)/shard_map/ppermute | solution.py:316
  10.8 0.9 %copy-done.1 = bf16[384,256]{1,0:T(8,128)(2,1)S(1)} copy-done((bf16[384,256]{1,0:T(8,128)(2,1)S(1)}, bf16[384,256]{1,0:T(8,128)(2,1)}, u32[]{:S(2)}) %copy-start.1) | copy-done | bytes 196632
  12.0 6.1 %collective-permute-done.1.p2.refs_5_.refs_2_ = bf16[384,256]{1,0:T(8,128)(2,1)S(1)} collective-permute-done((bf16[384,256]{1,0:T(8,128)(2,1)}, bf16[384,256]{1,0:T(8,128)(2,1)S(1)}, u32[]{:S(2)}, u32[]{:S(2)}) %collective-permute-start.1) | collective-permute-done | bytes 196640 | tf_op jit(solution)/shard_map/ppermute | solution.py:316
  18.3 2.7 %collective-permute-start.6 = (bf16[640,256]{1,0:T(8,128)(2,1)S(1)}, bf16[640,256]{1,0:T(8,128)(2,1)S(1)}, u32[]{:S(2)}, u32[]{:S(2)}) collective-permute-start(bf16[640,256]{1,0:T(8,128)(2,1)S(1)} %get-tuple-element.81.refs_6_), channel_id=1, source_target_pairs={{0,16},{1,17},{2,18},{3,19},{4,20},{5,21},{6,22},{7,23},{8,24},{9,... | collective-permute-start | bytes 983048 | tf_op jit(solution)/shard_map/ppermute | solution.py:316
  21.0 1.6 %collective-permute-start.5 = (bf16[640,256]{1,0:T(8,128)(2,1)S(1)}, bf16[640,256]{1,0:T(8,128)(2,1)S(1)}, u32[]{:S(2)}, u32[]{:S(2)}) collective-permute-start(bf16[640,256]{1,0:T(8,128)(2,1)S(1)} %get-tuple-element.81.refs_6_), channel_id=1, source_target_pairs={{0,8},{1,9},{2,10},{3,11},{4,12},{5,13},{6,14},{7,15},{8,0},{9,1},... | collective-permute-start | bytes 983048 | tf_op jit(solution)/shard_map/ppermute | solution.py:316
  22.6 10.7 %collective-permute-done.6.refs_8_ = bf16[640,256]{1,0:T(8,128)(2,1)S(1)} collective-permute-done((bf16[640,256]{1,0:T(8,128)(2,1)S(1)}, bf16[640,256]{1,0:T(8,128)(2,1)S(1)}, u32[]{:S(2)}, u32[]{:S(2)}) %collective-permute-start.6) | collective-permute-done | bytes 327712 | tf_op jit(solution)/shard_map/ppermute | solution.py:316
  34.4 4.7 %collective-permute-done.4.refs_2_ = bf16[128,4096]{1,0:T(8,128)(2,1)S(1)} collective-permute-done((bf16[128,4096]{1,0:T(8,128)(2,1)}, bf16[128,4096]{1,0:T(8,128)(2,1)S(1)}, u32[]{:S(2)}, u32[]{:S(2)}) %collective-permute-start.4) | collective-permute-done | bytes 1048608 | tf_op jit(solution)/shard_map/ppermute | solution.py:316
  39.6 1.7 %collective-permute-start.13 = (bf16[64,4096]{1,0:T(8,128)(2,1)S(1)}, bf16[64,4096]{1,0:T(8,128)(2,1)S(1)}, u32[]{:S(2)}, u32[]{:S(2)}) collective-permute-start(bf16[64,4096]{1,0:T(8,128)(2,1)S(1)} %slice.9), channel_id=1, source_target_pairs={{0,4},{1,5},{2,6},{3,7},{4,0},{5,1},{6,2},{7,3},{8,12},{9,13},{10,... | collective-permute-start | bytes 1572872 | tf_op jit(solution)/shard_map/ppermute | solution.py:316
  42.4 1.0 %collective-permute-done.11.refs_13_ = bf16[640,256]{1,0:T(8,128)(2,1)S(1)} collective-permute-done((bf16[640,256]{1,0:T(8,128)(2,1)S(1)}, bf16[640,256]{1,0:T(8,128)(2,1)S(1)}, u32[]{:S(2)}, u32[]{:S(2)}) %collective-permute-start.11) | collective-permute-done | bytes 327712 | tf_op jit(solution)/shard_map/ppermute | solution.py:316
  43.4 0.8 collective-permute-done.12.refs_15_
  44.3 3.8 %shard_map.87 = (bf16[3,128,128]{2,1,0:T(8,128)(2,1)S(1)}, bf16[256,384]{1,0:T(8,128)(2,1)S(1)}, bf16[3,256,128]{2,1,0:T(8,128)(2,1)S(1)}, bf16[3,128,256]{2,1,0...) custom-call(s32[1]{0:T(128)} %bitcast.place, ...), custom_call_target="tpu_custom_call" | custom-call | flops 805306368 | bytes 10092548 | tf_op jit(solution)/shard_map/pallas_call | solution.py:41
  48.0 3.7 %collective-permute-done.14.bottom.refs_4_ = bf16[64,4096]{1,0:T(8,128)(2,1)S(1)} collective-permute-done((bf16[64,4096]{1,0:T(8,128)(2,1)S(1)}, bf16[64,4096]{1,0:T(8,128)(2,1)S(1)}, u32[]{:S(2)}, u32[]{:S(2)}) %collective-permute-start.14) | collective-permute-done | bytes 524320 | tf_op jit(solution)/shard_map/ppermute | solution.py:316
  52.1 1.9 %shard_map.89 = (bf16[1,128,128]{2,1,0:T(8,128)(2,1)S(1)}, bf16[256,128]{1,0:T(8,128)(2,1)S(1)}, bf16[1,256,128]{2,1,0:T(8,128)(2,1)}, bf16[1,128,256]{2,1,0:T(8...) custom-call(s32[1]{0:T(128)} %bitcast.place, ...), custom_call_target="tpu_custom_call" | custom-call | flops 268435456 | bytes 4259844 | tf_op jit(solution)/shard_map/pallas_call | solution.py:41
  56.4 1.6 %collective-permute-start.17 = (bf16[288,512]{1,0:T(8,128)(2,1)S(1)}, bf16[288,512]{1,0:T(8,128)(2,1)S(1)}, u32[]{:S(2)}, u32[]{:S(2)}) collective-permute-start(bf16[288,512]{1,0:T(8,128)(2,1)S(1)} %get-tuple-element.106), channel_id=1, source_target_pairs={{0,8},{1,9},{2,10},{3,11},{4,12},{5,13},{6,14},{7,15},{8,0},{9,1},... | collective-permute-start | bytes 884744 | tf_op jit(solution)/shard_map/ppermute | solution.py:316
  60.5 5.9 %collective-permute-done.17.load = bf16[288,512]{1,0:T(8,128)(2,1)S(1)} collective-permute-done((bf16[288,512]{1,0:T(8,128)(2,1)S(1)}, bf16[288,512]{1,0:T(8,128)(2,1)S(1)}, u32[]{:S(2)}, u32[]{:S(2)}) %collective-permute-start.17) | collective-permute-done | bytes 294944 | tf_op jit(solution)/shard_map/ppermute | solution.py:316
  66.3 2.6 %collective-permute-start.19 = (bf16[128,128]{1,0:T(8,128)(2,1)S(1)}, bf16[128,128]{1,0:T(8,128)(2,1)S(1)}, u32[]{:S(2)}, u32[]{:S(2)}) collective-permute-start(bf16[128,128]{1,0:T(8,128)(2,1)S(1)} %get-tuple-element.112), channel_id=1, source_target_pairs={{0,16},{1,17},{2,18},{3,19},{4,20},{5,21},{6,22},{7,23},{8,24},{9,... | collective-permute-start | bytes 98312 | tf_op jit(solution)/shard_map/ppermute | solution.py:316
  69.5 2.2 %collective-permute-done.19.refs_1_ = bf16[128,128]{1,0:T(8,128)(2,1)S(1)} collective-permute-done((bf16[128,128]{1,0:T(8,128)(2,1)S(1)}, bf16[128,128]{1,0:T(8,128)(2,1)S(1)}, u32[]{:S(2)}, u32[]{:S(2)}) %collective-permute-start.19) | collective-permute-done | bytes 32800 | tf_op jit(solution)/shard_map/ppermute | solution.py:316
  71.9 1.1 %collective-permute-done.20.refs_13_ = bf16[128,128]{1,0:T(8,128)(2,1)S(1)} collective-permute-done((bf16[128,128]{1,0:T(8,128)(2,1)S(1)}, bf16[128,128]{1,0:T(8,128)(2,1)S(1)}, u32[]{:S(2)}, u32[]{:S(2)}) %collective-permute-start.20) | collective-permute-done | bytes 32800 | tf_op jit(solution)/shard_map/ppermute | solution.py:316
  73.0 0.7 shard_map.96
  73.7 2.4 %collective-permute-start.21 = (bf16[128,512]{1,0:T(8,128)(2,1)S(1)}, bf16[128,512]{1,0:T(8,128)(2,1)S(1)}, u32[]{:S(2)}, u32[]{:S(2)}) collective-permute-start(bf16[128,512]{1,0:T(8,128)(2,1)S(1)} %get-tuple-element.113), channel_id=1, source_target_pairs={{0,6},{1,7},{2,4},{3,5},{4,2},{5,3},{6,0},{7,1},{8,14},{9,15},{10,... | collective-permute-start | bytes 393224 | tf_op jit(solution)/shard_map/ppermute | solution.py:316
  76.6 0.7 collective-permute-start.23
  77.3 6.1 %collective-permute-done.27.refs_1_ = bf16[256,512]{1,0:T(8,128)(2,1)S(1)} collective-permute-done((bf16[256,512]{1,0:T(8,128)(2,1)S(1)}, bf16[256,512]{1,0:T(8,128)(2,1)S(1)}, u32[]{:S(2)}, u32[]{:S(2)}) %collective-permute-start.27) | collective-permute-done | bytes 262176 | tf_op jit(solution)/shard_map/ppermute | solution.py:316
  83.5 2.4 %collective-permute-start.28 = (bf16[256,128]{1,0:T(8,128)(2,1)S(1)}, bf16[256,128]{1,0:T(8,128)(2,1)S(1)}, u32[]{:S(2)}, u32[]{:S(2)}) collective-permute-start(bf16[256,128]{1,0:T(8,128)(2,1)S(1)} %get-tuple-element.122), channel_id=1, source_target_pairs={{0,6},{1,7},{2,4},{3,5},{4,2},{5,3},{6,0},{7,1},{8,14},{9,15},{10,... | collective-permute-start | bytes 196616 | tf_op jit(solution)/shard_map/ppermute | solution.py:316
  86.4 0.7 collective-permute-start.30
  87.1 0.9 shard_map.97
  87.9 1.1 %collective-permute-done.28.refs_0_ = bf16[256,128]{1,0:T(8,128)(2,1)S(1)} collective-permute-done((bf16[256,128]{1,0:T(8,128)(2,1)S(1)}, bf16[256,128]{1,0:T(8,128)(2,1)S(1)}, u32[]{:S(2)}, u32[]{:S(2)}) %collective-permute-start.28) | collective-permute-done | bytes 65568 | tf_op jit(solution)/shard_map/ppermute | solution.py:316
  89.0 1.2 %collective-permute-done.29.refs_1_ = bf16[256,128]{1,0:T(8,128)(2,1)S(1)} collective-permute-done((bf16[256,128]{1,0:T(8,128)(2,1)S(1)}, bf16[256,128]{1,0:T(8,128)(2,1)S(1)}, u32[]{:S(2)}, u32[]{:S(2)}) %collective-permute-start.29) | collective-permute-done | bytes 65568 | tf_op jit(solution)/shard_map/ppermute | solution.py:316
  90.7 1.0 %shard_map.101 = f32[128,1024]{1,0:T(8,128)} custom-call(s32[1]{0:T(128)} %bitcast.place, bf16[256,128]{1,0:T(8,128)(2,1)S(1)} %collective-permute-done.28.refs_0_, bf16[256,128]{1,0:T(8,128)(2,1)S(1)} %collective-permute-done.29.refs_1_, bf16[256,128]{1,0:T(8,128)(2,1)S(1)} %collective-permute-done.30.refs_2_, f32[256,128]{1,0:T(8,128)S(1)} %get-tuple-element.125.refs_3_), custom_call_target="tpu_custom_call" | custom-call | bytes 851972 | tf_op jit(solution)/shard_map/pallas_call | solution.py:41
  (59 shorter events, 10.7 us)
Async XLA Ops:
  2.8 9.1 %collective-permute-start = (bf16[384,256]{1,0:T(8,128)(2,1)}, bf16[384,256]{1,0:T(8,128)(2,1)S(1)}, u32[]{:S(2)}, u32[]{:S(2)}) collective-permute-start(bf16[384,256]{1,0:T(8,128)(2,1)} %get-tuple-element.71), channel_id=1, source_target_pairs={{0,2},{1,3},{2,0},{3,1},{4,6},{5,7},{6,4},{7,5},{8,10},{9,11},{10,... | collective-permute-start | bytes 589832 | tf_op jit(solution)/shard_map/ppermute | solution.py:316
  5.8 12.2 %collective-permute-start.1 = (bf16[384,256]{1,0:T(8,128)(2,1)}, bf16[384,256]{1,0:T(8,128)(2,1)S(1)}, u32[]{:S(2)}, u32[]{:S(2)}) collective-permute-start(bf16[384,256]{1,0:T(8,128)(2,1)} %get-tuple-element.72), channel_id=1, source_target_pairs={{0,4},{1,5},{2,6},{3,7},{4,0},{5,1},{6,2},{7,3},{8,12},{9,13},{10,... | collective-permute-start | bytes 589832 | tf_op jit(solution)/shard_map/ppermute | solution.py:316
  7.3 10.7 %collective-permute-start.2 = (bf16[384,256]{1,0:T(8,128)(2,1)}, bf16[384,256]{1,0:T(8,128)(2,1)S(1)}, u32[]{:S(2)}, u32[]{:S(2)}) collective-permute-start(bf16[384,256]{1,0:T(8,128)(2,1)} %get-tuple-element.73), channel_id=1, source_target_pairs={{0,6},{1,7},{2,4},{3,5},{4,2},{5,3},{6,0},{7,1},{8,14},{9,15},{10,... | collective-permute-start | bytes 589832 | tf_op jit(solution)/shard_map/ppermute | solution.py:316
  7.4 31.7 %collective-permute-start.4 = (bf16[128,4096]{1,0:T(8,128)(2,1)}, bf16[128,4096]{1,0:T(8,128)(2,1)S(1)}, u32[]{:S(2)}, u32[]{:S(2)}) collective-permute-start(bf16[128,4096]{1,0:T(8,128)(2,1)} %refs_0_.4), channel_id=1, source_target_pairs={{0,4},{1,5},{2,6},{3,7},{4,0},{5,1},{6,2},{7,3},{8,12},{9,13},{10,... | collective-permute-start | bytes 3145736 | tf_op jit(solution)/shard_map/ppermute | solution.py:316
  9.3 29.7 %collective-permute-start.3 = (bf16[128,4096]{1,0:T(8,128)(2,1)}, bf16[128,4096]{1,0:T(8,128)(2,1)S(1)}, u32[]{:S(2)}, u32[]{:S(2)}) collective-permute-start(bf16[128,4096]{1,0:T(8,128)(2,1)} %refs_0_.4), channel_id=1, source_target_pairs={{0,2},{1,3},{2,0},{3,1},{4,6},{5,7},{6,4},{7,5},{8,10},{9,11},{10,... | collective-permute-start | bytes 3145736 | tf_op jit(solution)/shard_map/ppermute | solution.py:316
  18.3 25.9 %copy-start = (bf16[128,4096]{1,0:T(8,128)(2,1)S(1)}, bf16[128,4096]{1,0:T(8,128)(2,1)}, u32[]{:S(2)}) copy-start(bf16[128,4096]{1,0:T(8,128)(2,1)} %refs_0_.4) | copy-start | bytes 3145732
  18.3 14.9 %collective-permute-start.6 = (bf16[640,256]{1,0:T(8,128)(2,1)S(1)}, bf16[640,256]{1,0:T(8,128)(2,1)S(1)}, u32[]{:S(2)}, u32[]{:S(2)}) collective-permute-start(bf16[640,256]{1,0:T(8,128)(2,1)S(1)} %get-tuple-element.81.refs_6_), channel_id=1, source_target_pairs={{0,16},{1,17},{2,18},{3,19},{4,20},{5,21},{6,22},{7,23},{8,24},{9,... | collective-permute-start | bytes 983048 | tf_op jit(solution)/shard_map/ppermute | solution.py:316
  21.0 12.9 %collective-permute-start.5 = (bf16[640,256]{1,0:T(8,128)(2,1)S(1)}, bf16[640,256]{1,0:T(8,128)(2,1)S(1)}, u32[]{:S(2)}, u32[]{:S(2)}) collective-permute-start(bf16[640,256]{1,0:T(8,128)(2,1)S(1)} %get-tuple-element.81.refs_6_), channel_id=1, source_target_pairs={{0,8},{1,9},{2,10},{3,11},{4,12},{5,13},{6,14},{7,15},{8,0},{9,1},... | collective-permute-start | bytes 983048 | tf_op jit(solution)/shard_map/ppermute | solution.py:316
  33.3 8.5 %collective-permute-start.7 = (bf16[640,256]{1,0:T(8,128)(2,1)S(1)}, bf16[640,256]{1,0:T(8,128)(2,1)S(1)}, u32[]{:S(2)}, u32[]{:S(2)}) collective-permute-start(bf16[640,256]{1,0:T(8,128)(2,1)S(1)} %collective-permute-done.6.refs_8_), channel_id=1, source_target_pairs={{0,8},{1,9},{2,10},{3,11},{4,12},{5,13},{6,14},{7,15},{8,0},{9,1},... | collective-permute-start | bytes 983048 | tf_op jit(solution)/shard_map/ppermute | solution.py:316
  33.9 7.9 %collective-permute-start.10 = (bf16[640,256]{1,0:T(8,128)(2,1)S(1)}, bf16[640,256]{1,0:T(8,128)(2,1)S(1)}, u32[]{:S(2)}, u32[]{:S(2)}) collective-permute-start(bf16[640,256]{1,0:T(8,128)(2,1)S(1)} %collective-permute-done.6.refs_8_), channel_id=1, source_target_pairs={{0,1},{1,0},{2,3},{3,2},{4,5},{5,4},{6,7},{7,6},{8,9},{9,8},{10,11... | collective-permute-start | bytes 983048 | tf_op jit(solution)/shard_map/ppermute | solution.py:316
  33.9 8.4 %collective-permute-start.9 = (bf16[640,256]{1,0:T(8,128)(2,1)S(1)}, bf16[640,256]{1,0:T(8,128)(2,1)S(1)}, u32[]{:S(2)}, u32[]{:S(2)}) collective-permute-start(bf16[640,256]{1,0:T(8,128)(2,1)S(1)} %collective-permute-done.5.refs_7_), channel_id=1, source_target_pairs={{0,1},{1,0},{2,3},{3,2},{4,5},{5,4},{6,7},{7,6},{8,9},{9,8},{10,11... | collective-permute-start | bytes 983048 | tf_op jit(solution)/shard_map/ppermute | solution.py:316
  39.2 12.5 %collective-permute-start.14 = (bf16[64,4096]{1,0:T(8,128)(2,1)S(1)}, bf16[64,4096]{1,0:T(8,128)(2,1)S(1)}, u32[]{:S(2)}, u32[]{:S(2)}) collective-permute-start(bf16[64,4096]{1,0:T(8,128)(2,1)S(1)} %slice.10), channel_id=1, source_target_pairs={{0,2},{1,3},{2,0},{3,1},{4,6},{5,7},{6,4},{7,5},{8,10},{9,11},{10,... | collective-permute-start | bytes 1572872 | tf_op jit(solution)/shard_map/ppermute | solution.py:316
  39.6 12.5 %collective-permute-start.13 = (bf16[64,4096]{1,0:T(8,128)(2,1)S(1)}, bf16[64,4096]{1,0:T(8,128)(2,1)S(1)}, u32[]{:S(2)}, u32[]{:S(2)}) collective-permute-start(bf16[64,4096]{1,0:T(8,128)(2,1)S(1)} %slice.9), channel_id=1, source_target_pairs={{0,4},{1,5},{2,6},{3,7},{4,0},{5,1},{6,2},{7,3},{8,12},{9,13},{10,... | collective-permute-start | bytes 1572872 | tf_op jit(solution)/shard_map/ppermute | solution.py:316
  41.8 1.6 %collective-permute-start.11 = (bf16[640,256]{1,0:T(8,128)(2,1)S(1)}, bf16[640,256]{1,0:T(8,128)(2,1)S(1)}, u32[]{:S(2)}, u32[]{:S(2)}) collective-permute-start(bf16[640,256]{1,0:T(8,128)(2,1)S(1)} %collective-permute-done.7.refs_9_), channel_id=1, source_target_pairs={{0,1},{1,0},{2,3},{3,2},{4,5},{5,4},{6,7},{7,6},{8,9},{9,8},{10,11... | collective-permute-start | bytes 983048 | tf_op jit(solution)/shard_map/ppermute | solution.py:316
  41.8 2.5 %collective-permute-start.8 = (bf16[640,256]{1,0:T(8,128)(2,1)S(1)}, bf16[640,256]{1,0:T(8,128)(2,1)S(1)}, u32[]{:S(2)}, u32[]{:S(2)}) collective-permute-start(bf16[640,256]{1,0:T(8,128)(2,1)S(1)} %get-tuple-element.81.refs_6_), channel_id=1, source_target_pairs={{0,1},{1,0},{2,3},{3,2},{4,5},{5,4},{6,7},{7,6},{8,9},{9,8},{10,11... | collective-permute-start | bytes 983048 | tf_op jit(solution)/shard_map/ppermute | solution.py:316
  42.3 2.0 %collective-permute-start.12 = (bf16[4,256,128]{2,1,0:T(8,128)(2,1)S(1)}, bf16[4,256,128]{2,1,0:T(8,128)(2,1)S(1)}, u32[]{:S(2)}, u32[]{:S(2)}) collective-permute-start(bf16[4,256,128]{2,1,0:T(8,128)(2,1)S(1)} %get-tuple-element.82.refs_14_), channel_id=1, source_target_pairs={{0,1},{1,0},{2,3},{3,2},{4,5},{5,4},{6,7},{7,6},{8,9},{9,8},{10,11... | collective-permute-start | bytes 786440 | tf_op jit(solution)/shard_map/ppermute | solution.py:316
  54.0 1.9 %collective-permute-start.15 = (bf16[4,256,128]{2,1,0:T(8,128)(2,1)S(1)}, bf16[4,256,128]{2,1,0:T(8,128)(2,1)S(1)}, u32[]{:S(2)}, u32[]{:S(2)}) collective-permute-start(bf16[4,256,128]{2,1,0:T(8,128)(2,1)S(1)} %get-tuple-element.101.refs_0_.refs_10_), channel_id=1, source_target_pairs={{0,1},{1,0},{2,3},{3,2},{4,5},{5,4},{6,7},{7,6},{8,9},{9,8},{10,11... | collective-permute-start | bytes 786440 | tf_op jit(solution)/shard_map/ppermute | solution.py:316
  54.5 1.7 %collective-permute-start.16 = (bf16[256,512]{1,0:T(8,128)(2,1)S(1)}, bf16[256,512]{1,0:T(8,128)(2,1)S(1)}, u32[]{:S(2)}, u32[]{:S(2)}) collective-permute-start(bf16[256,512]{1,0:T(8,128)(2,1)S(1)} %get-tuple-element.105), channel_id=1, source_target_pairs={{0,1},{1,0},{2,3},{3,2},{4,5},{5,4},{6,7},{7,6},{8,9},{9,8},{10,11... | collective-permute-start | bytes 786440 | tf_op jit(solution)/shard_map/ppermute | solution.py:316
  55.6 4.3 %collective-permute-start.18 = (bf16[256,512]{1,0:T(8,128)(2,1)S(1)}, bf16[256,512]{1,0:T(8,128)(2,1)S(1)}, u32[]{:S(2)}, u32[]{:S(2)}) collective-permute-start(bf16[256,512]{1,0:T(8,128)(2,1)S(1)} %get-tuple-element.108), channel_id=1, source_target_pairs={{0,1},{1,0},{2,3},{3,2},{4,5},{5,4},{6,7},{7,6},{8,9},{9,8},{10,11... | collective-permute-start | bytes 786440 | tf_op jit(solution)/shard_map/ppermute | solution.py:316
  56.4 9.9 %collective-permute-start.17 = (bf16[288,512]{1,0:T(8,128)(2,1)S(1)}, bf16[288,512]{1,0:T(8,128)(2,1)S(1)}, u32[]{:S(2)}, u32[]{:S(2)}) collective-permute-start(bf16[288,512]{1,0:T(8,128)(2,1)S(1)} %get-tuple-element.106), channel_id=1, source_target_pairs={{0,8},{1,9},{2,10},{3,11},{4,12},{5,13},{6,14},{7,15},{8,0},{9,1},... | collective-permute-start | bytes 884744 | tf_op jit(solution)/shard_map/ppermute | solution.py:316
  58.5 10.4 %collective-permute-start.26 = (bf16[256,512]{1,0:T(8,128)(2,1)S(1)}, bf16[256,512]{1,0:T(8,128)(2,1)S(1)}, u32[]{:S(2)}, u32[]{:S(2)}) collective-permute-start(bf16[256,512]{1,0:T(8,128)(2,1)S(1)} %get-tuple-element.121), channel_id=1, source_target_pairs={{0,1},{1,0},{2,3},{3,2},{4,5},{5,4},{6,7},{7,6},{8,9},{9,8},{10,11... | collective-permute-start | bytes 786440 | tf_op jit(solution)/shard_map/ppermute | solution.py:316
  59.1 12.7 %collective-permute-start.24 = (bf16[256,512]{1,0:T(8,128)(2,1)S(1)}, bf16[256,512]{1,0:T(8,128)(2,1)S(1)}, u32[]{:S(2)}, u32[]{:S(2)}) collective-permute-start(bf16[256,512]{1,0:T(8,128)(2,1)S(1)} %get-tuple-element.119), channel_id=1, source_target_pairs={{0,1},{1,0},{2,3},{3,2},{4,5},{5,4},{6,7},{7,6},{8,9},{9,8},{10,11... | collective-permute-start | bytes 786440 | tf_op jit(solution)/shard_map/ppermute | solution.py:316
  60.0 17.3 %collective-permute-start.25 = (bf16[256,512]{1,0:T(8,128)(2,1)S(1)}, bf16[256,512]{1,0:T(8,128)(2,1)S(1)}, u32[]{:S(2)}, u32[]{:S(2)}) collective-permute-start(bf16[256,512]{1,0:T(8,128)(2,1)S(1)} %add_convert_fusion.1), channel_id=1, source_target_pairs={{0,8},{1,9},{2,10},{3,11},{4,12},{5,13},{6,14},{7,15},{8,0},{9,1},... | collective-permute-start | bytes 786440 | tf_op jit(solution)/shard_map/ppermute | solution.py:316
  66.3 5.4 %collective-permute-start.19 = (bf16[128,128]{1,0:T(8,128)(2,1)S(1)}, bf16[128,128]{1,0:T(8,128)(2,1)S(1)}, u32[]{:S(2)}, u32[]{:S(2)}) collective-permute-start(bf16[128,128]{1,0:T(8,128)(2,1)S(1)} %get-tuple-element.112), channel_id=1, source_target_pairs={{0,16},{1,17},{2,18},{3,19},{4,20},{5,21},{6,22},{7,23},{8,24},{9,... | collective-permute-start | bytes 98312 | tf_op jit(solution)/shard_map/ppermute | solution.py:316
  69.1 14.2 %collective-permute-start.27 = (bf16[256,512]{1,0:T(8,128)(2,1)S(1)}, bf16[256,512]{1,0:T(8,128)(2,1)S(1)}, u32[]{:S(2)}, u32[]{:S(2)}) collective-permute-start(bf16[256,512]{1,0:T(8,128)(2,1)S(1)} %add_convert_fusion), channel_id=1, source_target_pairs={{0,16},{1,17},{2,18},{3,19},{4,20},{5,21},{6,22},{7,23},{8,24},{9,... | collective-permute-start | bytes 786440 | tf_op jit(solution)/shard_map/ppermute | solution.py:316
  71.7 1.3 %collective-permute-start.20 = (bf16[128,128]{1,0:T(8,128)(2,1)S(1)}, bf16[128,128]{1,0:T(8,128)(2,1)S(1)}, u32[]{:S(2)}, u32[]{:S(2)}) collective-permute-start(bf16[128,128]{1,0:T(8,128)(2,1)S(1)} %shard_map.95.refs_12_), channel_id=1, source_target_pairs={{0,1},{1,0},{2,3},{3,2},{4,5},{5,4},{6,7},{7,6},{8,9},{9,8},{10,11... | collective-permute-start | bytes 98312 | tf_op jit(solution)/shard_map/ppermute | solution.py:316
  73.7 12.7 %collective-permute-start.21 = (bf16[128,512]{1,0:T(8,128)(2,1)S(1)}, bf16[128,512]{1,0:T(8,128)(2,1)S(1)}, u32[]{:S(2)}, u32[]{:S(2)}) collective-permute-start(bf16[128,512]{1,0:T(8,128)(2,1)S(1)} %get-tuple-element.113), channel_id=1, source_target_pairs={{0,6},{1,7},{2,4},{3,5},{4,2},{5,3},{6,0},{7,1},{8,14},{9,15},{10,... | collective-permute-start | bytes 393224 | tf_op jit(solution)/shard_map/ppermute | solution.py:316
  76.1 11.0 %collective-permute-start.22 = (bf16[128,512]{1,0:T(8,128)(2,1)S(1)}, bf16[128,512]{1,0:T(8,128)(2,1)S(1)}, u32[]{:S(2)}, u32[]{:S(2)}) collective-permute-start(bf16[128,512]{1,0:T(8,128)(2,1)S(1)} %get-tuple-element.114), channel_id=1, source_target_pairs={{0,4},{1,5},{2,6},{3,7},{4,0},{5,1},{6,2},{7,3},{8,12},{9,13},{10,... | collective-permute-start | bytes 393224 | tf_op jit(solution)/shard_map/ppermute | solution.py:316
  76.6 10.5 %collective-permute-start.23 = (bf16[128,512]{1,0:T(8,128)(2,1)S(1)}, bf16[128,512]{1,0:T(8,128)(2,1)S(1)}, u32[]{:S(2)}, u32[]{:S(2)}) collective-permute-start(bf16[128,512]{1,0:T(8,128)(2,1)S(1)} %get-tuple-element.115), channel_id=1, source_target_pairs={{0,2},{1,3},{2,0},{3,1},{4,6},{5,7},{6,4},{7,5},{8,10},{9,11},{10,... | collective-permute-start | bytes 393224 | tf_op jit(solution)/shard_map/ppermute | solution.py:316
  83.5 5.5 %collective-permute-start.28 = (bf16[256,128]{1,0:T(8,128)(2,1)S(1)}, bf16[256,128]{1,0:T(8,128)(2,1)S(1)}, u32[]{:S(2)}, u32[]{:S(2)}) collective-permute-start(bf16[256,128]{1,0:T(8,128)(2,1)S(1)} %get-tuple-element.122), channel_id=1, source_target_pairs={{0,6},{1,7},{2,4},{3,5},{4,2},{5,3},{6,0},{7,1},{8,14},{9,15},{10,... | collective-permute-start | bytes 196616 | tf_op jit(solution)/shard_map/ppermute | solution.py:316
  85.9 4.3 %collective-permute-start.29 = (bf16[256,128]{1,0:T(8,128)(2,1)S(1)}, bf16[256,128]{1,0:T(8,128)(2,1)S(1)}, u32[]{:S(2)}, u32[]{:S(2)}) collective-permute-start(bf16[256,128]{1,0:T(8,128)(2,1)S(1)} %get-tuple-element.123), channel_id=1, source_target_pairs={{0,4},{1,5},{2,6},{3,7},{4,0},{5,1},{6,2},{7,3},{8,12},{9,13},{10,... | collective-permute-start | bytes 196616 | tf_op jit(solution)/shard_map/ppermute | solution.py:316
  86.4 4.3 %collective-permute-start.30 = (bf16[256,128]{1,0:T(8,128)(2,1)S(1)}, bf16[256,128]{1,0:T(8,128)(2,1)S(1)}, u32[]{:S(2)}, u32[]{:S(2)}) collective-permute-start(bf16[256,128]{1,0:T(8,128)(2,1)S(1)} %get-tuple-element.124), channel_id=1, source_target_pairs={{0,2},{1,3},{2,0},{3,1},{4,6},{5,7},{6,4},{7,5},{8,10},{9,11},{10,... | collective-permute-start | bytes 196616 | tf_op jit(solution)/shard_map/ppermute | solution.py:316
  (2 other events, 26.9 us)

commit v7 on v6

--- a/solution.py
+++ b/solution.py
@@ -414,7 +414,6 @@
     for k in order[:-1]:
         came, onward = plane_swap(sums[k].astype(BF16), k & -k), k & k - 1
         if k == order[0]:
-            came, _ = lax.optimization_barrier((came, sums[order[1]].astype(BF16)))
             near, window = call(
                 unload_kernel, [((HALF, HEAD_DIM), BF16)] * 2, [place, came, half]
             )

time: 91.8 us -> 91.8 us (level)
  no operation moved by 1% of the time
where the time goes in v7:
time: 91.8 us; the launch traced here: 91.6 us
  waiting for transfers between devices  46.2 us (50%)
  starting transfers between devices  29.8 us (32%)
  Pallas kernels  13.5 us (15%)
  local copies, waits for them, and re-layouts  1.01 us (1%)
    ppermute x31, waiting for transfers between devices, swap(): return lax.ppermute(block, 'ctx', [(i, i ^ bits) for i in range(count)])  46.2 us
    ppermute x31, starting transfers between devices, swap(): return lax.ppermute(block, 'ctx', [(i, i ^ bits) for i in range(count)])  29.8 us
    pallas_call x18, Pallas kernels, call(): pl.pallas_call(kernel, out_shape=shapes, in_specs=[pl.BlockSpec(memory_sp...  13.5 us
  transfers between devices with their start and end apart: 31, of which 16 were waited for; matrix products, arithmetic and copies ran while one was open for 0% of the time, Pallas kernels for 9%

profile of v7, /device:TPU:0, one launch (start us, length us, event | category | flops | bytes accessed | tf_op | source)
XLA Modules:
  0.0 91.6 jit_solution(9081760815240272134)
XLA Ops:
  0.6 2.2 %shard_map.84 = (bf16[384,256]{1,0:T(8,128)(2,1)}, bf16[384,256]{1,0:T(8,128)(2,1)}, bf16[384,256]{1,0:T(8,128)(2,1)}, bf16[384,256]{1,0:T(8,128)(2,1)}) custom-call(s32[1]{0:T(128)} %bitcast.place, bf16[128,1024]{1,0:T(8,128)(2,1)} %w.1, bf16[128,1024]{1,0:T(8,128)(2,1)} %key.1, bf16[128,512]{1,0:T(8,128)(2,1)} %val.1, bf16[128,512]{1,0:T(8,128)(2,1)} %cot.1), custom_call_target="tpu_custom_call" | custom-call | bytes 1572868 | tf_op jit(solution)/shard_map/pallas_call | solution.py:41
  2.8 3.0 %collective-permute-start = (bf16[384,256]{1,0:T(8,128)(2,1)}, bf16[384,256]{1,0:T(8,128)(2,1)S(1)}, u32[]{:S(2)}, u32[]{:S(2)}) collective-permute-start(bf16[384,256]{1,0:T(8,128)(2,1)} %get-tuple-element.70), channel_id=1, source_target_pairs={{0,2},{1,3},{2,0},{3,1},{4,6},{5,7},{6,4},{7,5},{8,10},{9,11},{10,... | collective-permute-start | bytes 589832 | tf_op jit(solution)/shard_map/ppermute | solution.py:316
  5.8 1.5 %collective-permute-start.1 = (bf16[384,256]{1,0:T(8,128)(2,1)}, bf16[384,256]{1,0:T(8,128)(2,1)S(1)}, u32[]{:S(2)}, u32[]{:S(2)}) collective-permute-start(bf16[384,256]{1,0:T(8,128)(2,1)} %get-tuple-element.71), channel_id=1, source_target_pairs={{0,4},{1,5},{2,6},{3,7},{4,0},{5,1},{6,2},{7,3},{8,12},{9,13},{10,... | collective-permute-start | bytes 589832 | tf_op jit(solution)/shard_map/ppermute | solution.py:316
  7.4 2.0 %collective-permute-start.4 = (bf16[128,4096]{1,0:T(8,128)(2,1)}, bf16[128,4096]{1,0:T(8,128)(2,1)S(1)}, u32[]{:S(2)}, u32[]{:S(2)}) collective-permute-start(bf16[128,4096]{1,0:T(8,128)(2,1)} %refs_0_.4), channel_id=1, source_target_pairs={{0,4},{1,5},{2,6},{3,7},{4,0},{5,1},{6,2},{7,3},{8,12},{9,13},{10,... | collective-permute-start | bytes 3145736 | tf_op jit(solution)/shard_map/ppermute | solution.py:316
  9.3 1.5 %collective-permute-start.3 = (bf16[128,4096]{1,0:T(8,128)(2,1)}, bf16[128,4096]{1,0:T(8,128)(2,1)S(1)}, u32[]{:S(2)}, u32[]{:S(2)}) collective-permute-start(bf16[128,4096]{1,0:T(8,128)(2,1)} %refs_0_.4), channel_id=1, source_target_pairs={{0,2},{1,3},{2,0},{3,1},{4,6},{5,7},{6,4},{7,5},{8,10},{9,11},{10,... | collective-permute-start | bytes 3145736 | tf_op jit(solution)/shard_map/ppermute | solution.py:316
  10.8 0.9 %copy-done.1 = bf16[384,256]{1,0:T(8,128)(2,1)S(1)} copy-done((bf16[384,256]{1,0:T(8,128)(2,1)S(1)}, bf16[384,256]{1,0:T(8,128)(2,1)}, u32[]{:S(2)}) %copy-start.1) | copy-done | bytes 196632
  12.0 6.1 %collective-permute-done.1.p2.refs_5_.refs_2_ = bf16[384,256]{1,0:T(8,128)(2,1)S(1)} collective-permute-done((bf16[384,256]{1,0:T(8,128)(2,1)}, bf16[384,256]{1,0:T(8,128)(2,1)S(1)}, u32[]{:S(2)}, u32[]{:S(2)}) %collective-permute-start.1) | collective-permute-done | bytes 196640 | tf_op jit(solution)/shard_map/ppermute | solution.py:316
  18.3 2.7 %collective-permute-start.6 = (bf16[640,256]{1,0:T(8,128)(2,1)S(1)}, bf16[640,256]{1,0:T(8,128)(2,1)S(1)}, u32[]{:S(2)}, u32[]{:S(2)}) collective-permute-start(bf16[640,256]{1,0:T(8,128)(2,1)S(1)} %get-tuple-element.80.refs_6_), channel_id=1, source_target_pairs={{0,16},{1,17},{2,18},{3,19},{4,20},{5,21},{6,22},{7,23},{8,24},{9,... | collective-permute-start | bytes 983048 | tf_op jit(solution)/shard_map/ppermute | solution.py:316
  21.0 1.6 %collective-permute-start.5 = (bf16[640,256]{1,0:T(8,128)(2,1)S(1)}, bf16[640,256]{1,0:T(8,128)(2,1)S(1)}, u32[]{:S(2)}, u32[]{:S(2)}) collective-permute-start(bf16[640,256]{1,0:T(8,128)(2,1)S(1)} %get-tuple-element.80.refs_6_), channel_id=1, source_target_pairs={{0,8},{1,9},{2,10},{3,11},{4,12},{5,13},{6,14},{7,15},{8,0},{9,1},... | collective-permute-start | bytes 983048 | tf_op jit(solution)/shard_map/ppermute | solution.py:316
  22.6 10.7 %collective-permute-done.6.refs_8_ = bf16[640,256]{1,0:T(8,128)(2,1)S(1)} collective-permute-done((bf16[640,256]{1,0:T(8,128)(2,1)S(1)}, bf16[640,256]{1,0:T(8,128)(2,1)S(1)}, u32[]{:S(2)}, u32[]{:S(2)}) %collective-permute-start.6) | collective-permute-done | bytes 327712 | tf_op jit(solution)/shard_map/ppermute | solution.py:316
  34.4 4.7 %collective-permute-done.4.refs_2_ = bf16[128,4096]{1,0:T(8,128)(2,1)S(1)} collective-permute-done((bf16[128,4096]{1,0:T(8,128)(2,1)}, bf16[128,4096]{1,0:T(8,128)(2,1)S(1)}, u32[]{:S(2)}, u32[]{:S(2)}) %collective-permute-start.4) | collective-permute-done | bytes 1048608 | tf_op jit(solution)/shard_map/ppermute | solution.py:316
  39.6 1.7 %collective-permute-start.13 = (bf16[64,4096]{1,0:T(8,128)(2,1)S(1)}, bf16[64,4096]{1,0:T(8,128)(2,1)S(1)}, u32[]{:S(2)}, u32[]{:S(2)}) collective-permute-start(bf16[64,4096]{1,0:T(8,128)(2,1)S(1)} %slice.9), channel_id=1, source_target_pairs={{0,4},{1,5},{2,6},{3,7},{4,0},{5,1},{6,2},{7,3},{8,12},{9,13},{10,... | collective-permute-start | bytes 1572872 | tf_op jit(solution)/shard_map/ppermute | solution.py:316
  42.4 1.0 %collective-permute-done.11.refs_13_ = bf16[640,256]{1,0:T(8,128)(2,1)S(1)} collective-permute-done((bf16[640,256]{1,0:T(8,128)(2,1)S(1)}, bf16[640,256]{1,0:T(8,128)(2,1)S(1)}, u32[]{:S(2)}, u32[]{:S(2)}) %collective-permute-start.11) | collective-permute-done | bytes 327712 | tf_op jit(solution)/shard_map/ppermute | solution.py:316
  43.4 0.8 collective-permute-done.12.refs_15_
  44.3 3.8 %shard_map.87 = (bf16[3,128,128]{2,1,0:T(8,128)(2,1)S(1)}, bf16[256,384]{1,0:T(8,128)(2,1)S(1)}, bf16[3,256,128]{2,1,0:T(8,128)(2,1)S(1)}, bf16[3,128,256]{2,1,0...) custom-call(s32[1]{0:T(128)} %bitcast.place, ...), custom_call_target="tpu_custom_call" | custom-call | flops 805306368 | bytes 10092548 | tf_op jit(solution)/shard_map/pallas_call | solution.py:41
  48.0 3.7 %collective-permute-done.14.bottom.refs_4_ = bf16[64,4096]{1,0:T(8,128)(2,1)S(1)} collective-permute-done((bf16[64,4096]{1,0:T(8,128)(2,1)S(1)}, bf16[64,4096]{1,0:T(8,128)(2,1)S(1)}, u32[]{:S(2)}, u32[]{:S(2)}) %collective-permute-start.14) | collective-permute-done | bytes 524320 | tf_op jit(solution)/shard_map/ppermute | solution.py:316
  52.1 1.9 %shard_map.89 = (bf16[1,128,128]{2,1,0:T(8,128)(2,1)S(1)}, bf16[256,128]{1,0:T(8,128)(2,1)S(1)}, bf16[1,256,128]{2,1,0:T(8,128)(2,1)}, bf16[1,128,256]{2,1,0:T(8...) custom-call(s32[1]{0:T(128)} %bitcast.place, ...), custom_call_target="tpu_custom_call" | custom-call | flops 268435456 | bytes 4259844 | tf_op jit(solution)/shard_map/pallas_call | solution.py:41
  56.4 1.6 %collective-permute-start.17 = (bf16[288,512]{1,0:T(8,128)(2,1)S(1)}, bf16[288,512]{1,0:T(8,128)(2,1)S(1)}, u32[]{:S(2)}, u32[]{:S(2)}) collective-permute-start(bf16[288,512]{1,0:T(8,128)(2,1)S(1)} %get-tuple-element.105), channel_id=1, source_target_pairs={{0,8},{1,9},{2,10},{3,11},{4,12},{5,13},{6,14},{7,15},{8,0},{9,1},... | collective-permute-start | bytes 884744 | tf_op jit(solution)/shard_map/ppermute | solution.py:316
  60.5 5.9 %collective-permute-done.17.load = bf16[288,512]{1,0:T(8,128)(2,1)S(1)} collective-permute-done((bf16[288,512]{1,0:T(8,128)(2,1)S(1)}, bf16[288,512]{1,0:T(8,128)(2,1)S(1)}, u32[]{:S(2)}, u32[]{:S(2)}) %collective-permute-start.17) | collective-permute-done | bytes 294944 | tf_op jit(solution)/shard_map/ppermute | solution.py:316
  66.3 2.6 %collective-permute-start.18 = (bf16[128,128]{1,0:T(8,128)(2,1)S(1)}, bf16[128,128]{1,0:T(8,128)(2,1)S(1)}, u32[]{:S(2)}, u32[]{:S(2)}) collective-permute-start(bf16[128,128]{1,0:T(8,128)(2,1)S(1)} %get-tuple-element.108), channel_id=1, source_target_pairs={{0,16},{1,17},{2,18},{3,19},{4,20},{5,21},{6,22},{7,23},{8,24},{9,... | collective-permute-start | bytes 98312 | tf_op jit(solution)/shard_map/ppermute | solution.py:316
  69.5 2.2 %collective-permute-done.18.refs_1_ = bf16[128,128]{1,0:T(8,128)(2,1)S(1)} collective-permute-done((bf16[128,128]{1,0:T(8,128)(2,1)S(1)}, bf16[128,128]{1,0:T(8,128)(2,1)S(1)}, u32[]{:S(2)}, u32[]{:S(2)}) %collective-permute-start.18) | collective-permute-done | bytes 32800 | tf_op jit(solution)/shard_map/ppermute | solution.py:316
  71.9 1.1 %collective-permute-done.19.refs_13_ = bf16[128,128]{1,0:T(8,128)(2,1)S(1)} collective-permute-done((bf16[128,128]{1,0:T(8,128)(2,1)S(1)}, bf16[128,128]{1,0:T(8,128)(2,1)S(1)}, u32[]{:S(2)}, u32[]{:S(2)}) %collective-permute-start.19) | collective-permute-done | bytes 32800 | tf_op jit(solution)/shard_map/ppermute | solution.py:316
  73.0 0.7 shard_map.95
  73.7 2.4 %collective-permute-start.20 = (bf16[128,512]{1,0:T(8,128)(2,1)S(1)}, bf16[128,512]{1,0:T(8,128)(2,1)S(1)}, u32[]{:S(2)}, u32[]{:S(2)}) collective-permute-start(bf16[128,512]{1,0:T(8,128)(2,1)S(1)} %get-tuple-element.109), channel_id=1, source_target_pairs={{0,6},{1,7},{2,4},{3,5},{4,2},{5,3},{6,0},{7,1},{8,14},{9,15},{10,... | collective-permute-start | bytes 393224 | tf_op jit(solution)/shard_map/ppermute | solution.py:316
  76.6 0.7 collective-permute-start.22
  77.3 6.1 %collective-permute-done.27.refs_1_ = bf16[256,512]{1,0:T(8,128)(2,1)S(1)} collective-permute-done((bf16[256,512]{1,0:T(8,128)(2,1)S(1)}, bf16[256,512]{1,0:T(8,128)(2,1)S(1)}, u32[]{:S(2)}, u32[]{:S(2)}) %collective-permute-start.27) | collective-permute-done | bytes 262176 | tf_op jit(solution)/shard_map/ppermute | solution.py:316
  83.5 2.4 %collective-permute-start.28 = (bf16[256,128]{1,0:T(8,128)(2,1)S(1)}, bf16[256,128]{1,0:T(8,128)(2,1)S(1)}, u32[]{:S(2)}, u32[]{:S(2)}) collective-permute-start(bf16[256,128]{1,0:T(8,128)(2,1)S(1)} %get-tuple-element.120), channel_id=1, source_target_pairs={{0,6},{1,7},{2,4},{3,5},{4,2},{5,3},{6,0},{7,1},{8,14},{9,15},{10,... | collective-permute-start | bytes 196616 | tf_op jit(solution)/shard_map/ppermute | solution.py:316
  86.4 0.7 collective-permute-start.30
  87.1 0.9 shard_map.96
  87.9 1.1 %collective-permute-done.28.refs_0_ = bf16[256,128]{1,0:T(8,128)(2,1)S(1)} collective-permute-done((bf16[256,128]{1,0:T(8,128)(2,1)S(1)}, bf16[256,128]{1,0:T(8,128)(2,1)S(1)}, u32[]{:S(2)}, u32[]{:S(2)}) %collective-permute-start.28) | collective-permute-done | bytes 65568 | tf_op jit(solution)/shard_map/ppermute | solution.py:316
  89.0 1.2 %collective-permute-done.29.refs_1_ = bf16[256,128]{1,0:T(8,128)(2,1)S(1)} collective-permute-done((bf16[256,128]{1,0:T(8,128)(2,1)S(1)}, bf16[256,128]{1,0:T(8,128)(2,1)S(1)}, u32[]{:S(2)}, u32[]{:S(2)}) %collective-permute-start.29) | collective-permute-done | bytes 65568 | tf_op jit(solution)/shard_map/ppermute | solution.py:316
  90.7 1.0 %shard_map.101 = f32[128,1024]{1,0:T(8,128)} custom-call(s32[1]{0:T(128)} %bitcast.place, bf16[256,128]{1,0:T(8,128)(2,1)S(1)} %collective-permute-done.28.refs_0_, bf16[256,128]{1,0:T(8,128)(2,1)S(1)} %collective-permute-done.29.refs_1_, bf16[256,128]{1,0:T(8,128)(2,1)S(1)} %collective-permute-done.30.refs_2_, f32[256,128]{1,0:T(8,128)S(1)} %get-tuple-element.123.refs_3_), custom_call_target="tpu_custom_call" | custom-call | bytes 851972 | tf_op jit(solution)/shard_map/pallas_call | solution.py:41
  (59 shorter events, 10.7 us)
Async XLA Ops:
  2.8 9.1 %collective-permute-start = (bf16[384,256]{1,0:T(8,128)(2,1)}, bf16[384,256]{1,0:T(8,128)(2,1)S(1)}, u32[]{:S(2)}, u32[]{:S(2)}) collective-permute-start(bf16[384,256]{1,0:T(8,128)(2,1)} %get-tuple-element.70), channel_id=1, source_target_pairs={{0,2},{1,3},{2,0},{3,1},{4,6},{5,7},{6,4},{7,5},{8,10},{9,11},{10,... | collective-permute-start | bytes 589832 | tf_op jit(solution)/shard_map/ppermute | solution.py:316
  5.8 12.2 %collective-permute-start.1 = (bf16[384,256]{1,0:T(8,128)(2,1)}, bf16[384,256]{1,0:T(8,128)(2,1)S(1)}, u32[]{:S(2)}, u32[]{:S(2)}) collective-permute-start(bf16[384,256]{1,0:T(8,128)(2,1)} %get-tuple-element.71), channel_id=1, source_target_pairs={{0,4},{1,5},{2,6},{3,7},{4,0},{5,1},{6,2},{7,3},{8,12},{9,13},{10,... | collective-permute-start | bytes 589832 | tf_op jit(solution)/shard_map/ppermute | solution.py:316
  7.3 10.7 %collective-permute-start.2 = (bf16[384,256]{1,0:T(8,128)(2,1)}, bf16[384,256]{1,0:T(8,128)(2,1)S(1)}, u32[]{:S(2)}, u32[]{:S(2)}) collective-permute-start(bf16[384,256]{1,0:T(8,128)(2,1)} %get-tuple-element.72), channel_id=1, source_target_pairs={{0,6},{1,7},{2,4},{3,5},{4,2},{5,3},{6,0},{7,1},{8,14},{9,15},{10,... | collective-permute-start | bytes 589832 | tf_op jit(solution)/shard_map/ppermute | solution.py:316
  7.4 31.7 %collective-permute-start.4 = (bf16[128,4096]{1,0:T(8,128)(2,1)}, bf16[128,4096]{1,0:T(8,128)(2,1)S(1)}, u32[]{:S(2)}, u32[]{:S(2)}) collective-permute-start(bf16[128,4096]{1,0:T(8,128)(2,1)} %refs_0_.4), channel_id=1, source_target_pairs={{0,4},{1,5},{2,6},{3,7},{4,0},{5,1},{6,2},{7,3},{8,12},{9,13},{10,... | collective-permute-start | bytes 3145736 | tf_op jit(solution)/shard_map/ppermute | solution.py:316
  9.3 29.7 %collective-permute-start.3 = (bf16[128,4096]{1,0:T(8,128)(2,1)}, bf16[128,4096]{1,0:T(8,128)(2,1)S(1)}, u32[]{:S(2)}, u32[]{:S(2)}) collective-permute-start(bf16[128,4096]{1,0:T(8,128)(2,1)} %refs_0_.4), channel_id=1, source_target_pairs={{0,2},{1,3},{2,0},{3,1},{4,6},{5,7},{6,4},{7,5},{8,10},{9,11},{10,... | collective-permute-start | bytes 3145736 | tf_op jit(solution)/shard_map/ppermute | solution.py:316
  18.3 25.9 %copy-start = (bf16[128,4096]{1,0:T(8,128)(2,1)S(1)}, bf16[128,4096]{1,0:T(8,128)(2,1)}, u32[]{:S(2)}) copy-start(bf16[128,4096]{1,0:T(8,128)(2,1)} %refs_0_.4) | copy-start | bytes 3145732
  18.3 14.9 %collective-permute-start.6 = (bf16[640,256]{1,0:T(8,128)(2,1)S(1)}, bf16[640,256]{1,0:T(8,128)(2,1)S(1)}, u32[]{:S(2)}, u32[]{:S(2)}) collective-permute-start(bf16[640,256]{1,0:T(8,128)(2,1)S(1)} %get-tuple-element.80.refs_6_), channel_id=1, source_target_pairs={{0,16},{1,17},{2,18},{3,19},{4,20},{5,21},{6,22},{7,23},{8,24},{9,... | collective-permute-start | bytes 983048 | tf_op jit(solution)/shard_map/ppermute | solution.py:316
  21.0 12.9 %collective-permute-start.5 = (bf16[640,256]{1,0:T(8,128)(2,1)S(1)}, bf16[640,256]{1,0:T(8,128)(2,1)S(1)}, u32[]{:S(2)}, u32[]{:S(2)}) collective-permute-start(bf16[640,256]{1,0:T(8,128)(2,1)S(1)} %get-tuple-element.80.refs_6_), channel_id=1, source_target_pairs={{0,8},{1,9},{2,10},{3,11},{4,12},{5,13},{6,14},{7,15},{8,0},{9,1},... | collective-permute-start | bytes 983048 | tf_op jit(solution)/shard_map/ppermute | solution.py:316
  33.3 8.5 %collective-permute-start.7 = (bf16[640,256]{1,0:T(8,128)(2,1)S(1)}, bf16[640,256]{1,0:T(8,128)(2,1)S(1)}, u32[]{:S(2)}, u32[]{:S(2)}) collective-permute-start(bf16[640,256]{1,0:T(8,128)(2,1)S(1)} %collective-permute-done.6.refs_8_), channel_id=1, source_target_pairs={{0,8},{1,9},{2,10},{3,11},{4,12},{5,13},{6,14},{7,15},{8,0},{9,1},... | collective-permute-start | bytes 983048 | tf_op jit(solution)/shard_map/ppermute | solution.py:316
  33.9 7.9 %collective-permute-start.10 = (bf16[640,256]{1,0:T(8,128)(2,1)S(1)}, bf16[640,256]{1,0:T(8,128)(2,1)S(1)}, u32[]{:S(2)}, u32[]{:S(2)}) collective-permute-start(bf16[640,256]{1,0:T(8,128)(2,1)S(1)} %collective-permute-done.6.refs_8_), channel_id=1, source_target_pairs={{0,1},{1,0},{2,3},{3,2},{4,5},{5,4},{6,7},{7,6},{8,9},{9,8},{10,11... | collective-permute-start | bytes 983048 | tf_op jit(solution)/shard_map/ppermute | solution.py:316
  33.9 8.4 %collective-permute-start.9 = (bf16[640,256]{1,0:T(8,128)(2,1)S(1)}, bf16[640,256]{1,0:T(8,128)(2,1)S(1)}, u32[]{:S(2)}, u32[]{:S(2)}) collective-permute-start(bf16[640,256]{1,0:T(8,128)(2,1)S(1)} %collective-permute-done.5.refs_7_), channel_id=1, source_target_pairs={{0,1},{1,0},{2,3},{3,2},{4,5},{5,4},{6,7},{7,6},{8,9},{9,8},{10,11... | collective-permute-start | bytes 983048 | tf_op jit(solution)/shard_map/ppermute | solution.py:316
  39.2 12.5 %collective-permute-start.14 = (bf16[64,4096]{1,0:T(8,128)(2,1)S(1)}, bf16[64,4096]{1,0:T(8,128)(2,1)S(1)}, u32[]{:S(2)}, u32[]{:S(2)}) collective-permute-start(bf16[64,4096]{1,0:T(8,128)(2,1)S(1)} %slice.10), channel_id=1, source_target_pairs={{0,2},{1,3},{2,0},{3,1},{4,6},{5,7},{6,4},{7,5},{8,10},{9,11},{10,... | collective-permute-start | bytes 1572872 | tf_op jit(solution)/shard_map/ppermute | solution.py:316
  39.6 12.5 %collective-permute-start.13 = (bf16[64,4096]{1,0:T(8,128)(2,1)S(1)}, bf16[64,4096]{1,0:T(8,128)(2,1)S(1)}, u32[]{:S(2)}, u32[]{:S(2)}) collective-permute-start(bf16[64,4096]{1,0:T(8,128)(2,1)S(1)} %slice.9), channel_id=1, source_target_pairs={{0,4},{1,5},{2,6},{3,7},{4,0},{5,1},{6,2},{7,3},{8,12},{9,13},{10,... | collective-permute-start | bytes 1572872 | tf_op jit(solution)/shard_map/ppermute | solution.py:316
  41.8 1.6 %collective-permute-start.11 = (bf16[640,256]{1,0:T(8,128)(2,1)S(1)}, bf16[640,256]{1,0:T(8,128)(2,1)S(1)}, u32[]{:S(2)}, u32[]{:S(2)}) collective-permute-start(bf16[640,256]{1,0:T(8,128)(2,1)S(1)} %collective-permute-done.7.refs_9_), channel_id=1, source_target_pairs={{0,1},{1,0},{2,3},{3,2},{4,5},{5,4},{6,7},{7,6},{8,9},{9,8},{10,11... | collective-permute-start | bytes 983048 | tf_op jit(solution)/shard_map/ppermute | solution.py:316
  41.8 2.5 %collective-permute-start.8 = (bf16[640,256]{1,0:T(8,128)(2,1)S(1)}, bf16[640,256]{1,0:T(8,128)(2,1)S(1)}, u32[]{:S(2)}, u32[]{:S(2)}) collective-permute-start(bf16[640,256]{1,0:T(8,128)(2,1)S(1)} %get-tuple-element.80.refs_6_), channel_id=1, source_target_pairs={{0,1},{1,0},{2,3},{3,2},{4,5},{5,4},{6,7},{7,6},{8,9},{9,8},{10,11... | collective-permute-start | bytes 983048 | tf_op jit(solution)/shard_map/ppermute | solution.py:316
  42.3 2.0 %collective-permute-start.12 = (bf16[4,256,128]{2,1,0:T(8,128)(2,1)S(1)}, bf16[4,256,128]{2,1,0:T(8,128)(2,1)S(1)}, u32[]{:S(2)}, u32[]{:S(2)}) collective-permute-start(bf16[4,256,128]{2,1,0:T(8,128)(2,1)S(1)} %get-tuple-element.81.refs_14_), channel_id=1, source_target_pairs={{0,1},{1,0},{2,3},{3,2},{4,5},{5,4},{6,7},{7,6},{8,9},{9,8},{10,11... | collective-permute-start | bytes 786440 | tf_op jit(solution)/shard_map/ppermute | solution.py:316
  54.0 1.9 %collective-permute-start.15 = (bf16[4,256,128]{2,1,0:T(8,128)(2,1)S(1)}, bf16[4,256,128]{2,1,0:T(8,128)(2,1)S(1)}, u32[]{:S(2)}, u32[]{:S(2)}) collective-permute-start(bf16[4,256,128]{2,1,0:T(8,128)(2,1)S(1)} %get-tuple-element.100.refs_0_.refs_10_), channel_id=1, source_target_pairs={{0,1},{1,0},{2,3},{3,2},{4,5},{5,4},{6,7},{7,6},{8,9},{9,8},{10,11... | collective-permute-start | bytes 786440 | tf_op jit(solution)/shard_map/ppermute | solution.py:316
  54.5 1.7 %collective-permute-start.16 = (bf16[256,512]{1,0:T(8,128)(2,1)S(1)}, bf16[256,512]{1,0:T(8,128)(2,1)S(1)}, u32[]{:S(2)}, u32[]{:S(2)}) collective-permute-start(bf16[256,512]{1,0:T(8,128)(2,1)S(1)} %get-tuple-element.104), channel_id=1, source_target_pairs={{0,1},{1,0},{2,3},{3,2},{4,5},{5,4},{6,7},{7,6},{8,9},{9,8},{10,11... | collective-permute-start | bytes 786440 | tf_op jit(solution)/shard_map/ppermute | solution.py:316
  55.6 4.3 %collective-permute-start.24 = (bf16[256,512]{1,0:T(8,128)(2,1)S(1)}, bf16[256,512]{1,0:T(8,128)(2,1)S(1)}, u32[]{:S(2)}, u32[]{:S(2)}) collective-permute-start(bf16[256,512]{1,0:T(8,128)(2,1)S(1)} %get-tuple-element.117), channel_id=1, source_target_pairs={{0,1},{1,0},{2,3},{3,2},{4,5},{5,4},{6,7},{7,6},{8,9},{9,8},{10,11... | collective-permute-start | bytes 786440 | tf_op jit(solution)/shard_map/ppermute | solution.py:316
  56.4 9.9 %collective-permute-start.17 = (bf16[288,512]{1,0:T(8,128)(2,1)S(1)}, bf16[288,512]{1,0:T(8,128)(2,1)S(1)}, u32[]{:S(2)}, u32[]{:S(2)}) collective-permute-start(bf16[288,512]{1,0:T(8,128)(2,1)S(1)} %get-tuple-element.105), channel_id=1, source_target_pairs={{0,8},{1,9},{2,10},{3,11},{4,12},{5,13},{6,14},{7,15},{8,0},{9,1},... | collective-permute-start | bytes 884744 | tf_op jit(solution)/shard_map/ppermute | solution.py:316
  58.5 10.4 %collective-permute-start.26 = (bf16[256,512]{1,0:T(8,128)(2,1)S(1)}, bf16[256,512]{1,0:T(8,128)(2,1)S(1)}, u32[]{:S(2)}, u32[]{:S(2)}) collective-permute-start(bf16[256,512]{1,0:T(8,128)(2,1)S(1)} %get-tuple-element.119), channel_id=1, source_target_pairs={{0,1},{1,0},{2,3},{3,2},{4,5},{5,4},{6,7},{7,6},{8,9},{9,8},{10,11... | collective-permute-start | bytes 786440 | tf_op jit(solution)/shard_map/ppermute | solution.py:316
  59.1 12.7 %collective-permute-start.23 = (bf16[256,512]{1,0:T(8,128)(2,1)S(1)}, bf16[256,512]{1,0:T(8,128)(2,1)S(1)}, u32[]{:S(2)}, u32[]{:S(2)}) collective-permute-start(bf16[256,512]{1,0:T(8,128)(2,1)S(1)} %get-tuple-element.115), channel_id=1, source_target_pairs={{0,1},{1,0},{2,3},{3,2},{4,5},{5,4},{6,7},{7,6},{8,9},{9,8},{10,11... | collective-permute-start | bytes 786440 | tf_op jit(solution)/shard_map/ppermute | solution.py:316
  60.0 17.3 %collective-permute-start.25 = (bf16[256,512]{1,0:T(8,128)(2,1)S(1)}, bf16[256,512]{1,0:T(8,128)(2,1)S(1)}, u32[]{:S(2)}, u32[]{:S(2)}) collective-permute-start(bf16[256,512]{1,0:T(8,128)(2,1)S(1)} %add_convert_fusion.1), channel_id=1, source_target_pairs={{0,8},{1,9},{2,10},{3,11},{4,12},{5,13},{6,14},{7,15},{8,0},{9,1},... | collective-permute-start | bytes 786440 | tf_op jit(solution)/shard_map/ppermute | solution.py:316
  66.3 5.4 %collective-permute-start.18 = (bf16[128,128]{1,0:T(8,128)(2,1)S(1)}, bf16[128,128]{1,0:T(8,128)(2,1)S(1)}, u32[]{:S(2)}, u32[]{:S(2)}) collective-permute-start(bf16[128,128]{1,0:T(8,128)(2,1)S(1)} %get-tuple-element.108), channel_id=1, source_target_pairs={{0,16},{1,17},{2,18},{3,19},{4,20},{5,21},{6,22},{7,23},{8,24},{9,... | collective-permute-start | bytes 98312 | tf_op jit(solution)/shard_map/ppermute | solution.py:316
  69.1 14.2 %collective-permute-start.27 = (bf16[256,512]{1,0:T(8,128)(2,1)S(1)}, bf16[256,512]{1,0:T(8,128)(2,1)S(1)}, u32[]{:S(2)}, u32[]{:S(2)}) collective-permute-start(bf16[256,512]{1,0:T(8,128)(2,1)S(1)} %add_convert_fusion), channel_id=1, source_target_pairs={{0,16},{1,17},{2,18},{3,19},{4,20},{5,21},{6,22},{7,23},{8,24},{9,... | collective-permute-start | bytes 786440 | tf_op jit(solution)/shard_map/ppermute | solution.py:316
  71.7 1.3 %collective-permute-start.19 = (bf16[128,128]{1,0:T(8,128)(2,1)S(1)}, bf16[128,128]{1,0:T(8,128)(2,1)S(1)}, u32[]{:S(2)}, u32[]{:S(2)}) collective-permute-start(bf16[128,128]{1,0:T(8,128)(2,1)S(1)} %shard_map.94.refs_12_), channel_id=1, source_target_pairs={{0,1},{1,0},{2,3},{3,2},{4,5},{5,4},{6,7},{7,6},{8,9},{9,8},{10,11... | collective-permute-start | bytes 98312 | tf_op jit(solution)/shard_map/ppermute | solution.py:316
  73.7 12.7 %collective-permute-start.20 = (bf16[128,512]{1,0:T(8,128)(2,1)S(1)}, bf16[128,512]{1,0:T(8,128)(2,1)S(1)}, u32[]{:S(2)}, u32[]{:S(2)}) collective-permute-start(bf16[128,512]{1,0:T(8,128)(2,1)S(1)} %get-tuple-element.109), channel_id=1, source_target_pairs={{0,6},{1,7},{2,4},{3,5},{4,2},{5,3},{6,0},{7,1},{8,14},{9,15},{10,... | collective-permute-start | bytes 393224 | tf_op jit(solution)/shard_map/ppermute | solution.py:316
  76.1 11.0 %collective-permute-start.21 = (bf16[128,512]{1,0:T(8,128)(2,1)S(1)}, bf16[128,512]{1,0:T(8,128)(2,1)S(1)}, u32[]{:S(2)}, u32[]{:S(2)}) collective-permute-start(bf16[128,512]{1,0:T(8,128)(2,1)S(1)} %get-tuple-element.110), channel_id=1, source_target_pairs={{0,4},{1,5},{2,6},{3,7},{4,0},{5,1},{6,2},{7,3},{8,12},{9,13},{10,... | collective-permute-start | bytes 393224 | tf_op jit(solution)/shard_map/ppermute | solution.py:316
  76.6 10.5 %collective-permute-start.22 = (bf16[128,512]{1,0:T(8,128)(2,1)S(1)}, bf16[128,512]{1,0:T(8,128)(2,1)S(1)}, u32[]{:S(2)}, u32[]{:S(2)}) collective-permute-start(bf16[128,512]{1,0:T(8,128)(2,1)S(1)} %get-tuple-element.111), channel_id=1, source_target_pairs={{0,2},{1,3},{2,0},{3,1},{4,6},{5,7},{6,4},{7,5},{8,10},{9,11},{10,... | collective-permute-start | bytes 393224 | tf_op jit(solution)/shard_map/ppermute | solution.py:316
  83.5 5.5 %collective-permute-start.28 = (bf16[256,128]{1,0:T(8,128)(2,1)S(1)}, bf16[256,128]{1,0:T(8,128)(2,1)S(1)}, u32[]{:S(2)}, u32[]{:S(2)}) collective-permute-start(bf16[256,128]{1,0:T(8,128)(2,1)S(1)} %get-tuple-element.120), channel_id=1, source_target_pairs={{0,6},{1,7},{2,4},{3,5},{4,2},{5,3},{6,0},{7,1},{8,14},{9,15},{10,... | collective-permute-start | bytes 196616 | tf_op jit(solution)/shard_map/ppermute | solution.py:316
  85.9 4.3 %collective-permute-start.29 = (bf16[256,128]{1,0:T(8,128)(2,1)S(1)}, bf16[256,128]{1,0:T(8,128)(2,1)S(1)}, u32[]{:S(2)}, u32[]{:S(2)}) collective-permute-start(bf16[256,128]{1,0:T(8,128)(2,1)S(1)} %get-tuple-element.121), channel_id=1, source_target_pairs={{0,4},{1,5},{2,6},{3,7},{4,0},{5,1},{6,2},{7,3},{8,12},{9,13},{10,... | collective-permute-start | bytes 196616 | tf_op jit(solution)/shard_map/ppermute | solution.py:316
  86.4 4.3 %collective-permute-start.30 = (bf16[256,128]{1,0:T(8,128)(2,1)S(1)}, bf16[256,128]{1,0:T(8,128)(2,1)S(1)}, u32[]{:S(2)}, u32[]{:S(2)}) collective-permute-start(bf16[256,128]{1,0:T(8,128)(2,1)S(1)} %get-tuple-element.122), channel_id=1, source_target_pairs={{0,2},{1,3},{2,0},{3,1},{4,6},{5,7},{6,4},{7,5},{8,10},{9,11},{10,... | collective-permute-start | bytes 196616 | tf_op jit(solution)/shard_map/ppermute | solution.py:316
  (2 other events, 26.9 us)
